TPU v7x, 128 devices: a whole 4x4x4 slice. The times are simulated.
128 devices in a mesh: blocks: 16 (over z, y), depth: 8 (over x, core).
Axes of the slice: x: 4, y: 4, z: 4, core: 2. Of those that a mesh axis runs over, the one named last changes fastest.
Arguments:
- estimate0: float32 [512, 512, 128], P('depth', 'blocks'), may hold values from 0.5 to 1.5
- tiles: float32 [128, 512, 8, 128], P('blocks', 'depth'), may hold values from 0.2 to 2
- psf_z: float32 [6, 61], replicated
- psf_x: float32 [6, 31], replicated
- psf_y: float32 [6, 31], replicated
- tile_pair: int32 [128], P('blocks'), may hold values from 0 to 383, as said below
- tile_shift: int32 [128], P('blocks'), may hold values from -8 to 8
Outputs:
- estimate: float32 [512, 512, 128], P('depth', 'blocks')
Inputs may be any that keep to these rules, and one draw needn't show every extreme that they name: `tile_pair`: each entry is view * 64 + block for one of 6 views and one of 64 joined blocks; no pair appears twice and every block appears. Block b belongs to blocks index b // 4. Of the 8 tiles held by one blocks index, at most 1 belong to the blocks of any one blocks index, and some holder reaches 1; the tiles of one blocks index's blocks number at most 16 in all, and some blocks index has 16.
All inputs are finite; a program needn't handle non-finite values.
Results may differ from a plain program's by a relative error of at most 0.0003.
Values sent between devices are 32-bit elements; how exact they have to be, the bound alone decides.
No kernel may reach another device: no remote copies, remote signals or barrier semaphores. Data moves between devices by JAX's collectives and lax.ppermute only.
A program may use at most 128 MiB of HBM per device.

v0:
```python
import jax
import jax.numpy as jnp
from jax import lax
from jax.sharding import PartitionSpec as P

BLK_DEV = 4
OFF = 8
ITERS = 2


exact_mode = lax.Precision.HIGHEST


def with_halo(cells, sides, width):
    for axis, dim in sides:
        count = lax.axis_size(axis)
        ends = count - 1
        head = lax.slice_in_dim(cells, 0, width, axis=dim)
        tail = lax.slice_in_dim(cells, cells.shape[dim] - width, cells.shape[dim], axis=dim)
        cells = jnp.concatenate(
            [
                lax.ppermute(tail, axis, [(i, (i + 1) % count) for i in range(ends)]),
                cells,
                lax.ppermute(head, axis, [((i + 1) % count, i) for i in range(ends)]),
            ],
            axis=dim,
        )
    return cells


def band_table(kernel, rows, columns, lead):
    offset = jnp.arange(columns)[None, :] - jnp.arange(rows)[:, None] + lead
    table = jnp.zeros((kernel.shape[0], rows, columns), jnp.float32)
    for position in range(kernel.shape[1]):
        table = (
            table
            + kernel[:, position][:, None, None] * (offset == position).astype(jnp.float32)[None]
        )
    return table


def extend_depth(field, width):
    return with_halo(field, (("depth", 0),), width)


def extend_blocks(field, width):
    return with_halo(field, (("blocks", 1),), width)


def fold_depth_rims(total, width):
    length = total.shape[0]
    rims = jnp.concatenate([total[:width], total[length - width :]], axis=0)
    beside_all = with_halo(rims, (("depth", 0),), width)
    inner = total[width : length - width]
    inner = inner.at[:width].add(beside_all[:width])
    return inner.at[inner.shape[0] - width :].add(beside_all[3 * width :])


def fold_block_rims(total, width):
    length = total.shape[1]
    rims = jnp.concatenate([total[:, :width], total[:, length - width :]], axis=1)
    beside_all = with_halo(rims, (("blocks", 1),), width)
    inner = total[:, width : length - width]
    inner = inner.at[:, :width].add(beside_all[:, :width])
    return inner.at[:, inner.shape[1] - width :].add(beside_all[:, 3 * width :])


def local(estimate0, tiles, psf_z, psf_x, psf_y, tile_pair, tile_shift):
    depth_cells, width_cells, cells_y = estimate0.shape
    views, taps_z = psf_z.shape
    taps_x = psf_x.shape[1]
    taps_y = psf_y.shape[1]
    half_z = (taps_z - 1) // 2
    half_x = (taps_x - 1) // 2
    half_y = (taps_y - 1) // 2
    block_cells = tiles.shape[2]
    local_count = tiles.shape[0]
    owners = lax.axis_size("blocks")
    all_blocks = BLK_DEV * owners
    capacity = max(1, (4 * BLK_DEV + owners - 1) // owners)
    slot_count = capacity * owners
    first_block = lax.axis_index("blocks") * BLK_DEV
    z_table = band_table(
        psf_z / jnp.sum(psf_z, axis=1, keepdims=True), depth_cells, depth_cells + taps_z - 1, 0
    )
    x_table = band_table(
        psf_x / jnp.sum(psf_x, axis=1, keepdims=True), block_cells, block_cells + taps_x - 1, 0
    )
    y_table = band_table(psf_y / jnp.sum(psf_y, axis=1, keepdims=True), cells_y, cells_y, half_y)
    owner_of = tile_pair % all_blocks // BLK_DEV
    tile_index = jnp.arange(local_count)
    earlier = (owner_of[None, :] == owner_of[:, None]) & (tile_index[None, :] < tile_index[:, None])
    ranked = jnp.sum(earlier.astype(jnp.int32), axis=1)
    slot_of = owner_of * capacity + ranked
    placing = (slot_of[None, :] == jnp.arange(slot_count)[:, None]).astype(jnp.int32)
    sent = jnp.einsum("st,tzxy->szxy", placing.astype(jnp.float32), tiles, precision=exact_mode)
    sent_pair = jnp.sum(placing * (tile_pair + 1)[None, :], axis=1) - 1
    sent_shift = jnp.sum(placing * tile_shift[None, :], axis=1)
    got, got_pair, got_shift = (
        lax.all_to_all(sent, "blocks", split_axis=0, concat_axis=0, tiled=True),
        lax.all_to_all(sent_pair, "blocks", split_axis=0, concat_axis=0, tiled=True),
        lax.all_to_all(sent_shift, "blocks", split_axis=0, concat_axis=0, tiled=True),
    )
    columns = jnp.arange(cells_y)

    def register(record, shift_value):
        padded = jnp.pad(record, ((0, 0), (0, 0), (OFF, OFF)))
        moved = lax.dynamic_slice_in_dim(padded, OFF - shift_value, cells_y, 2)
        inside = ((columns >= shift_value) & (columns < cells_y + shift_value)).astype(jnp.float32)
        return (moved * inside, inside)

    aligned, inside_all = jax.vmap(register)(got, got_shift)
    live = (got_pair >= 0).astype(jnp.int32)
    live_count = jnp.sum(live)
    position = jnp.cumsum(live) - 1
    picking = (position[None, :] == jnp.arange(slot_count)[:, None]) & (live[None, :] > 0)
    order = jnp.sum(picking.astype(jnp.int32) * jnp.arange(slot_count)[None, :], axis=1)

    def predict(source, local_block, z_pick, x_pick, y_pick):
        piece_ext = lax.dynamic_slice(
            source,
            (0, local_block * block_cells, 0),
            (depth_cells + 2 * half_z, block_cells + 2 * half_x, cells_y),
        )
        z_part = jnp.einsum("ij,jxy->ixy", z_pick, piece_ext, precision=exact_mode)
        x_part = jnp.einsum("ab,iby->iay", x_pick, z_part, precision=exact_mode)
        return jnp.einsum("iay,cy->iac", x_part, y_pick, precision=exact_mode)

    def spread(carry, ratio, local_block, z_pick, x_pick, y_pick):
        y_part = jnp.einsum("iay,yc->iac", ratio, y_pick, precision=exact_mode)
        x_part = jnp.einsum("ab,iay->iby", x_pick, y_part, precision=exact_mode)
        z_part = jnp.einsum("ij,ixy->jxy", z_pick, x_part, precision=exact_mode)
        start = (0, local_block * block_cells, 0)
        current = lax.dynamic_slice(carry, start, z_part.shape)
        return lax.dynamic_update_slice(carry, current + z_part, start)

    def fold_all(total):
        return fold_block_rims(fold_depth_rims(total, half_z), half_x)

    def accumulate(source, use_data):
        empty = jnp.zeros(
            (depth_cells + 2 * half_z, width_cells + 2 * half_x, cells_y), jnp.float32
        )

        def visit(number, carry):
            slot_id = lax.dynamic_index_in_dim(order, number, 0, keepdims=False)
            pair_id = lax.dynamic_index_in_dim(got_pair, slot_id, 0, keepdims=False)
            view_id = pair_id // all_blocks
            local_block = pair_id % all_blocks - first_block
            z_pick = lax.dynamic_index_in_dim(z_table, view_id, 0, keepdims=False)
            x_pick = lax.dynamic_index_in_dim(x_table, view_id, 0, keepdims=False)
            y_pick = lax.dynamic_index_in_dim(y_table, view_id, 0, keepdims=False)
            if use_data:
                record = lax.dynamic_index_in_dim(aligned, slot_id, 0, keepdims=False)
                ratio = record / predict(source, local_block, z_pick, x_pick, y_pick)
            else:
                inside = lax.dynamic_index_in_dim(inside_all, slot_id, 0, keepdims=False)
                ratio = jnp.broadcast_to(inside, (depth_cells, block_cells, cells_y))
            return spread(carry, ratio, local_block, z_pick, x_pick, y_pick)

        carry = lax.fori_loop(0, live_count, visit, empty)
        return fold_all(carry)

    weight = jnp.maximum(accumulate(None, False), 1.0)
    estimate = estimate0
    for iteration in range(ITERS):
        widened = extend_blocks(extend_depth(estimate, half_z), half_x)
        source = widened
        estimate = estimate * accumulate(source, True) / weight
    return estimate


def solution(mesh):
    in_specs = (
        P("depth", "blocks", None),
        P("blocks", "depth", None, None),
        P(),
        P(),
        P(),
        P("blocks"),
        P("blocks"),
    )
    out_specs = P("depth", "blocks", None)
    return jax.shard_map(local, mesh=mesh, in_specs=in_specs, out_specs=out_specs, check_vma=False)
```

profile of v0, /device:TPU:34, one launch (start us, length us, event | category | flops | bytes accessed | tf_op | source)
XLA Modules:
  0.0 1206.4 jit_solution(11967290963738139032)
XLA Ops:
  3.5 8.1 all-to-all-start
  83.4 7.2 all-to-all-start.2
  91.3 5.5 all-to-all-done.2
  96.8 5.7 all-to-all-start.1
  117.4 107.5 %while.49 = (s32[]{:T(128)}, f32[124,62,128]{2,0,1:T(8,128)}, s32[]{:T(128)}, s32[16]{0:T(128)S(1)}, s32[16]{0:T(128)S(1)}, /*index=5*/s32[]{:T(128)}, f32[6,64,...) while((s32[]{:T(128)}, f32[124,62,128]{2,0,1:T(8,128)}, ...), condition=%wide.region_12.13_spmd, body=%wide.region_11.12_spmd.sunk | while | flops 594359296 | bytes 8165428 | solution.py:161
  125.4 5.4 add_dynamic-update-slice_fusion.7
  138.9 5.4 add_dynamic-update-slice_fusion.7
  242.6 9.4 copy.120
  252.0 8.7 pad.29
  260.8 8.7 gather_fusion
  269.5 7.9 broadcast_multiply_fusion
  277.4 6.8 copy.125
  286.6 162.1 %while.48 = (s32[]{:T(128)}, f32[124,62,128]{2,0,1:T(8,128)}, s32[]{:T(128)}, s32[16]{0:T(128)S(1)}, s32[16]{0:T(128)S(1)}, /*index=5*/s32[]{:T(128)}, f32[6,64,...) while((s32[]{:T(128)}, f32[124,62,128]{2,0,1:T(8,128)}, ...), condition=%wide.region_10.11_spmd, body=%wide.region_9.10_spmd.sunk | while | flops 1188180992 | bytes 14557772 | solution.py:161
  465.1 6.0 collective-permute-start.11
  474.3 267.0 %collective-permute-start.6 = (f32[64,15,128]{2,1,0:T(8,128)}, f32[64,15,128]{2,1,0:T(8,128)}, u32[]{:S(2)}, u32[]{:S(2)}) collective-permute-start(f32[64,15,128]{2,1,0:T(8,128)} %get-tuple-element.904), channel_id=1, source_target_pairs={{0,8},{8,16},{16,24},{24,32},{32,40},{40,48},{48,56},{56,64},{64,7... | collective-permute-start | bytes 1474568 | tf_op jit(solution)/shard_map/ppermute | solution.py:22
  758.5 5.8 collective-permute-done.7
  793.3 19.0 %collective-permute-done.14 = f32[124,15,128]{2,0,1:T(8,128)S(1)} collective-permute-done((f32[124,15,128]{2,0,1:T(8,128)S(1)}, f32[124,15,128]{2,0,1:T(8,128)S(1)}, u32[]{:S(2)}, u32[]{:S(2)}) %collective-permute-start.14) | collective-permute-done | bytes 952352 | tf_op jit(solution)/shard_map/ppermute | solution.py:22
  826.1 162.6 %while.50 = (s32[]{:T(128)}, f32[124,62,128]{2,0,1:T(8,128)}, s32[]{:T(128)}, s32[16]{0:T(128)S(1)}, s32[16]{0:T(128)S(1)}, /*index=5*/s32[]{:T(128)}, f32[6,64,...) while((s32[]{:T(128)}, f32[124,62,128]{2,0,1:T(8,128)}, ...), condition=%wide.region_14.15_spmd, body=%wide.region_13.14_spmd.sunk | while | flops 1188180992 | bytes 14557772 | solution.py:161
  841.2 5.4 add_dynamic-update-slice_fusion.8
  861.5 5.4 add_dynamic-update-slice_fusion.8
  999.1 9.7 collective-permute-done.16
  1013.6 6.0 collective-permute-start.19
  1020.8 8.6 collective-permute-done.18
  1034.5 162.7 %collective-permute-done.19 = f32[64,15,128]{2,1,0:T(8,128)} collective-permute-done((f32[64,15,128]{2,1,0:T(8,128)}, f32[64,15,128]{2,1,0:T(8,128)}, u32[]{:S(2)}, u32[]{:S(2)}) %collective-permute-start.19) | collective-permute-done | bytes 491552 | tf_op jit(solution)/shard_map/ppermute | solution.py:24
  (464 shorter events, 510.2 us)
Async XLA Ops:
  0.0 67.3 %copy-start = (f32[8,64,8,128]{3,2,1,0:T(8,128)S(1)}, f32[8,64,8,128]{3,2,1,0:T(8,128)}, u32[]{:S(2)}) copy-start(f32[8,64,8,128]{3,2,1,0:T(8,128)} %param.38) | copy-start | bytes 6291460
  3.5 79.9 %all-to-all-start = ((s32[16,1,1]{2,1,0:T(1,128)}), s32[16,1,1]{2,1,0:T(1,128)S(1)}, u32[]{:S(2)}, u32[]{:S(2)}) async-start(s32[16,1,1]{2,1,0:T(1,128)} %copy.116), calls=%async_computation | async-start | bytes 16384 | tf_op jit(solution)/shard_map/all_to_all | solution.py:101
  14.6 89.7 %collective-permute-start = (f32[30,32,128]{2,0,1:T(8,128)}, f32[30,32,128]{2,0,1:T(8,128)}, u32[]{:S(2)}, u32[]{:S(2)}) collective-permute-start(f32[30,32,128]{2,0,1:T(8,128)} %get-tuple-element.911), channel_id=1, source_target_pairs={{0,1},{1,2},{2,3},{3,4},{4,5},{5,6},{6,7},{8,9},{9,10},{10,11},{11... | collective-permute-start | bytes 1474568 | tf_op jit(solution)/shard_map/ppermute | solution.py:22
  16.6 87.6 %collective-permute-start.1 = (f32[30,32,128]{2,0,1:T(8,128)}, f32[30,32,128]{2,0,1:T(8,128)}, u32[]{:S(2)}, u32[]{:S(2)}) collective-permute-start(f32[30,32,128]{2,0,1:T(8,128)} %get-tuple-element.912), channel_id=1, source_target_pairs={{1,0},{2,1},{3,2},{4,3},{5,4},{6,5},{7,6},{9,8},{10,9},{11,10},{12... | collective-permute-start | bytes 1474568 | tf_op jit(solution)/shard_map/ppermute | solution.py:24
  83.4 13.4 %all-to-all-start.2 = ((s32[16,1,1]{2,1,0:T(1,128)}), s32[16,1,1]{2,1,0:T(1,128)S(1)}, u32[]{:S(2)}, u32[]{:S(2)}) async-start(s32[16,1,1]{2,1,0:T(1,128)} %copy.121), calls=%async_computation.2 | async-start | bytes 16384 | tf_op jit(solution)/shard_map/all_to_all | solution.py:102
  96.8 145.8 %all-to-all-start.1 = ((f32[16,64,8,128]{3,2,1,0:T(8,128)}), f32[16,64,8,128]{3,2,1,0:T(8,128)}, u32[]{:S(2)}, u32[]{:S(2)}) async-start(f32[16,64,8,128]{3,2,1,0:T(8,128)} %copy.119), calls=%async_computation.1 | async-start | bytes 8388608 | tf_op jit(solution)/shard_map/all_to_all | solution.py:100
  107.0 131.3 %collective-permute-start.2 = (f32[124,15,128]{2,0,1:T(8,128)}, f32[124,15,128]{2,0,1:T(8,128)}, u32[]{:S(2)}, u32[]{:S(2)}) collective-permute-start(f32[124,15,128]{2,0,1:T(8,128)} %get-tuple-element.905), channel_id=1, source_target_pairs={{0,8},{8,16},{16,24},{24,32},{32,40},{40,48},{48,56},{56,64},{64,7... | collective-permute-start | bytes 2856968 | tf_op jit(solution)/shard_map/ppermute | solution.py:22
  110.4 127.9 %collective-permute-start.3 = (f32[124,15,128]{2,0,1:T(8,128)}, f32[124,15,128]{2,0,1:T(8,128)}, u32[]{:S(2)}, u32[]{:S(2)}) collective-permute-start(f32[124,15,128]{2,0,1:T(8,128)} %get-tuple-element.906), channel_id=1, source_target_pairs={{8,0},{16,8},{24,16},{32,24},{40,32},{48,40},{56,48},{64,56},{72,6... | collective-permute-start | bytes 2856968 | tf_op jit(solution)/shard_map/ppermute | solution.py:24
  232.7 226.5 %collective-permute-start.8 = (f32[30,62,128]{2,1,0:T(8,128)}, f32[30,62,128]{2,1,0:T(8,128)}, u32[]{:S(2)}, u32[]{:S(2)}) collective-permute-start(f32[30,62,128]{2,1,0:T(8,128)} %get-tuple-element.896), channel_id=1, source_target_pairs={{0,1},{1,2},{2,3},{3,4},{4,5},{5,6},{6,7},{8,9},{9,10},{10,11},{11... | collective-permute-start | bytes 2856968 | tf_op jit(solution)/shard_map/ppermute | solution.py:22
  234.7 226.0 %collective-permute-start.9 = (f32[30,62,128]{2,1,0:T(8,128)}, f32[30,62,128]{2,1,0:T(8,128)}, u32[]{:S(2)}, u32[]{:S(2)}) collective-permute-start(f32[30,62,128]{2,1,0:T(8,128)} %get-tuple-element.895), channel_id=1, source_target_pairs={{1,0},{2,1},{3,2},{4,3},{5,4},{6,5},{7,6},{9,8},{10,9},{11,10},{12... | collective-permute-start | bytes 2856968 | tf_op jit(solution)/shard_map/ppermute | solution.py:24
  453.4 17.9 %collective-permute-start.4 = (f32[30,62,128]{2,1,0:T(8,128)S(1)}, f32[30,62,128]{2,1,0:T(8,128)S(1)}, u32[]{:S(2)}, u32[]{:S(2)}) collective-permute-start(f32[30,62,128]{2,1,0:T(8,128)S(1)} %get-tuple-element.898), channel_id=1, source_target_pairs={{0,1},{1,2},{2,3},{3,4},{4,5},{5,6},{6,7},{8,9},{9,10},{10,11},{11... | collective-permute-start | bytes 2856968 | tf_op jit(solution)/shard_map/ppermute | solution.py:22
  455.7 15.8 %collective-permute-start.5 = (f32[30,62,128]{2,1,0:T(8,128)S(1)}, f32[30,62,128]{2,1,0:T(8,128)S(1)}, u32[]{:S(2)}, u32[]{:S(2)}) collective-permute-start(f32[30,62,128]{2,1,0:T(8,128)S(1)} %get-tuple-element.897), channel_id=1, source_target_pairs={{1,0},{2,1},{3,2},{4,3},{5,4},{6,5},{7,6},{9,8},{10,9},{11,10},{12... | collective-permute-start | bytes 2856968 | tf_op jit(solution)/shard_map/ppermute | solution.py:24
  463.1 278.2 %collective-permute-start.10 = (f32[64,15,128]{2,1,0:T(8,128)S(1)}, f32[64,15,128]{2,1,0:T(8,128)S(1)}, u32[]{:S(2)}, u32[]{:S(2)}) collective-permute-start(f32[64,15,128]{2,1,0:T(8,128)S(1)} %get-tuple-element.902), channel_id=1, source_target_pairs={{0,8},{8,16},{16,24},{24,32},{32,40},{40,48},{48,56},{56,64},{64,7... | collective-permute-start | bytes 1474568 | tf_op jit(solution)/shard_map/ppermute | solution.py:22
  465.1 283.2 %collective-permute-start.11 = (f32[64,15,128]{2,1,0:T(8,128)}, f32[64,15,128]{2,1,0:T(8,128)}, u32[]{:S(2)}, u32[]{:S(2)}) collective-permute-start(f32[64,15,128]{2,1,0:T(8,128)} %get-tuple-element.901), channel_id=1, source_target_pairs={{8,0},{16,8},{24,16},{32,24},{40,32},{48,40},{56,48},{64,56},{72,6... | collective-permute-start | bytes 1474568 | tf_op jit(solution)/shard_map/ppermute | solution.py:24
  474.3 278.7 %collective-permute-start.6 = (f32[64,15,128]{2,1,0:T(8,128)}, f32[64,15,128]{2,1,0:T(8,128)}, u32[]{:S(2)}, u32[]{:S(2)}) collective-permute-start(f32[64,15,128]{2,1,0:T(8,128)} %get-tuple-element.904), channel_id=1, source_target_pairs={{0,8},{8,16},{16,24},{24,32},{32,40},{40,48},{48,56},{56,64},{64,7... | collective-permute-start | bytes 1474568 | tf_op jit(solution)/shard_map/ppermute | solution.py:22
  745.5 18.8 %collective-permute-start.7 = (f32[64,15,128]{2,1,0:T(8,128)}, f32[64,15,128]{2,1,0:T(8,128)}, u32[]{:S(2)}, u32[]{:S(2)}) collective-permute-start(f32[64,15,128]{2,1,0:T(8,128)} %get-tuple-element.903), channel_id=1, source_target_pairs={{8,0},{16,8},{24,16},{32,24},{40,32},{48,40},{56,48},{64,56},{72,6... | collective-permute-start | bytes 1474568 | tf_op jit(solution)/shard_map/ppermute | solution.py:24
  771.1 10.1 collective-permute-start.12
  773.1 9.8 collective-permute-start.13
  784.1 28.2 %collective-permute-start.14 = (f32[124,15,128]{2,0,1:T(8,128)S(1)}, f32[124,15,128]{2,0,1:T(8,128)S(1)}, u32[]{:S(2)}, u32[]{:S(2)}) collective-permute-start(f32[124,15,128]{2,0,1:T(8,128)S(1)} %copy.134), channel_id=1, source_target_pairs={{0,8},{8,16},{16,24},{24,32},{32,40},{40,48},{48,56},{56,64},{64,7... | collective-permute-start | bytes 2856968 | tf_op jit(solution)/shard_map/ppermute | solution.py:22
  789.6 26.2 %collective-permute-start.15 = (f32[124,15,128]{2,0,1:T(8,128)}, f32[124,15,128]{2,0,1:T(8,128)}, u32[]{:S(2)}, u32[]{:S(2)}) collective-permute-start(f32[124,15,128]{2,0,1:T(8,128)} %copy.135), channel_id=1, source_target_pairs={{8,0},{16,8},{24,16},{32,24},{40,32},{48,40},{56,48},{64,56},{72,6... | collective-permute-start | bytes 2856968 | tf_op jit(solution)/shard_map/ppermute | solution.py:24
  993.4 15.4 %collective-permute-start.16 = (f32[30,62,128]{2,1,0:T(8,128)S(1)}, f32[30,62,128]{2,1,0:T(8,128)S(1)}, u32[]{:S(2)}, u32[]{:S(2)}) collective-permute-start(f32[30,62,128]{2,1,0:T(8,128)S(1)} %get-tuple-element.894), channel_id=1, source_target_pairs={{0,1},{1,2},{2,3},{3,4},{4,5},{5,6},{6,7},{8,9},{9,10},{10,11},{11... | collective-permute-start | bytes 2856968 | tf_op jit(solution)/shard_map/ppermute | solution.py:22
  996.0 14.6 %collective-permute-start.17 = (f32[30,62,128]{2,1,0:T(8,128)S(1)}, f32[30,62,128]{2,1,0:T(8,128)S(1)}, u32[]{:S(2)}, u32[]{:S(2)}) collective-permute-start(f32[30,62,128]{2,1,0:T(8,128)S(1)} %get-tuple-element.893), channel_id=1, source_target_pairs={{1,0},{2,1},{3,2},{4,3},{5,4},{6,5},{7,6},{9,8},{10,9},{11,10},{12... | collective-permute-start | bytes 2856968 | tf_op jit(solution)/shard_map/ppermute | solution.py:24
  1011.7 17.7 %collective-permute-start.18 = (f32[64,15,128]{2,1,0:T(8,128)S(1)}, f32[64,15,128]{2,1,0:T(8,128)S(1)}, u32[]{:S(2)}, u32[]{:S(2)}) collective-permute-start(f32[64,15,128]{2,1,0:T(8,128)S(1)} %get-tuple-element.900), channel_id=1, source_target_pairs={{0,8},{8,16},{16,24},{24,32},{32,40},{40,48},{48,56},{56,64},{64,7... | collective-permute-start | bytes 1474568 | tf_op jit(solution)/shard_map/ppermute | solution.py:22
  1013.6 183.6 %collective-permute-start.19 = (f32[64,15,128]{2,1,0:T(8,128)}, f32[64,15,128]{2,1,0:T(8,128)}, u32[]{:S(2)}, u32[]{:S(2)}) collective-permute-start(f32[64,15,128]{2,1,0:T(8,128)} %get-tuple-element.899), channel_id=1, source_target_pairs={{8,0},{16,8},{24,16},{32,24},{40,32},{48,40},{56,48},{64,56},{72,6... | collective-permute-start | bytes 1474568 | tf_op jit(solution)/shard_map/ppermute | solution.py:24
  (53 other events, 304.2 us)
where the time goes:
time: 1230 us; the launch traced here: 1210 us
  starting transfers between devices  350 us (28%)
  matrix products  289 us (23%)
  waiting for transfers between devices  223 us (18%)
  local copies, waits for them, and re-layouts  139 us (11%)
  loops' own time  120 us (10%)
  other arithmetic  83.9 us (7%)
    ppermute x10, starting transfers between devices, with_halo(): lax.ppermute(tail, axis, [(i, (i + 1) % count) for i in range(ends)])  289 us
    ppermute x10, waiting for transfers between devices, with_halo(): lax.ppermute(head, axis, [((i + 1) % count, i) for i in range(ends)])  176 us
    dot_general x24, matrix products, spread(): z_part = jnp.einsum('ij,ixy->jxy', z_pick, x_part, precision=exact_mode)  128 us
    another operation x3, loops' own time, accumulate(): carry = lax.fori_loop(0, live_count, visit, empty)  120 us
    dot_general x16, matrix products, predict(): z_part = jnp.einsum('ij,jxy->ixy', z_pick, piece_ext, precision=exact_mode)  49.6 us
    ppermute x10, waiting for transfers between devices, with_halo(): lax.ppermute(tail, axis, [(i, (i + 1) % count) for i in range(ends)])  41.9 us
    ppermute x10, starting transfers between devices, with_halo(): lax.ppermute(head, axis, [((i + 1) % count, i) for i in range(ends)])  39.7 us
    convert_element_type x63, other arithmetic, band_table(): (offset == position).astype(jnp.float32)[None]  37.2 us
  transfers between devices with their start and end apart: 23, of which 11 were waited for; matrix products, arithmetic and copies ran while one was open for 29% of the time, Pallas kernels for 0%

commit v1 on v0

v1 whole, which is shorter than its diff:
```python
import functools

import jax
import jax.numpy as jnp
from jax import lax
from jax.experimental import pallas as pl
from jax.experimental.pallas import tpu as pltpu
from jax.sharding import PartitionSpec as P

BLK_DEV = 4
BX = 8
OFF = 8
ITERS = 2
V = 6
NY = 128
DZ = 64
DX = 32
RZ = 30
PZ = 32
RX = 16
EZ = DZ + 2 * PZ
EX = DX + 2 * RX
ROWS = V * DX
MIB = 1 << 20

exact_mode = lax.Precision.HIGHEST


def split(value):
    high = value.astype(jnp.bfloat16)
    low = (value - high.astype(jnp.float32)).astype(jnp.bfloat16)
    return high, low


def mul(a, b):
    return jnp.dot(a, b, preferred_element_type=jnp.float32)


def pair_columns(value, rows):
    return value[:, : value.shape[1] // 2], value[:, value.shape[1] // 2 :]


def blur_x(xf, planes, store):
    both = jnp.concatenate(planes, axis=1)
    high, low = split(both)
    out = mul(xf, jnp.concatenate([high, low, high], axis=0))
    store(out[:, :NY], out[:, NY:])


def forward_x(s_ref, xf_ref, est, left, right, topc, tops, botc, bots):
    zeros = jnp.zeros((2, ROWS, NY), jnp.float32)
    s_ref[0:2] = zeros
    s_ref[EZ - 2 : EZ] = zeros

    def put(base):
        def store(first, second):
            s_ref[base] = first
            s_ref[base + 1] = second

        return store

    def rim(centre, sides, start):
        @pl.loop(0, RZ // 2)
        def _(k):
            planes = []
            for z in (2 * k, 2 * k + 1):
                planes.append(
                    jnp.concatenate([sides[z, :RX], centre[z], sides[z, RX:]], axis=0)
                )
            blur_x(xf_ref[...], planes, put(start + 2 * k))

    @pl.loop(0, DZ // 2)
    def _(k):
        planes = []
        for z in (2 * k, 2 * k + 1):
            planes.append(jnp.concatenate([left[z], est[z], right[z]], axis=0))
        blur_x(xf_ref[...], planes, put(PZ + 2 * k))

    rim(topc, tops, PZ - RZ)
    rim(botc, bots, PZ + DZ)


def shifted_y(yt_ref, view, shift):
    table = yt_ref[view, pl.ds(OFF + shift, NY), :]
    row = lax.broadcasted_iota(jnp.int32, (NY, NY), 0) + shift
    return split(jnp.where((row >= 0) & (row < NY), table, 0.0))


def forward_tile(s_ref, zf_ref, table, view, row):
    field = jnp.swapaxes(s_ref[:, pl.ds(row, BX), :], 0, 1)
    parts = []
    for p in range(BX // 2):
        high, low = split(jnp.concatenate([field[2 * p], field[2 * p + 1]], axis=1))
        out = mul(zf_ref[view], jnp.concatenate([high, low], axis=0))
        out = out[:DZ] + out[DZ:]
        parts += [out[:, :NY], out[:, NY:]]
    high, low = split(jnp.concatenate(parts, axis=0))
    whigh, wlow = table
    rhs = jnp.concatenate(
        [jnp.concatenate([whigh, whigh], axis=1), jnp.concatenate([wlow, wlow], axis=1)], axis=0
    )
    out = lax.dot_general(
        jnp.concatenate([high, low], axis=1),
        rhs,
        (((1,), (1,)), ((), ())),
        preferred_element_type=jnp.float32,
    )
    return out[:, :NY] + out[:, NY:]


def ratio_of(record, predicted, shift):
    data = jnp.swapaxes(record, 0, 1).reshape(BX * DZ, NY)
    lane = lax.broadcasted_iota(jnp.int32, (BX * DZ, NY), 1) + shift
    inside = (lane >= 0) & (lane < NY)
    return jnp.where(inside, data / jnp.where(inside, predicted, 1.0), 0.0)


def backward_tile(s_ref, zb_ref, table, view, row, ratio):
    whigh, wlow = table
    high, low = split(ratio)
    half = jnp.concatenate([whigh, wlow], axis=1)
    out = mul(jnp.concatenate([high, low], axis=1), jnp.concatenate([half, half], axis=0))
    out = out[:, :NY] + out[:, NY:]
    parts = []
    for p in range(BX // 2):
        first = out[2 * p * DZ : (2 * p + 1) * DZ]
        second = out[(2 * p + 1) * DZ : (2 * p + 2) * DZ]
        high, low = split(jnp.concatenate([first, second], axis=1))
        res = mul(zb_ref[view], jnp.concatenate([high, low, high], axis=0))
        parts += [res[:, :NY], res[:, NY:]]
    s_ref[:, pl.ds(row, BX), :] = jnp.swapaxes(jnp.stack(parts, axis=0), 0, 1)


def backward_x(s_ref, xb_ref, midc, midl, midr, topc, tops, botc, bots):
    def spread_pair(base):
        both = jnp.concatenate([s_ref[base], s_ref[base + 1]], axis=1)
        high, low = split(both)
        out = mul(xb_ref[...], jnp.concatenate([high, low], axis=0))
        out = out[:EX] + out[EX:]
        return out[:, :NY], out[:, NY:]

    def rim(centre, sides, start):
        @pl.loop(0, RZ // 2)
        def _(k):
            for i, plane in enumerate(spread_pair(start + 2 * k)):
                z = 2 * k + i
                sides[z] = jnp.concatenate([plane[:RX], plane[RX + DX :]], axis=0)
                centre[z] = plane[RX : RX + DX]

    rim(topc, tops, PZ - RZ)
    rim(botc, bots, PZ + DZ)

    @pl.loop(0, DZ // 2)
    def _(k):
        for i, plane in enumerate(spread_pair(PZ + 2 * k)):
            z = 2 * k + i
            midl[z] = plane[:RX]
            midc[z] = plane[RX : RX + DX]
            midr[z] = plane[RX + DX :]


def sweep_body(slots, meta, est, left, right, topc, tops, botc, bots, data, xf, xb, zf, zb, yt,
               omidc, omidl, omidr, otopc, otops, obotc, obots, s_ref):
    forward_x(s_ref, xf, est, left, right, topc, tops, botc, bots)

    @pl.loop(0, V * BLK_DEV)
    def _(pair):
        @pl.when(meta[4 * slots + pair] == 0)
        def _():
            s_ref[:, pl.ds(pl.multiple_of(pair * BX, BX), BX), :] = jnp.zeros(
                (EZ, BX, NY), jnp.float32
            )

    @pl.loop(0, slots)
    def _(slot):
        view = meta[slots + slot]
        row = pl.multiple_of(view * DX + meta[2 * slots + slot] * BX, BX)
        shift = meta[3 * slots + slot]

        @pl.when(meta[slot] > 0)
        def _():
            table = shifted_y(yt, view, shift)
            predicted = forward_tile(s_ref, zf, table, view, row)
            ratio = ratio_of(data[slot], predicted, shift)
            backward_tile(s_ref, zb, table, view, row, ratio)

    backward_x(s_ref, xb, omidc, omidl, omidr, otopc, otops, obotc, obots)


def f32(*shape):
    return jax.ShapeDtypeStruct(shape, jnp.float32)


VM = pl.BlockSpec(memory_space=pltpu.VMEM)
SM = pl.BlockSpec(memory_space=pltpu.SMEM)
PIECES = (
    f32(DZ, DX, NY),
    f32(DZ, RX, NY),
    f32(DZ, RX, NY),
    f32(RZ, DX, NY),
    f32(RZ, 2 * RX, NY),
    f32(RZ, DX, NY),
    f32(RZ, 2 * RX, NY),
)


def sweep(meta, pieces, data, tables):
    slots = data.shape[0]
    return pl.pallas_call(
        functools.partial(sweep_body, slots),
        out_shape=PIECES,
        in_specs=[SM] + [VM] * 13,
        out_specs=[VM] * 7,
        scratch_shapes=[pltpu.VMEM((EZ, ROWS, NY), jnp.float32)],
        compiler_params=pltpu.CompilerParams(vmem_limit_bytes=56 * MIB),
        name="sweep",
    )(meta, *pieces, data, *tables)


def place_body(where, tiles, out, sem):
    count = where.shape[0]
    for slot in range(count):

        @pl.when(where[slot] >= 0)
        def _():
            pltpu.make_async_copy(tiles.at[where[slot]], out.at[slot], sem.at[slot]).start()

    for slot in range(count):

        @pl.when(where[slot] >= 0)
        def _():
            pltpu.make_async_copy(tiles.at[where[slot]], out.at[slot], sem.at[slot]).wait()


def place(where, tiles):
    count = where.shape[0]
    return pl.pallas_call(
        place_body,
        out_shape=f32(count, *tiles.shape[1:]),
        in_specs=[SM, VM],
        out_specs=pl.BlockSpec(memory_space=pl.ANY),
        scratch_shapes=[pltpu.SemaphoreType.DMA((count,))],
        compiler_params=pltpu.CompilerParams(vmem_limit_bytes=32 * MIB),
        name="place",
    )(where, tiles)


def rims_body(midl, midr, above, below, outl, outr):
    for mid, out, at in ((midl, outl, 0), (midr, outr, RX)):
        cols = pl.ds(at, RX)
        out[:RZ] = mid[:RZ] + above[:, cols]
        out[RZ : DZ - RZ] = mid[RZ : DZ - RZ]
        out[DZ - RZ :] = mid[DZ - RZ :] + below[:, cols]


def fold_rims(midl, midr, above, below):
    return pl.pallas_call(
        rims_body,
        out_shape=(f32(DZ, RX, NY), f32(DZ, RX, NY)),
        in_specs=[VM] * 4,
        out_specs=[VM] * 2,
        compiler_params=pltpu.CompilerParams(vmem_limit_bytes=32 * MIB),
        name="fold_rims",
    )(midl, midr, above, below)


def update_body(wz, est, midc, above, below, froml, fromr, gain, *outs):
    def step(z, extra):
        total = midc[z]
        if extra is not None:
            total = total + extra
        total = total + jnp.concatenate([froml[z], fromr[z]], axis=0)
        weight = wz[0, z] * gain[0]
        for view in range(1, V):
            weight = weight + wz[view, z] * gain[view]
        return est[z] * total / jnp.maximum(weight, 1.0)

    def write(z, new):
        outs[0][z] = new
        if len(outs) > 1:
            outs[1][z] = new[:RX]
            outs[2][z] = new[RX:]

    @pl.loop(0, RZ)
    def _(z):
        new = step(z, above[z])
        write(z, new)
        if len(outs) > 1:
            outs[3][z] = new

    for z in range(RZ, DZ - RZ):
        write(z, step(z, None))

    @pl.loop(0, RZ)
    def _(k):
        new = step(k + DZ - RZ, below[k])
        write(k + DZ - RZ, new)
        if len(outs) > 1:
            outs[4][k] = new


def update(wz, est, midc, above, below, froml, fromr, gain, last):
    shapes = [f32(DZ, DX, NY)]
    if not last:
        shapes += [f32(DZ, RX, NY)] * 2 + [f32(RZ, DX, NY)] * 2
    return pl.pallas_call(
        update_body,
        out_shape=tuple(shapes),
        in_specs=[SM] + [VM] * 7,
        out_specs=[VM] * len(shapes),
        compiler_params=pltpu.CompilerParams(vmem_limit_bytes=32 * MIB),
        name="update",
    )(wz, est, midc, above, below, froml, fromr, gain)


def band(row, rows, first):
    table = jnp.broadcast_to(row, (rows, row.shape[1]))
    return pltpu.roll(table, first % row.shape[1], 1, stride=1, stride_axis=0)


def tables_body(kz, kx, ky, xf, xb, zf, zb, yt):
    for view in range(V):
        full = band(kz[view : view + 1], DZ, PZ - RZ)
        high, low = split(full)
        zf[view] = jnp.concatenate(
            [jnp.concatenate([high, high], axis=1), jnp.concatenate([low, low], axis=1)], axis=0
        )
        high, low = split(full.T)
        zb[view] = jnp.concatenate([high, high, low], axis=1)
        yt[view] = band(ky[view : view + 1], NY + 2 * OFF, -15 - OFF)[:, :NY]
    full = jnp.concatenate([band(kx[v : v + 1], DX, RX - 15) for v in range(V)], axis=0)
    high, low = split(full[:, :EX])
    xf[...] = jnp.concatenate([high, high, low], axis=1)
    high, low = split(full.T[:EX])
    both = jnp.concatenate([high, low], axis=0)
    xb[...] = jnp.concatenate([both, both], axis=1)


def make_tables(kernel_z, kernel_x, kernel_y):
    def bf16(*shape):
        return jax.ShapeDtypeStruct(shape, jnp.bfloat16)

    def padded(kernel, lanes):
        return jnp.pad(kernel, ((0, 8 - V), (0, lanes - kernel.shape[1])))

    return pl.pallas_call(
        tables_body,
        out_shape=(
            bf16(ROWS, 3 * EX),
            bf16(2 * EX, 2 * ROWS),
            bf16(V, 2 * DZ, 2 * EZ),
            bf16(V, EZ, 3 * DZ),
            f32(V, NY + 2 * OFF, NY),
        ),
        in_specs=[VM] * 3,
        out_specs=[VM] * 5,
        compiler_params=pltpu.CompilerParams(vmem_limit_bytes=32 * MIB),
        name="tables",
    )(padded(kernel_z, 128), padded(kernel_x, 128), padded(kernel_y, 256))


def send(value, axis, step):
    count = lax.axis_size(axis)
    if step > 0:
        pairs = [(i, i + 1) for i in range(count - 1)]
    else:
        pairs = [(i + 1, i) for i in range(count - 1)]
    return lax.ppermute(value, axis, pairs)


def halo(est, coll, colr, planet, planeb):
    right = send(coll, "blocks", -1)
    left = send(colr, "blocks", 1)
    botc = send(planet, "depth", -1)
    topc = send(planeb, "depth", 1)
    sides_t = jnp.concatenate([left[:RZ], right[:RZ]], axis=1)
    sides_b = jnp.concatenate([left[DZ - RZ :], right[DZ - RZ :]], axis=1)
    bots = send(sides_t, "depth", -1)
    tops = send(sides_b, "depth", 1)
    return est, left, right, topc, tops, botc, bots


def weight_parts(pairs, shifts, kernel_z, kernel_x, kernel_y, yt, all_blocks):
    planes = lax.axis_size("depth") * DZ
    view = pairs // all_blocks
    block = pairs % all_blocks
    taps = jnp.arange(kernel_z.shape[1])[None, :]
    z = lax.axis_index("depth") * DZ + jnp.arange(DZ)[:, None]
    reached = ((z - taps + RZ >= 0) & (z - taps + RZ < planes)).astype(jnp.float32)
    wz = jnp.einsum("va,za->vz", kernel_z, reached, precision=exact_mode)
    hot = (view[:, None] == jnp.arange(V)[None, :]).astype(jnp.float32)
    x = lax.axis_index("blocks") * DX + jnp.arange(DX)
    lead = x[None, :, None] + 15 - BX * block[:, None, None] - jnp.arange(kernel_x.shape[1])[None, None, :]
    covers = ((lead >= 0) & (lead < BX)).astype(jnp.float32)
    along_x = jnp.einsum("txb,vb->vtx", covers, kernel_x, precision=exact_mode) * hot.T[:, :, None]
    y = jnp.arange(NY)
    inside = (y[None, :] >= shifts[:, None]) & (y[None, :] < NY + shifts[:, None])
    along_y = jnp.einsum("ty,vyc->vtc", inside.astype(jnp.float32), yt[:, OFF : OFF + NY], precision=exact_mode)
    gain = jnp.einsum("vtx,vtc->vxc", along_x, along_y, precision=exact_mode)
    return wz, gain


def local(estimate0, tiles, psf_z, psf_x, psf_y, tile_pair, tile_shift):
    owners = lax.axis_size("blocks")
    all_blocks = BLK_DEV * owners
    me = lax.axis_index("blocks")
    kernel_z = psf_z / jnp.sum(psf_z, axis=1, keepdims=True)
    kernel_x = psf_x / jnp.sum(psf_x, axis=1, keepdims=True)
    kernel_y = psf_y / jnp.sum(psf_y, axis=1, keepdims=True)

    held = tile_pair % all_blocks // BLK_DEV
    number = jnp.arange(tiles.shape[0])
    goes = held[None, :] == jnp.arange(owners)[:, None]
    where = jnp.max(jnp.where(goes, number[None, :], -1), axis=1)
    got = lax.all_to_all(place(where, tiles), "blocks", split_axis=0, concat_axis=0, tiled=True)

    packed = tile_pair * 32 + (tile_shift + OFF)
    everyone = lax.all_gather(packed, "blocks", axis=0, tiled=True)
    pairs = everyone // 32
    shifts = everyone % 32 - OFF
    mine = (pairs % all_blocks // BLK_DEV == me).reshape(owners, -1)
    live = jnp.max(mine.astype(jnp.int32), axis=1)
    got_pair = jnp.sum(jnp.where(mine, pairs.reshape(owners, -1), 0), axis=1)
    got_shift = jnp.sum(jnp.where(mine, shifts.reshape(owners, -1), 0), axis=1)
    got_view = got_pair // all_blocks
    got_block = jnp.where(live > 0, got_pair % all_blocks - me * BLK_DEV, 0)
    cell = got_view * BLK_DEV + got_block
    present = jnp.max(
        jnp.where(cell[None, :] == jnp.arange(V * BLK_DEV)[:, None], live[None, :], 0), axis=1
    )
    meta = jnp.concatenate([live, got_view, got_block, got_shift, present]).astype(jnp.int32)

    tables = make_tables(kernel_z, kernel_x, kernel_y)
    wz, gain = weight_parts(pairs, shifts, kernel_z, kernel_x, kernel_y, tables[4], all_blocks)

    est = estimate0
    rims = (est[:, :RX], est[:, DX - RX :], est[:RZ], est[DZ - RZ :])
    for iteration in range(ITERS):
        pieces = halo(est, *rims)
        midc, midl, midr, topc, tops, botc, bots = sweep(meta, pieces, got, tables)
        below_s = send(tops, "depth", -1)
        above_s = send(bots, "depth", 1)
        below_c = send(topc, "depth", -1)
        above_c = send(botc, "depth", 1)
        rim_l, rim_r = fold_rims(midl, midr, above_s, below_s)
        fromr = send(rim_l, "blocks", -1)
        froml = send(rim_r, "blocks", 1)
        est, *rims = update(
            wz, est, midc, above_c, below_c, froml, fromr, gain, iteration == ITERS - 1
        )
    return est


def solution(mesh):
    in_specs = (
        P("depth", "blocks", None),
        P("blocks", "depth", None, None),
        P(),
        P(),
        P(),
        P("blocks"),
        P("blocks"),
    )
    out_specs = P("depth", "blocks", None)
    return jax.shard_map(local, mesh=mesh, in_specs=in_specs, out_specs=out_specs, check_vma=False)
```

time: 1230 us -> 310 us (0.25)
  the two profiles are of different devices: /device:TPU:34 before, /device:TPU:99 now
where the time goes in v1:
time: 310 us; the launch traced here: 309 us
  Pallas kernels  93.9 us (30%)
  starting transfers between devices  80.7 us (26%)
  blocking collectives  64.1 us (21%)
  waiting for transfers between devices  44.7 us (14%)
  local copies, waits for them, and re-layouts  18.4 us (6%)
  other arithmetic  4.15 us (1%)
    pallas_call x2, Pallas kernels, sweep(): pl.pallas_call(functools.partial(sweep_body, slots), out_shape=PIECES, in...  86.2 us
    ppermute x24, starting transfers between devices, send(): return lax.ppermute(value, axis, pairs)  74 us
    unnamed x1, blocking collectives  64.1 us
    ppermute x24, waiting for transfers between devices, send(): return lax.ppermute(value, axis, pairs)  44.7 us
    unnamed x68, local copies, waits for them, and re-layouts  16.3 us
    all_to_all x1, starting transfers between devices, local(): lax.all_to_all(place(where, tiles), 'blocks', split_axis=0, concat_axis=0...  6.74 us
  transfers between devices with their start and end apart: 25, of which 12 were waited for; matrix products, arithmetic and copies ran while one was open for 2% of the time, Pallas kernels for 0%

profile of v1, /device:TPU:99, one launch (start us, length us, event | category | flops | bytes accessed | tf_op | source)
XLA Modules:
  0.0 309.0 jit_solution(3003364184792343031)
XLA Ops:
  7.4 6.7 %all-to-all-start = ((f32[16,64,8,128]{3,2,1,0:T(8,128)}), f32[16,64,8,128]{3,2,1,0:T(8,128)}, u32[]{:S(2)}, u32[]{:S(2)}) async-start(f32[16,64,8,128]{3,2,1,0:T(8,128)} %copy-done), calls=%async_computation | async-start | bytes 8388608 | tf_op jit(solution)/shard_map/all_to_all | solution.py:415
  15.2 3.1 %collective-permute-start.4 = (f32[30,32,128]{2,1,0:T(8,128)}, f32[30,32,128]{2,1,0:T(8,128)S(1)}, u32[]{:S(2)}, u32[]{:S(2)}) collective-permute-start(f32[30,32,128]{2,1,0:T(8,128)} %get-tuple-element.71), channel_id=1, source_target_pairs={{1,0},{2,1},{3,2},{4,3},{5,4},{6,5},{7,6},{9,8},{10,9},{11,10},{12... | collective-permute-start | bytes 1474568 | tf_op jit(solution)/shard_map/ppermute | solution.py:368
  18.3 3.0 collective-permute-start.2
  21.4 4.6 %collective-permute-start.1 = (f32[64,16,128]{2,1,0:T(8,128)S(1)}, f32[64,16,128]{2,1,0:T(8,128)S(1)}, u32[]{:S(2)}, u32[]{:S(2)}) collective-permute-start(f32[64,16,128]{2,1,0:T(8,128)S(1)} %get-tuple-element.73), channel_id=1, source_target_pairs={{8,0},{16,8},{24,16},{32,24},{40,32},{48,40},{56,48},{64,56},{72,6... | collective-permute-start | bytes 1572872 | tf_op jit(solution)/shard_map/ppermute | solution.py:368
  28.2 64.1 %all-reduce.3 = s32[128]{0:T(128)S(1)} all-reduce(s32[128]{0:T(128)S(1)} %get-tuple-element.86), channel_id=1, replica_groups=mesh['blocks'=16,'depth'=8] {'blocks'}, use_global_device_ids=true, to_apply=%add.3 | all-reduce | flops 128 | bytes 1024
  94.4 6.6 %collective-permute-start.3 = (f32[30,32,128]{2,1,0:T(8,128)}, f32[30,32,128]{2,1,0:T(8,128)S(1)}, u32[]{:S(2)}, u32[]{:S(2)}) collective-permute-start(f32[30,32,128]{2,1,0:T(8,128)} %pad_maximum_fusion), channel_id=1, source_target_pairs={{0,1},{1,2},{2,3},{3,4},{4,5},{5,6},{6,7},{8,9},{9,10},{10,11},{11... | collective-permute-start | bytes 1474568 | tf_op jit(solution)/shard_map/ppermute | solution.py:368
  112.9 43.1 %sweep.2 = (f32[64,32,128]{2,1,0:T(8,128)}, f32[64,16,128]{2,1,0:T(8,128)}, f32[64,16,128]{2,1,0:T(8,128)}, f32[30,32,128]{2,1,0:T(8,128)}, f32[30,32,128]{2,1,0...) custom-call(s32[88]{0:T(128)} %concatenate.15.meta, f32[64,32,128]{2,1,0:T(8,128)} %est.3, ...), custom_call_target="tpu_custom_call" | custom-call | tf_op jit(solution)/shard_map/sweep/pallas_call | solution.py:209
  160.9 3.2 %collective-permute-start.6 = (f32[30,32,128]{2,1,0:T(8,128)}, f32[30,32,128]{2,1,0:T(8,128)S(1)}, u32[]{:S(2)}, u32[]{:S(2)}) collective-permute-start(f32[30,32,128]{2,1,0:T(8,128)} %get-tuple-element.39), channel_id=1, source_target_pairs={{0,1},{1,2},{2,3},{3,4},{4,5},{5,6},{6,7},{8,9},{9,10},{10,11},{11... | collective-permute-start | bytes 1474568 | tf_op jit(solution)/shard_map/ppermute | solution.py:368
  166.0 2.7 collective-permute-done.9.below
  172.9 5.5 %collective-permute-start.11 = (f32[64,16,128]{2,1,0:T(8,128)S(1)}, f32[64,16,128]{2,1,0:T(8,128)S(1)}, u32[]{:S(2)}, u32[]{:S(2)}) collective-permute-start(f32[64,16,128]{2,1,0:T(8,128)S(1)} %get-tuple-element.46), channel_id=1, source_target_pairs={{8,0},{16,8},{24,16},{32,24},{40,32},{48,40},{56,48},{64,56},{72,6... | collective-permute-start | bytes 1572872 | tf_op jit(solution)/shard_map/ppermute | solution.py:368
  179.9 7.7 %collective-permute-done.10.froml = f32[64,16,128]{2,1,0:T(8,128)S(1)} collective-permute-done((f32[64,16,128]{2,1,0:T(8,128)S(1)}, f32[64,16,128]{2,1,0:T(8,128)S(1)}, u32[]{:S(2)}, u32[]{:S(2)}) %collective-permute-start.10) | collective-permute-done | bytes 524320 | tf_op jit(solution)/shard_map/ppermute | solution.py:368
  194.4 5.9 %collective-permute-start.13 = (f32[64,16,128]{2,1,0:T(8,128)S(1)}, f32[64,16,128]{2,1,0:T(8,128)S(1)}, u32[]{:S(2)}, u32[]{:S(2)}) collective-permute-start(f32[64,16,128]{2,1,0:T(8,128)S(1)} %get-tuple-element.49), channel_id=1, source_target_pairs={{8,0},{16,8},{24,16},{32,24},{40,32},{48,40},{56,48},{64,56},{72,6... | collective-permute-start | bytes 1572872 | tf_op jit(solution)/shard_map/ppermute | solution.py:368
  200.3 3.6 %collective-permute-start.14 = (f32[30,32,128]{2,1,0:T(8,128)S(1)}, f32[30,32,128]{2,1,0:T(8,128)S(1)}, u32[]{:S(2)}, u32[]{:S(2)}) collective-permute-start(f32[30,32,128]{2,1,0:T(8,128)S(1)} %get-tuple-element.50), channel_id=1, source_target_pairs={{0,1},{1,2},{2,3},{3,4},{4,5},{5,6},{6,7},{8,9},{9,10},{10,11},{11... | collective-permute-start | bytes 1474568 | tf_op jit(solution)/shard_map/ppermute | solution.py:368
  205.9 4.8 %collective-permute-done.12.left = f32[64,16,128]{2,1,0:T(8,128)S(1)} collective-permute-done((f32[64,16,128]{2,1,0:T(8,128)S(1)}, f32[64,16,128]{2,1,0:T(8,128)S(1)}, u32[]{:S(2)}, u32[]{:S(2)}) %collective-permute-start.12) | collective-permute-done | bytes 524320 | tf_op jit(solution)/shard_map/ppermute | solution.py:368
  211.7 3.8 %collective-permute-start.15 = (f32[30,32,128]{2,1,0:T(8,128)S(1)}, f32[30,32,128]{2,1,0:T(8,128)S(1)}, u32[]{:S(2)}, u32[]{:S(2)}) collective-permute-start(f32[30,32,128]{2,1,0:T(8,128)S(1)} %pad_maximum_fusion.2), channel_id=1, source_target_pairs={{0,1},{1,2},{2,3},{3,4},{4,5},{5,6},{6,7},{8,9},{9,10},{10,11},{11... | collective-permute-start | bytes 1474568 | tf_op jit(solution)/shard_map/ppermute | solution.py:368
  217.5 3.7 %collective-permute-done.15.tops = f32[30,32,128]{2,1,0:T(8,128)S(1)} collective-permute-done((f32[30,32,128]{2,1,0:T(8,128)S(1)}, f32[30,32,128]{2,1,0:T(8,128)S(1)}, u32[]{:S(2)}, u32[]{:S(2)}) %collective-permute-start.15) | collective-permute-done | bytes 491552 | tf_op jit(solution)/shard_map/ppermute | solution.py:368
  221.3 4.5 %collective-permute-done.17.bots = f32[30,32,128]{2,1,0:T(8,128)S(1)} collective-permute-done((f32[30,32,128]{2,1,0:T(8,128)S(1)}, f32[30,32,128]{2,1,0:T(8,128)S(1)}, u32[]{:S(2)}, u32[]{:S(2)}) %collective-permute-start.17) | collective-permute-done | bytes 491552 | tf_op jit(solution)/shard_map/ppermute | solution.py:368
  226.5 43.1 %sweep.3 = (f32[64,32,128]{2,1,0:T(8,128)}, f32[64,16,128]{2,1,0:T(8,128)}, f32[64,16,128]{2,1,0:T(8,128)}, f32[30,32,128]{2,1,0:T(8,128)}, f32[30,32,128]{2,1,0...) custom-call(s32[88]{0:T(128)} %concatenate.15.meta, f32[64,32,128]{2,1,0:T(8,128)} %copy-done.3, ...), custom_call_target="tpu_custom_call" | custom-call | tf_op jit(solution)/shard_map/sweep/pallas_call | solution.py:209
  273.9 3.7 %collective-permute-done.20.above = f32[30,32,128]{2,1,0:T(8,128)S(1)} collective-permute-done((f32[30,32,128]{2,1,0:T(8,128)}, f32[30,32,128]{2,1,0:T(8,128)S(1)}, u32[]{:S(2)}, u32[]{:S(2)}) %collective-permute-start.20) | collective-permute-done | bytes 491552 | tf_op jit(solution)/shard_map/ppermute | solution.py:368
  277.6 4.3 %collective-permute-done.21.below = f32[30,32,128]{2,1,0:T(8,128)S(1)} collective-permute-done((f32[30,32,128]{2,1,0:T(8,128)}, f32[30,32,128]{2,1,0:T(8,128)S(1)}, u32[]{:S(2)}, u32[]{:S(2)}) %collective-permute-start.21) | collective-permute-done | bytes 491552 | tf_op jit(solution)/shard_map/ppermute | solution.py:368
  286.0 6.2 %collective-permute-start.23 = (f32[64,16,128]{2,1,0:T(8,128)S(1)}, f32[64,16,128]{2,1,0:T(8,128)S(1)}, u32[]{:S(2)}, u32[]{:S(2)}) collective-permute-start(f32[64,16,128]{2,1,0:T(8,128)S(1)} %get-tuple-element.60), channel_id=1, source_target_pairs={{8,0},{16,8},{24,16},{32,24},{40,32},{48,40},{56,48},{64,56},{72,6... | collective-permute-start | bytes 1572872 | tf_op jit(solution)/shard_map/ppermute | solution.py:368
  296.6 3.9 %collective-permute-done.18.above = f32[30,32,128]{2,1,0:T(8,128)S(1)} collective-permute-done((f32[30,32,128]{2,1,0:T(8,128)}, f32[30,32,128]{2,1,0:T(8,128)S(1)}, u32[]{:S(2)}, u32[]{:S(2)}) %collective-permute-start.18) | collective-permute-done | bytes 491552 | tf_op jit(solution)/shard_map/ppermute | solution.py:368
  300.4 4.3 %collective-permute-done.19.below = f32[30,32,128]{2,1,0:T(8,128)S(1)} collective-permute-done((f32[30,32,128]{2,1,0:T(8,128)}, f32[30,32,128]{2,1,0:T(8,128)S(1)}, u32[]{:S(2)}, u32[]{:S(2)}) %collective-permute-start.19) | collective-permute-done | bytes 491552 | tf_op jit(solution)/shard_map/ppermute | solution.py:368
  306.0 3.0 update.3
  (146 shorter events, 62.7 us)
Async XLA Ops:
  7.4 104.7 %all-to-all-start = ((f32[16,64,8,128]{3,2,1,0:T(8,128)}), f32[16,64,8,128]{3,2,1,0:T(8,128)}, u32[]{:S(2)}, u32[]{:S(2)}) async-start(f32[16,64,8,128]{3,2,1,0:T(8,128)} %copy-done), calls=%async_computation | async-start | bytes 8388608 | tf_op jit(solution)/shard_map/all_to_all | solution.py:415
  15.2 94.4 %collective-permute-start.4 = (f32[30,32,128]{2,1,0:T(8,128)}, f32[30,32,128]{2,1,0:T(8,128)S(1)}, u32[]{:S(2)}, u32[]{:S(2)}) collective-permute-start(f32[30,32,128]{2,1,0:T(8,128)} %get-tuple-element.71), channel_id=1, source_target_pairs={{1,0},{2,1},{3,2},{4,3},{5,4},{6,5},{7,6},{9,8},{10,9},{11,10},{12... | collective-permute-start | bytes 1474568 | tf_op jit(solution)/shard_map/ppermute | solution.py:368
  18.3 91.3 %collective-permute-start.2 = (f32[30,32,128]{2,1,0:T(8,128)}, f32[30,32,128]{2,1,0:T(8,128)S(1)}, u32[]{:S(2)}, u32[]{:S(2)}) collective-permute-start(f32[30,32,128]{2,1,0:T(8,128)} %get-tuple-element.72), channel_id=1, source_target_pairs={{0,1},{1,2},{2,3},{3,4},{4,5},{5,6},{6,7},{8,9},{9,10},{10,11},{11... | collective-permute-start | bytes 1474568 | tf_op jit(solution)/shard_map/ppermute | solution.py:368
  21.4 71.8 %collective-permute-start.1 = (f32[64,16,128]{2,1,0:T(8,128)S(1)}, f32[64,16,128]{2,1,0:T(8,128)S(1)}, u32[]{:S(2)}, u32[]{:S(2)}) collective-permute-start(f32[64,16,128]{2,1,0:T(8,128)S(1)} %get-tuple-element.73), channel_id=1, source_target_pairs={{8,0},{16,8},{24,16},{32,24},{40,32},{48,40},{56,48},{64,56},{72,6... | collective-permute-start | bytes 1572872 | tf_op jit(solution)/shard_map/ppermute | solution.py:368
  26.0 67.2 %collective-permute-start = (f32[64,16,128]{2,1,0:T(8,128)S(1)}, f32[64,16,128]{2,1,0:T(8,128)S(1)}, u32[]{:S(2)}, u32[]{:S(2)}) collective-permute-start(f32[64,16,128]{2,1,0:T(8,128)S(1)} %get-tuple-element.74), channel_id=1, source_target_pairs={{0,8},{8,16},{16,24},{24,32},{32,40},{40,48},{48,56},{56,64},{64,7... | collective-permute-start | bytes 1572872 | tf_op jit(solution)/shard_map/ppermute | solution.py:368
  94.4 15.3 %collective-permute-start.3 = (f32[30,32,128]{2,1,0:T(8,128)}, f32[30,32,128]{2,1,0:T(8,128)S(1)}, u32[]{:S(2)}, u32[]{:S(2)}) collective-permute-start(f32[30,32,128]{2,1,0:T(8,128)} %pad_maximum_fusion), channel_id=1, source_target_pairs={{0,1},{1,2},{2,3},{3,4},{4,5},{5,6},{6,7},{8,9},{9,10},{10,11},{11... | collective-permute-start | bytes 1474568 | tf_op jit(solution)/shard_map/ppermute | solution.py:368
  101.8 10.3 %collective-permute-start.5 = (f32[30,32,128]{2,1,0:T(8,128)}, f32[30,32,128]{2,1,0:T(8,128)S(1)}, u32[]{:S(2)}, u32[]{:S(2)}) collective-permute-start(f32[30,32,128]{2,1,0:T(8,128)} %pad_maximum_fusion.1), channel_id=1, source_target_pairs={{1,0},{2,1},{3,2},{4,3},{5,4},{6,5},{7,6},{9,8},{10,9},{11,10},{12... | collective-permute-start | bytes 1474568 | tf_op jit(solution)/shard_map/ppermute | solution.py:368
  156.0 10.0 %collective-permute-start.8 = (f32[30,32,128]{2,1,0:T(8,128)}, f32[30,32,128]{2,1,0:T(8,128)S(1)}, u32[]{:S(2)}, u32[]{:S(2)}) collective-permute-start(f32[30,32,128]{2,1,0:T(8,128)} %get-tuple-element.43), channel_id=1, source_target_pairs={{0,1},{1,2},{2,3},{3,4},{4,5},{5,6},{6,7},{8,9},{9,10},{10,11},{11... | collective-permute-start | bytes 1474568 | tf_op jit(solution)/shard_map/ppermute | solution.py:368
  158.1 10.7 %collective-permute-start.9 = (f32[30,32,128]{2,1,0:T(8,128)}, f32[30,32,128]{2,1,0:T(8,128)S(1)}, u32[]{:S(2)}, u32[]{:S(2)}) collective-permute-start(f32[30,32,128]{2,1,0:T(8,128)} %get-tuple-element.44), channel_id=1, source_target_pairs={{1,0},{2,1},{3,2},{4,3},{5,4},{6,5},{7,6},{9,8},{10,9},{11,10},{12... | collective-permute-start | bytes 1474568 | tf_op jit(solution)/shard_map/ppermute | solution.py:368
  160.9 18.9 %collective-permute-start.6 = (f32[30,32,128]{2,1,0:T(8,128)}, f32[30,32,128]{2,1,0:T(8,128)S(1)}, u32[]{:S(2)}, u32[]{:S(2)}) collective-permute-start(f32[30,32,128]{2,1,0:T(8,128)} %get-tuple-element.39), channel_id=1, source_target_pairs={{0,1},{1,2},{2,3},{3,4},{4,5},{5,6},{6,7},{8,9},{9,10},{10,11},{11... | collective-permute-start | bytes 1474568 | tf_op jit(solution)/shard_map/ppermute | solution.py:368
  164.1 15.8 %collective-permute-start.7 = (f32[30,32,128]{2,1,0:T(8,128)}, f32[30,32,128]{2,1,0:T(8,128)S(1)}, u32[]{:S(2)}, u32[]{:S(2)}) collective-permute-start(f32[30,32,128]{2,1,0:T(8,128)} %get-tuple-element.40), channel_id=1, source_target_pairs={{1,0},{2,1},{3,2},{4,3},{5,4},{6,5},{7,6},{9,8},{10,9},{11,10},{12... | collective-permute-start | bytes 1474568 | tf_op jit(solution)/shard_map/ppermute | solution.py:368
  170.9 16.7 %collective-permute-start.10 = (f32[64,16,128]{2,1,0:T(8,128)S(1)}, f32[64,16,128]{2,1,0:T(8,128)S(1)}, u32[]{:S(2)}, u32[]{:S(2)}) collective-permute-start(f32[64,16,128]{2,1,0:T(8,128)S(1)} %get-tuple-element.45), channel_id=1, source_target_pairs={{0,8},{8,16},{16,24},{24,32},{32,40},{40,48},{48,56},{56,64},{64,7... | collective-permute-start | bytes 1572872 | tf_op jit(solution)/shard_map/ppermute | solution.py:368
  172.9 16.5 %collective-permute-start.11 = (f32[64,16,128]{2,1,0:T(8,128)S(1)}, f32[64,16,128]{2,1,0:T(8,128)S(1)}, u32[]{:S(2)}, u32[]{:S(2)}) collective-permute-start(f32[64,16,128]{2,1,0:T(8,128)S(1)} %get-tuple-element.46), channel_id=1, source_target_pairs={{8,0},{16,8},{24,16},{32,24},{40,32},{48,40},{56,48},{64,56},{72,6... | collective-permute-start | bytes 1572872 | tf_op jit(solution)/shard_map/ppermute | solution.py:368
  192.4 18.2 %collective-permute-start.12 = (f32[64,16,128]{2,1,0:T(8,128)S(1)}, f32[64,16,128]{2,1,0:T(8,128)S(1)}, u32[]{:S(2)}, u32[]{:S(2)}) collective-permute-start(f32[64,16,128]{2,1,0:T(8,128)S(1)} %get-tuple-element.48), channel_id=1, source_target_pairs={{0,8},{8,16},{16,24},{24,32},{32,40},{40,48},{48,56},{56,64},{64,7... | collective-permute-start | bytes 1572872 | tf_op jit(solution)/shard_map/ppermute | solution.py:368
  194.4 17.2 %collective-permute-start.13 = (f32[64,16,128]{2,1,0:T(8,128)S(1)}, f32[64,16,128]{2,1,0:T(8,128)S(1)}, u32[]{:S(2)}, u32[]{:S(2)}) collective-permute-start(f32[64,16,128]{2,1,0:T(8,128)S(1)} %get-tuple-element.49), channel_id=1, source_target_pairs={{8,0},{16,8},{24,16},{32,24},{40,32},{48,40},{56,48},{64,56},{72,6... | collective-permute-start | bytes 1572872 | tf_op jit(solution)/shard_map/ppermute | solution.py:368
  200.3 17.2 %collective-permute-start.14 = (f32[30,32,128]{2,1,0:T(8,128)S(1)}, f32[30,32,128]{2,1,0:T(8,128)S(1)}, u32[]{:S(2)}, u32[]{:S(2)}) collective-permute-start(f32[30,32,128]{2,1,0:T(8,128)S(1)} %get-tuple-element.50), channel_id=1, source_target_pairs={{0,1},{1,2},{2,3},{3,4},{4,5},{5,6},{6,7},{8,9},{9,10},{10,11},{11... | collective-permute-start | bytes 1474568 | tf_op jit(solution)/shard_map/ppermute | solution.py:368
  203.9 13.6 %collective-permute-start.16 = (f32[30,32,128]{2,1,0:T(8,128)S(1)}, f32[30,32,128]{2,1,0:T(8,128)S(1)}, u32[]{:S(2)}, u32[]{:S(2)}) collective-permute-start(f32[30,32,128]{2,1,0:T(8,128)S(1)} %get-tuple-element.51), channel_id=1, source_target_pairs={{1,0},{2,1},{3,2},{4,3},{5,4},{6,5},{7,6},{9,8},{10,9},{11,10},{12... | collective-permute-start | bytes 1474568 | tf_op jit(solution)/shard_map/ppermute | solution.py:368
  211.7 9.6 %collective-permute-start.15 = (f32[30,32,128]{2,1,0:T(8,128)S(1)}, f32[30,32,128]{2,1,0:T(8,128)S(1)}, u32[]{:S(2)}, u32[]{:S(2)}) collective-permute-start(f32[30,32,128]{2,1,0:T(8,128)S(1)} %pad_maximum_fusion.2), channel_id=1, source_target_pairs={{0,1},{1,2},{2,3},{3,4},{4,5},{5,6},{6,7},{8,9},{9,10},{10,11},{11... | collective-permute-start | bytes 1474568 | tf_op jit(solution)/shard_map/ppermute | solution.py:368
  215.6 10.1 %collective-permute-start.17 = (f32[30,32,128]{2,1,0:T(8,128)S(1)}, f32[30,32,128]{2,1,0:T(8,128)S(1)}, u32[]{:S(2)}, u32[]{:S(2)}) collective-permute-start(f32[30,32,128]{2,1,0:T(8,128)S(1)} %pad_maximum_fusion.3), channel_id=1, source_target_pairs={{1,0},{2,1},{3,2},{4,3},{5,4},{6,5},{7,6},{9,8},{10,9},{11,10},{12... | collective-permute-start | bytes 1474568 | tf_op jit(solution)/shard_map/ppermute | solution.py:368
  271.5 10.4 %collective-permute-start.21 = (f32[30,32,128]{2,1,0:T(8,128)}, f32[30,32,128]{2,1,0:T(8,128)S(1)}, u32[]{:S(2)}, u32[]{:S(2)}) collective-permute-start(f32[30,32,128]{2,1,0:T(8,128)} %get-tuple-element.58), channel_id=1, source_target_pairs={{1,0},{2,1},{3,2},{4,3},{5,4},{6,5},{7,6},{9,8},{10,9},{11,10},{12... | collective-permute-start | bytes 1474568 | tf_op jit(solution)/shard_map/ppermute | solution.py:368
  284.1 20.7 %collective-permute-start.22 = (f32[64,16,128]{2,1,0:T(8,128)S(1)}, f32[64,16,128]{2,1,0:T(8,128)S(1)}, u32[]{:S(2)}, u32[]{:S(2)}) collective-permute-start(f32[64,16,128]{2,1,0:T(8,128)S(1)} %get-tuple-element.59), channel_id=1, source_target_pairs={{0,8},{8,16},{16,24},{24,32},{32,40},{40,48},{48,56},{56,64},{64,7... | collective-permute-start | bytes 1572872 | tf_op jit(solution)/shard_map/ppermute | solution.py:368
  286.0 18.8 %collective-permute-start.23 = (f32[64,16,128]{2,1,0:T(8,128)S(1)}, f32[64,16,128]{2,1,0:T(8,128)S(1)}, u32[]{:S(2)}, u32[]{:S(2)}) collective-permute-start(f32[64,16,128]{2,1,0:T(8,128)S(1)} %get-tuple-element.60), channel_id=1, source_target_pairs={{8,0},{16,8},{24,16},{32,24},{40,32},{48,40},{56,48},{64,56},{72,6... | collective-permute-start | bytes 1572872 | tf_op jit(solution)/shard_map/ppermute | solution.py:368
  292.2 8.2 %collective-permute-start.18 = (f32[30,32,128]{2,1,0:T(8,128)}, f32[30,32,128]{2,1,0:T(8,128)S(1)}, u32[]{:S(2)}, u32[]{:S(2)}) collective-permute-start(f32[30,32,128]{2,1,0:T(8,128)} %get-tuple-element.53), channel_id=1, source_target_pairs={{0,1},{1,2},{2,3},{3,4},{4,5},{5,6},{6,7},{8,9},{9,10},{10,11},{11... | collective-permute-start | bytes 1474568 | tf_op jit(solution)/shard_map/ppermute | solution.py:368
  294.4 10.4 %collective-permute-start.19 = (f32[30,32,128]{2,1,0:T(8,128)}, f32[30,32,128]{2,1,0:T(8,128)S(1)}, u32[]{:S(2)}, u32[]{:S(2)}) collective-permute-start(f32[30,32,128]{2,1,0:T(8,128)} %get-tuple-element.54), channel_id=1, source_target_pairs={{1,0},{2,1},{3,2},{4,3},{5,4},{6,5},{7,6},{9,8},{10,9},{11,10},{12... | collective-permute-start | bytes 1474568 | tf_op jit(solution)/shard_map/ppermute | solution.py:368
  (34 other events, 462.9 us)

commit v2 on v1

v2 whole, which is shorter than its diff:
```python
import functools

import jax
import jax.numpy as jnp
from jax import lax
from jax.experimental import pallas as pl
from jax.experimental.pallas import tpu as pltpu
from jax.sharding import PartitionSpec as P

BLK_DEV = 4
BX = 8
OFF = 8
ITERS = 2
V = 6
NY = 128
DZ = 64
DX = 32
RZ = 30
PZ = 32
RX = 16
EZ = DZ + 2 * PZ
EX = DX + 2 * RX
ROWS = V * DX
MIB = 1 << 20

exact_mode = lax.Precision.HIGHEST


def split(value):
    high = value.astype(jnp.bfloat16)
    low = (value - high.astype(jnp.float32)).astype(jnp.bfloat16)
    return high, low


def mul(a, b):
    return jnp.dot(a, b, preferred_element_type=jnp.float32)


def pair_columns(value, rows):
    return value[:, : value.shape[1] // 2], value[:, value.shape[1] // 2 :]


def blur_x(xf, planes, store):
    both = jnp.concatenate(planes, axis=1)
    high, low = split(both)
    out = mul(xf, jnp.concatenate([high, low, high], axis=0))
    store(out[:, :NY], out[:, NY:])


def forward_x(s_ref, xf_ref, est, left, right, topc, tops, botc, bots):
    zeros = jnp.zeros((2, ROWS, NY), jnp.float32)
    s_ref[0:2, :ROWS] = zeros
    s_ref[EZ - 2 : EZ, :ROWS] = zeros

    def put(base):
        def store(first, second):
            s_ref[base, :ROWS] = first
            s_ref[base + 1, :ROWS] = second

        return store

    def rim(centre, sides, start):
        @pl.loop(0, RZ // 6)
        def _(group):
            for u in range(3):
                at = 6 * group + 2 * u
                planes = []
                for z in (at, at + 1):
                    planes.append(
                        jnp.concatenate([sides[z, :RX], centre[z], sides[z, RX:]], axis=0)
                    )
                blur_x(xf_ref[...], planes, put(start + at))

    @pl.loop(0, DZ // 8)
    def _(group):
        for u in range(4):
            at = 8 * group + 2 * u
            planes = []
            for z in (at, at + 1):
                planes.append(jnp.concatenate([left[z], est[z], right[z]], axis=0))
            blur_x(xf_ref[...], planes, put(PZ + at))

    rim(topc, tops, PZ - RZ)
    rim(botc, bots, PZ + DZ)


def halves(value):
    middle = value.shape[1] // 2
    return value[:, :middle], value[:, middle:]


def forward_tile(s_ref, zf_ref, yf_ref, view, row):
    field = jnp.swapaxes(s_ref[:, pl.ds(row, BX), :], 0, 1)
    parts = []
    for p in range(BX // 2):
        high, low = split(jnp.concatenate([field[2 * p], field[2 * p + 1]], axis=1))
        out = mul(zf_ref[view], jnp.concatenate([high, low], axis=0))
        parts += halves(out[:DZ] + out[DZ:])
    high, low = split(jnp.concatenate(parts, axis=0))
    first, second = halves(mul(jnp.concatenate([high, low], axis=1), yf_ref[view]))
    return first + second


def backward_tile(zb_ref, yb_ref, view, ratio):
    high, low = split(ratio)
    first, second = halves(mul(jnp.concatenate([high, low], axis=1), yb_ref[view]))
    out = first + second
    parts = []
    for p in range(BX // 2):
        at = 2 * p * DZ
        high, low = split(jnp.concatenate([out[at : at + DZ], out[at + DZ : at + 2 * DZ]], axis=1))
        parts += halves(mul(zb_ref[view], jnp.concatenate([high, low, high], axis=0)))
    return jnp.swapaxes(jnp.stack(parts, axis=0), 0, 1)


def backward_x(s_ref, xb_ref, midc, midl, midr, topc, tops, botc, bots):
    def spread_pair(base):
        both = jnp.concatenate([s_ref[base, :ROWS], s_ref[base + 1, :ROWS]], axis=1)
        high, low = split(both)
        out = mul(xb_ref[...], jnp.concatenate([high, low], axis=0))
        return halves(out[:EX] + out[EX:])

    def rim(centre, sides, start):
        @pl.loop(0, RZ // 6)
        def _(group):
            for u in range(3):
                at = 6 * group + 2 * u
                for i, plane in enumerate(spread_pair(start + at)):
                    sides[at + i] = jnp.concatenate([plane[:RX], plane[RX + DX :]], axis=0)
                    centre[at + i] = plane[RX : RX + DX]

    rim(topc, tops, PZ - RZ)
    rim(botc, bots, PZ + DZ)

    @pl.loop(0, DZ // 8)
    def _(group):
        for u in range(4):
            at = 8 * group + 2 * u
            for i, plane in enumerate(spread_pair(PZ + at)):
                midl[at + i] = plane[:RX]
                midc[at + i] = plane[RX : RX + DX]
                midr[at + i] = plane[RX + DX :]


def compact(slots, meta, order):
    count = jnp.int32(0)
    for slot in range(slots):
        order[count] = slot
        count = count + meta[slot]
    order[count] = slots
    return count


def clear_absent(slots, meta, s_ref):
    @pl.loop(0, V * BLK_DEV)
    def _(cell):
        @pl.when(meta[3 * (slots + 1) + cell] == 0)
        def _():
            s_ref[:, pl.ds(pl.multiple_of(cell * BX, BX), BX), :] = jnp.zeros(
                (EZ, BX, NY), jnp.float32
            )


def visit_pairs(slots, meta, order, s_ref, data, zb, yb, predict):
    count = compact(slots, meta, order)

    @pl.loop(0, (count + 1) // 2)
    def _(k):
        slot = (order[2 * k], order[2 * k + 1])
        view = [meta[slots + 1 + i] for i in slot]
        cell = [meta[2 * (slots + 1) + i] for i in slot]
        row = [pl.multiple_of(i * BX, BX) for i in cell]
        blurred = [predict(view[i], cell[i], row[i]) for i in (0, 1)]
        ratio = [data[jnp.minimum(slot[i], slots - 1), : BX * DZ] / blurred[i] for i in (0, 1)]
        out = [backward_tile(zb, yb, view[i], ratio[i]) for i in (0, 1)]
        for i in (0, 1):
            s_ref[:, pl.ds(row[i], BX), :] = out[i]


def sweep_body(slots, meta, est, left, right, topc, tops, botc, bots, data, xf, xb, zf, zb, yf, yb,
               omidc, omidl, omidr, otopc, otops, obotc, obots, s_ref, order):
    forward_x(s_ref, xf, est, left, right, topc, tops, botc, bots)
    clear_absent(slots, meta, s_ref)

    def predict(view, cell, row):
        return forward_tile(s_ref, zf, yf, view, row)

    visit_pairs(slots, meta, order, s_ref, data, zb, yb, predict)
    backward_x(s_ref, xb, omidc, omidl, omidr, otopc, otops, obotc, obots)


def blur_body(est, left, right, topc, tops, botc, bots, xf, zf, yf, out, s_ref):
    forward_x(s_ref, xf, est, left, right, topc, tops, botc, bots)

    @pl.loop(0, V * BLK_DEV // 2)
    def _(k):
        view = k // (BLK_DEV // 2)
        cells = (2 * k, 2 * k + 1)
        results = [
            forward_tile(s_ref, zf, yf, view, pl.multiple_of(cell * BX, BX)) for cell in cells
        ]
        for cell, result in zip(cells, results):
            out[cell] = result


def spread_body(slots, meta, blurred, data, xb, zb, yb,
                omidc, omidl, omidr, otopc, otops, obotc, obots, s_ref, order):
    clear_absent(slots, meta, s_ref)

    def predict(view, cell, row):
        return blurred[jnp.minimum(cell, V * BLK_DEV - 1)]

    visit_pairs(slots, meta, order, s_ref, data, zb, yb, predict)
    backward_x(s_ref, xb, omidc, omidl, omidr, otopc, otops, obotc, obots)


def f32(*shape):
    return jax.ShapeDtypeStruct(shape, jnp.float32)


VM = pl.BlockSpec(memory_space=pltpu.VMEM)
SM = pl.BlockSpec(memory_space=pltpu.SMEM)
PIECES = (
    f32(DZ, DX, NY),
    f32(DZ, RX, NY),
    f32(DZ, RX, NY),
    f32(RZ, DX, NY),
    f32(RZ, 2 * RX, NY),
    f32(RZ, DX, NY),
    f32(RZ, 2 * RX, NY),
)


def params(mib):
    return pltpu.CompilerParams(vmem_limit_bytes=mib * MIB)


FIELD = pltpu.VMEM((EZ, ROWS + BX, NY), jnp.float32)


def sweep(meta, pieces, data, tables):
    slots = data.shape[0]
    xf, xb, zf, zb, yf, yb = tables
    return pl.pallas_call(
        functools.partial(sweep_body, slots),
        out_shape=PIECES,
        in_specs=[SM] + [VM] * 14,
        out_specs=[VM] * 7,
        scratch_shapes=[FIELD, pltpu.SMEM((slots + 1,), jnp.int32)],
        compiler_params=params(36),
        name="sweep",
    )(meta, *pieces, data, xf, xb, zf, zb, yf, yb)


def blur_all(pieces, tables):
    xf, xb, zf, zb, yf, yb = tables
    return pl.pallas_call(
        blur_body,
        out_shape=f32(V * BLK_DEV, BX * DZ, NY),
        in_specs=[VM] * 10,
        out_specs=VM,
        scratch_shapes=[FIELD],
        compiler_params=params(34),
        name="blur_all",
    )(*pieces, xf, zf, yf)


def spread_ratio(meta, blurred, data, tables):
    slots = data.shape[0]
    xf, xb, zf, zb, yf, yb = tables
    return pl.pallas_call(
        functools.partial(spread_body, slots),
        out_shape=PIECES,
        in_specs=[SM] + [VM] * 5,
        out_specs=[VM] * 7,
        scratch_shapes=[FIELD, pltpu.SMEM((slots + 1,), jnp.int32)],
        compiler_params=params(34),
        name="spread_ratio",
    )(meta, blurred, data, xb, zb, yb)


def place_body(owner, pair, shift, tiles, out, staged, labels, sem, label_sem):
    count = tiles.shape[0]
    slots = out.shape[0]
    lane = lax.broadcasted_iota(jnp.int32, (8, NY), 1)
    values = jnp.zeros((8, NY), jnp.int32)
    for k in range(count):
        values = jnp.where(lane == k, pair[k], values)
        values = jnp.where(lane == count + k, shift[k], values)
    labels[...] = values.astype(jnp.float32)
    copies = []
    for slot in range(slots):
        copies.append(
            pltpu.make_async_copy(
                labels, out.at[slot, pl.ds(BX * DZ, 8)], label_sem.at[slot]
            )
        )
        copies[-1].start()
    column = lax.broadcasted_iota(jnp.int32, (DZ, BX, NY), 2)
    for k in range(count):
        moved = pltpu.roll(tiles[k], (shift[k] + NY) % NY, 2)
        source = column - shift[k]
        moved = jnp.where((source >= 0) & (source < NY), moved, 0.0)
        staged[k] = jnp.swapaxes(moved, 0, 1).reshape(BX * DZ, NY)
        copies.append(
            pltpu.make_async_copy(staged.at[k], out.at[owner[k], pl.ds(0, BX * DZ)], sem.at[k])
        )
        copies[-1].start()
    for copy in copies:
        copy.wait()


def place(owner, pair, shift, tiles, slots):
    count = tiles.shape[0]
    return pl.pallas_call(
        place_body,
        out_shape=f32(slots, BX * DZ + 8, NY),
        in_specs=[SM, SM, SM, VM],
        out_specs=pl.BlockSpec(memory_space=pltpu.HBM),
        scratch_shapes=[
            pltpu.VMEM((count, BX * DZ, NY), jnp.float32),
            pltpu.VMEM((8, NY), jnp.float32),
            pltpu.SemaphoreType.DMA((count,)),
            pltpu.SemaphoreType.DMA((slots,)),
        ],
        compiler_params=params(32),
        name="place",
    )(owner, pair, shift, tiles)


def rims_body(midl, midr, above, below, outl, outr):
    for mid, out, at in ((midl, outl, 0), (midr, outr, RX)):
        cols = pl.ds(at, RX)
        out[:RZ] = mid[:RZ] + above[:, cols]
        out[RZ : DZ - RZ] = mid[RZ : DZ - RZ]
        out[DZ - RZ :] = mid[DZ - RZ :] + below[:, cols]


def fold_rims(midl, midr, above, below):
    return pl.pallas_call(
        rims_body,
        out_shape=(f32(DZ, RX, NY), f32(DZ, RX, NY)),
        in_specs=[VM] * 4,
        out_specs=[VM] * 2,
        compiler_params=pltpu.CompilerParams(vmem_limit_bytes=32 * MIB),
        name="fold_rims",
    )(midl, midr, above, below)


def update_body(wz, est, midc, above, below, froml, fromr, gain, *outs):
    def step(z, extra):
        total = midc[z]
        if extra is not None:
            total = total + extra
        total = total + jnp.concatenate([froml[z], fromr[z]], axis=0)
        weight = wz[0, z] * gain[0]
        for view in range(1, V):
            weight = weight + wz[view, z] * gain[view]
        return est[z] * total / jnp.maximum(weight, 1.0)

    def write(z, new):
        outs[0][z] = new
        if len(outs) > 1:
            outs[1][z] = new[:RX]
            outs[2][z] = new[RX:]

    @pl.loop(0, RZ)
    def _(z):
        new = step(z, above[z])
        write(z, new)
        if len(outs) > 1:
            outs[3][z] = new

    for z in range(RZ, DZ - RZ):
        write(z, step(z, None))

    @pl.loop(0, RZ)
    def _(k):
        new = step(k + DZ - RZ, below[k])
        write(k + DZ - RZ, new)
        if len(outs) > 1:
            outs[4][k] = new


def update(wz, est, midc, above, below, froml, fromr, gain, last):
    shapes = [f32(DZ, DX, NY)]
    if not last:
        shapes += [f32(DZ, RX, NY)] * 2 + [f32(RZ, DX, NY)] * 2
    return pl.pallas_call(
        update_body,
        out_shape=tuple(shapes),
        in_specs=[SM] + [VM] * 7,
        out_specs=[VM] * len(shapes),
        compiler_params=pltpu.CompilerParams(vmem_limit_bytes=32 * MIB),
        name="update",
    )(wz, est, midc, above, below, froml, fromr, gain)


def band(row, rows, first):
    table = jnp.broadcast_to(row, (rows, row.shape[1]))
    return pltpu.roll(table, first % row.shape[1], 1, stride=1, stride_axis=0)


def tables_body(kz, kx, ky, xf, xb, zf, zb, yf, yb, yt):
    for view in range(V):
        full = band(kz[view : view + 1], DZ, PZ - RZ)
        high, low = split(full)
        zf[view] = jnp.concatenate(
            [jnp.concatenate([high, high], axis=1), jnp.concatenate([low, low], axis=1)], axis=0
        )
        high, low = split(full.T)
        zb[view] = jnp.concatenate([high, high, low], axis=1)
        full = band(ky[view : view + 1], NY, -15)[:, :NY]
        yt[view] = full
        high, low = split(full)
        half = jnp.concatenate([high, low], axis=1)
        yb[view] = jnp.concatenate([half, half], axis=0)
        high, low = split(full.T)
        half = jnp.concatenate([high, low], axis=1)
        yf[view] = jnp.concatenate([half, half], axis=0)
    full = jnp.concatenate([band(kx[v : v + 1], DX, RX - 15) for v in range(V)], axis=0)
    high, low = split(full[:, :EX])
    xf[...] = jnp.concatenate([high, high, low], axis=1)
    high, low = split(full.T[:EX])
    both = jnp.concatenate([high, low], axis=0)
    xb[...] = jnp.concatenate([both, both], axis=1)


def make_tables(kernel_z, kernel_x, kernel_y):
    def bf16(*shape):
        return jax.ShapeDtypeStruct(shape, jnp.bfloat16)

    def padded(kernel, lanes):
        return jnp.pad(kernel, ((0, 8 - V), (0, lanes - kernel.shape[1])))

    return pl.pallas_call(
        tables_body,
        out_shape=(
            bf16(ROWS, 3 * EX),
            bf16(2 * EX, 2 * ROWS),
            bf16(V, 2 * DZ, 2 * EZ),
            bf16(V, EZ, 3 * DZ),
            bf16(V, 2 * NY, 2 * NY),
            bf16(V, 2 * NY, 2 * NY),
            f32(V, NY, NY),
        ),
        in_specs=[VM] * 3,
        out_specs=[VM] * 7,
        compiler_params=params(32),
        name="tables",
    )(padded(kernel_z, 128), padded(kernel_x, 128), padded(kernel_y, 256))


def send(value, axis, step):
    count = lax.axis_size(axis)
    if step > 0:
        pairs = [(i, i + 1) for i in range(count - 1)]
    else:
        pairs = [(i + 1, i) for i in range(count - 1)]
    return lax.ppermute(value, axis, pairs)


def halo_columns(coll, colr):
    return send(colr, "blocks", 1), send(coll, "blocks", -1)


def halo(est, left, right, planet, planeb):
    botc = send(planet, "depth", -1)
    topc = send(planeb, "depth", 1)
    sides_t = jnp.concatenate([left[:RZ], right[:RZ]], axis=1)
    sides_b = jnp.concatenate([left[DZ - RZ :], right[DZ - RZ :]], axis=1)
    bots = send(sides_t, "depth", -1)
    tops = send(sides_b, "depth", 1)
    return est, left, right, topc, tops, botc, bots


def weight_parts(pairs, shifts, kernel_z, kernel_x, kernel_y, yt, all_blocks):
    planes = lax.axis_size("depth") * DZ
    view = pairs // all_blocks
    block = pairs % all_blocks
    taps = jnp.arange(kernel_z.shape[1])[None, :]
    z = lax.axis_index("depth") * DZ + jnp.arange(DZ)[:, None]
    reached = ((z - taps + RZ >= 0) & (z - taps + RZ < planes)).astype(jnp.float32)
    wz = jnp.einsum("va,za->vz", kernel_z, reached, precision=exact_mode)
    hot = (view[:, None] == jnp.arange(V)[None, :]).astype(jnp.float32)
    x = lax.axis_index("blocks") * DX + jnp.arange(DX)
    lead = x[None, :, None] + 15 - BX * block[:, None, None] - jnp.arange(kernel_x.shape[1])[None, None, :]
    covers = ((lead >= 0) & (lead < BX)).astype(jnp.float32)
    along_x = jnp.einsum("txb,vb->vtx", covers, kernel_x, precision=exact_mode) * hot.T[:, :, None]
    y = jnp.arange(NY)
    inside = (y[None, :] >= shifts[:, None]) & (y[None, :] < NY + shifts[:, None])
    along_y = jnp.einsum("ty,vyc->vtc", inside.astype(jnp.float32), yt, precision=exact_mode)
    gain = jnp.einsum("vtx,vtc->vxc", along_x, along_y, precision=exact_mode)
    return wz, gain


def local(estimate0, tiles, psf_z, psf_x, psf_y, tile_pair, tile_shift):
    owners = lax.axis_size("blocks")
    all_blocks = BLK_DEV * owners
    me = lax.axis_index("blocks")
    kernel_z = psf_z / jnp.sum(psf_z, axis=1, keepdims=True)
    kernel_x = psf_x / jnp.sum(psf_x, axis=1, keepdims=True)
    kernel_y = psf_y / jnp.sum(psf_y, axis=1, keepdims=True)

    held = tile_pair % all_blocks // BLK_DEV
    est = estimate0
    left, right = halo_columns(est[:, :RX], est[:, DX - RX :])
    sent = place(held, tile_pair, tile_shift, tiles, owners)
    sent, left, right = lax.optimization_barrier((sent, left, right))
    got = lax.all_to_all(sent, "blocks", split_axis=0, concat_axis=0, tiled=True)
    *tables, yt = make_tables(kernel_z, kernel_x, kernel_y)

    count = tiles.shape[0]
    labels = got[:, BX * DZ, : 2 * count].astype(jnp.int32)
    pairs, shifts = labels[:, :count], labels[:, count:]
    mine = pairs % all_blocks // BLK_DEV == me
    live = jnp.max(mine.astype(jnp.int32), axis=1)
    got_pair = jnp.sum(jnp.where(mine, pairs, 0), axis=1)
    view = got_pair // all_blocks
    cell = jnp.where(live > 0, view * BLK_DEV + got_pair % all_blocks - me * BLK_DEV, V * BLK_DEV)
    hit = cell[None, :] == jnp.arange(V * BLK_DEV)[:, None]
    present = jnp.max(hit.astype(jnp.int32), axis=1)
    end = lambda value: jnp.full((1,), value, jnp.int32)
    meta = jnp.concatenate([live, end(0), view, end(0), cell, end(V * BLK_DEV), present])
    meta = meta.astype(jnp.int32)
    wz, gain = weight_parts(
        pairs.reshape(-1), shifts.reshape(-1), kernel_z, kernel_x, kernel_y, yt, all_blocks
    )

    planes = est[:RZ], est[DZ - RZ :]
    for iteration in range(ITERS):
        pieces = halo(est, left, right, *planes)
        if iteration == 0:
            spread = spread_ratio(meta, blur_all(pieces, tables), got, tables)
        else:
            spread = sweep(meta, pieces, got, tables)
        midc, midl, midr, topc, tops, botc, bots = spread
        below_s = send(tops, "depth", -1)
        above_s = send(bots, "depth", 1)
        below_c = send(topc, "depth", -1)
        above_c = send(botc, "depth", 1)
        rim_l, rim_r = fold_rims(midl, midr, above_s, below_s)
        fromr = send(rim_l, "blocks", -1)
        froml = send(rim_r, "blocks", 1)
        last = iteration == ITERS - 1
        new = update(wz, est, midc, above_c, below_c, froml, fromr, gain, last)
        est = new[0]
        if not last:
            left, right = halo_columns(new[1], new[2])
            planes = new[3:]
    return est


def solution(mesh):
    in_specs = (
        P("depth", "blocks", None),
        P("blocks", "depth", None, None),
        P(),
        P(),
        P(),
        P("blocks"),
        P("blocks"),
    )
    out_specs = P("depth", "blocks", None)
    return jax.shard_map(local, mesh=mesh, in_specs=in_specs, out_specs=out_specs, check_vma=False)
```

time: 310 us -> 239 us (0.77)
  the two profiles are of different devices: /device:TPU:99 before, /device:TPU:34 now
where the time goes in v2:
time: 239 us; the launch traced here: 235 us
  starting transfers between devices  84.9 us (36%)
  waiting for transfers between devices  71.9 us (30%)
  Pallas kernels  52.5 us (22%)
  local copies, waits for them, and re-layouts  18.9 us (8%)
  other arithmetic  4.34 us (2%)
    ppermute x24, starting transfers between devices, send(): return lax.ppermute(value, axis, pairs)  79.1 us
    ppermute x24, waiting for transfers between devices, send(): return lax.ppermute(value, axis, pairs)  51 us
    all_to_all x1, waiting for transfers between devices, local(): lax.all_to_all(sent, 'blocks', split_axis=0, concat_axis=0, tiled=True)  20.9 us
    pallas_call x1, Pallas kernels, sweep(): pl.pallas_call(functools.partial(sweep_body, slots), out_shape=PIECES, in...  17.3 us
    unnamed x50, local copies, waits for them, and re-layouts  16.2 us
    pallas_call x1, Pallas kernels, blur_all(): pl.pallas_call(blur_body, out_shape=f32(V * BLK_DEV, BX * DZ, NY), in_spe...  14.7 us
    pallas_call x1, Pallas kernels, spread_ratio(): pl.pallas_call(functools.partial(spread_body, slots), out_shape=PIECES, i...  11.6 us
    all_to_all x1, starting transfers between devices, local(): lax.all_to_all(sent, 'blocks', split_axis=0, concat_axis=0, tiled=True)  5.73 us
  transfers between devices with their start and end apart: 25, of which 17 were waited for; matrix products, arithmetic and copies ran while one was open for 3% of the time, Pallas kernels for 8%

profile of v2, /device:TPU:34, one launch (start us, length us, event | category | flops | bytes accessed | tf_op | source)
XLA Modules:
  0.0 235.4 jit_solution(4279040714464793939)
XLA Ops:
  1.3 4.5 %collective-permute-start.1 = (f32[64,16,128]{2,1,0:T(8,128)S(1)}, f32[64,16,128]{2,1,0:T(8,128)S(1)}, u32[]{:S(2)}, u32[]{:S(2)}) collective-permute-start(f32[64,16,128]{2,1,0:T(8,128)S(1)} %get-tuple-element.77), channel_id=1, source_target_pairs={{8,0},{16,8},{24,16},{32,24},{40,32},{48,40},{56,48},{64,56},{72,6... | collective-permute-start | bytes 1572872 | tf_op jit(solution)/shard_map/ppermute | solution.py:460
  16.9 6.2 %collective-permute-done.left = f32[64,16,128]{2,1,0:T(8,128)S(1)} collective-permute-done((f32[64,16,128]{2,1,0:T(8,128)S(1)}, f32[64,16,128]{2,1,0:T(8,128)S(1)}, u32[]{:S(2)}, u32[]{:S(2)}) %collective-permute-start) | collective-permute-done | bytes 524320 | tf_op jit(solution)/shard_map/ppermute | solution.py:460
  23.1 5.7 %all-to-all-start = ((f32[16,520,128]{2,1,0:T(8,128)}), f32[16,520,128]{2,1,0:T(8,128)}, u32[]{:S(2)}, u32[]{:S(2)}) async-start(f32[16,520,128]{2,1,0:T(8,128)} %copy-done.2), calls=%async_computation | async-start | bytes 8519680 | tf_op jit(solution)/shard_map/all_to_all | solution.py:510
  35.7 3.0 %collective-permute-start.3 = (f32[30,32,128]{2,1,0:T(8,128)}, f32[30,32,128]{2,1,0:T(8,128)}, u32[]{:S(2)}, u32[]{:S(2)}) collective-permute-start(f32[30,32,128]{2,1,0:T(8,128)} %pad_maximum_fusion), channel_id=1, source_target_pairs={{0,1},{1,2},{2,3},{3,4},{4,5},{5,6},{6,7},{8,9},{9,10},{10,11},{11... | collective-permute-start | bytes 1474568 | tf_op jit(solution)/shard_map/ppermute | solution.py:460
  49.8 14.7 %blur_all.1.blurred = f32[24,512,128]{2,1,0:T(8,128)S(1)} custom-call(f32[64,32,128]{2,1,0:T(8,128)S(1)} %copy-done.3, f32[64,16,128]{2,1,0:T(8,128)S(1)} %copy-done.6, f32[64,16,128]{2,1,0:T(8,128)S(1)} %collective-permute-done.1.right, f32[30,32,128]{2,1,0:T(8,128)} %collective-permute-done.2.topc, f32[30,32,128]{2,1,0:T(8,128)} %collective-permute-done.3.tops, ...), custom_call_target="tpu_custom_call" | custom-call | tf_op jit(solution)/shard_map/blur_all/pallas_call | solution.py:257
  67.8 20.9 %all-to-all-done.data = f32[16,520,128]{2,1,0:T(8,128)} async-done(((f32[16,520,128]{2,1,0:T(8,128)}), f32[16,520,128]{2,1,0:T(8,128)}, u32[]{:S(2)}, u32[]{:S(2)}) %all-to-all-start) | async-done | bytes 4259872 | tf_op jit(solution)/shard_map/all_to_all | solution.py:510
  94.7 11.6 %spread_ratio.1 = (f32[64,32,128]{2,1,0:T(8,128)S(1)}, f32[64,16,128]{2,1,0:T(8,128)S(1)}, f32[64,16,128]{2,1,0:T(8,128)S(1)}, f32[30,32,128]{2,1,0:T(8,128)S(1)...) custom-call(s32[75]{0:T(128)S(1)} %concatenate.15.meta, ...), custom_call_target="tpu_custom_call" | custom-call | tf_op jit(solution)/shard_map/spread_ratio/pallas_call | solution.py:271
  108.3 3.6 %collective-permute-start.7 = (f32[30,32,128]{2,1,0:T(8,128)S(1)}, f32[30,32,128]{2,1,0:T(8,128)S(1)}, u32[]{:S(2)}, u32[]{:S(2)}) collective-permute-start(f32[30,32,128]{2,1,0:T(8,128)S(1)} %get-tuple-element.49), channel_id=1, source_target_pairs={{1,0},{2,1},{3,2},{4,3},{5,4},{6,5},{7,6},{9,8},{10,9},{11,10},{12... | collective-permute-start | bytes 1474568 | tf_op jit(solution)/shard_map/ppermute | solution.py:460
  113.9 3.6 %collective-permute-start.9 = (f32[30,32,128]{2,1,0:T(8,128)S(1)}, f32[30,32,128]{2,1,0:T(8,128)S(1)}, u32[]{:S(2)}, u32[]{:S(2)}) collective-permute-start(f32[30,32,128]{2,1,0:T(8,128)S(1)} %get-tuple-element.53), channel_id=1, source_target_pairs={{1,0},{2,1},{3,2},{4,3},{5,4},{6,5},{7,6},{9,8},{10,9},{11,10},{12... | collective-permute-start | bytes 1474568 | tf_op jit(solution)/shard_map/ppermute | solution.py:460
  118.0 4.1 %collective-permute-done.8.above = f32[30,32,128]{2,1,0:T(8,128)S(1)} collective-permute-done((f32[30,32,128]{2,1,0:T(8,128)S(1)}, f32[30,32,128]{2,1,0:T(8,128)S(1)}, u32[]{:S(2)}, u32[]{:S(2)}) %collective-permute-start.8) | collective-permute-done | bytes 491552 | tf_op jit(solution)/shard_map/ppermute | solution.py:460
  125.9 6.0 %collective-permute-start.11 = (f32[64,16,128]{2,1,0:T(8,128)S(1)}, f32[64,16,128]{2,1,0:T(8,128)S(1)}, u32[]{:S(2)}, u32[]{:S(2)}) collective-permute-start(f32[64,16,128]{2,1,0:T(8,128)S(1)} %get-tuple-element.55), channel_id=1, source_target_pairs={{8,0},{16,8},{24,16},{32,24},{40,32},{48,40},{56,48},{64,56},{72,6... | collective-permute-start | bytes 1572872 | tf_op jit(solution)/shard_map/ppermute | solution.py:460
  133.3 8.6 %collective-permute-done.10.froml = f32[64,16,128]{2,1,0:T(8,128)S(1)} collective-permute-done((f32[64,16,128]{2,1,0:T(8,128)S(1)}, f32[64,16,128]{2,1,0:T(8,128)S(1)}, u32[]{:S(2)}, u32[]{:S(2)}) %collective-permute-start.10) | collective-permute-done | bytes 524320 | tf_op jit(solution)/shard_map/ppermute | solution.py:460
  147.7 6.5 %collective-permute-start.13 = (f32[64,16,128]{2,1,0:T(8,128)S(1)}, f32[64,16,128]{2,1,0:T(8,128)S(1)}, u32[]{:S(2)}, u32[]{:S(2)}) collective-permute-start(f32[64,16,128]{2,1,0:T(8,128)S(1)} %get-tuple-element.59), channel_id=1, source_target_pairs={{8,0},{16,8},{24,16},{32,24},{40,32},{48,40},{56,48},{64,56},{72,6... | collective-permute-start | bytes 1572872 | tf_op jit(solution)/shard_map/ppermute | solution.py:460
  156.2 3.6 %collective-permute-start.16 = (f32[30,32,128]{2,1,0:T(8,128)S(1)}, f32[30,32,128]{2,1,0:T(8,128)S(1)}, u32[]{:S(2)}, u32[]{:S(2)}) collective-permute-start(f32[30,32,128]{2,1,0:T(8,128)S(1)} %get-tuple-element.61), channel_id=1, source_target_pairs={{1,0},{2,1},{3,2},{4,3},{5,4},{6,5},{7,6},{9,8},{10,9},{11,10},{12... | collective-permute-start | bytes 1474568 | tf_op jit(solution)/shard_map/ppermute | solution.py:460
  159.8 4.9 %collective-permute-done.12.left = f32[64,16,128]{2,1,0:T(8,128)S(1)} collective-permute-done((f32[64,16,128]{2,1,0:T(8,128)S(1)}, f32[64,16,128]{2,1,0:T(8,128)S(1)}, u32[]{:S(2)}, u32[]{:S(2)}) %collective-permute-start.12) | collective-permute-done | bytes 524320 | tf_op jit(solution)/shard_map/ppermute | solution.py:460
  168.0 3.6 %collective-permute-start.17 = (f32[30,32,128]{2,1,0:T(8,128)S(1)}, f32[30,32,128]{2,1,0:T(8,128)S(1)}, u32[]{:S(2)}, u32[]{:S(2)}) collective-permute-start(f32[30,32,128]{2,1,0:T(8,128)S(1)} %pad_maximum_fusion.3), channel_id=1, source_target_pairs={{1,0},{2,1},{3,2},{4,3},{5,4},{6,5},{7,6},{9,8},{10,9},{11,10},{12... | collective-permute-start | bytes 1474568 | tf_op jit(solution)/shard_map/ppermute | solution.py:460
  171.7 4.5 %collective-permute-done.15.tops = f32[30,32,128]{2,1,0:T(8,128)S(1)} collective-permute-done((f32[30,32,128]{2,1,0:T(8,128)S(1)}, f32[30,32,128]{2,1,0:T(8,128)S(1)}, u32[]{:S(2)}, u32[]{:S(2)}) %collective-permute-start.15) | collective-permute-done | bytes 491552 | tf_op jit(solution)/shard_map/ppermute | solution.py:460
  178.0 17.3 %sweep.1 = (f32[64,32,128]{2,1,0:T(8,128)S(1)}, f32[64,16,128]{2,1,0:T(8,128)S(1)}, f32[64,16,128]{2,1,0:T(8,128)S(1)}, f32[30,32,128]{2,1,0:T(8,128)S(1)}, f32[...) custom-call(s32[75]{0:T(128)S(1)} %concatenate.15.meta, ...), custom_call_target="tpu_custom_call" | custom-call | tf_op jit(solution)/shard_map/sweep/pallas_call | solution.py:244
  195.3 3.7 %collective-permute-start.20 = (f32[30,32,128]{2,1,0:T(8,128)S(1)}, f32[30,32,128]{2,1,0:T(8,128)S(1)}, u32[]{:S(2)}, u32[]{:S(2)}) collective-permute-start(f32[30,32,128]{2,1,0:T(8,128)S(1)} %get-tuple-element.67), channel_id=1, source_target_pairs={{0,1},{1,2},{2,3},{3,4},{4,5},{5,6},{6,7},{8,9},{9,10},{10,11},{11... | collective-permute-start | bytes 1474568 | tf_op jit(solution)/shard_map/ppermute | solution.py:460
  201.1 4.6 %collective-permute-done.20.above = f32[30,32,128]{2,1,0:T(8,128)S(1)} collective-permute-done((f32[30,32,128]{2,1,0:T(8,128)S(1)}, f32[30,32,128]{2,1,0:T(8,128)S(1)}, u32[]{:S(2)}, u32[]{:S(2)}) %collective-permute-start.20) | collective-permute-done | bytes 491552 | tf_op jit(solution)/shard_map/ppermute | solution.py:460
  209.4 10.8 %collective-permute-start.23 = (f32[64,16,128]{2,1,0:T(8,128)S(1)}, f32[64,16,128]{2,1,0:T(8,128)S(1)}, u32[]{:S(2)}, u32[]{:S(2)}) collective-permute-start(f32[64,16,128]{2,1,0:T(8,128)S(1)} %get-tuple-element.70), channel_id=1, source_target_pairs={{8,0},{16,8},{24,16},{32,24},{40,32},{48,40},{56,48},{64,56},{72,6... | collective-permute-start | bytes 1572872 | tf_op jit(solution)/shard_map/ppermute | solution.py:460
  220.3 3.4 %collective-permute-start.18 = (f32[30,32,128]{2,1,0:T(8,128)S(1)}, f32[30,32,128]{2,1,0:T(8,128)S(1)}, u32[]{:S(2)}, u32[]{:S(2)}) collective-permute-start(f32[30,32,128]{2,1,0:T(8,128)S(1)} %get-tuple-element.63), channel_id=1, source_target_pairs={{0,1},{1,2},{2,3},{3,4},{4,5},{5,6},{6,7},{8,9},{9,10},{10,11},{11... | collective-permute-start | bytes 1474568 | tf_op jit(solution)/shard_map/ppermute | solution.py:460
  226.0 4.6 %collective-permute-done.18.above = f32[30,32,128]{2,1,0:T(8,128)S(1)} collective-permute-done((f32[30,32,128]{2,1,0:T(8,128)S(1)}, f32[30,32,128]{2,1,0:T(8,128)S(1)}, u32[]{:S(2)}, u32[]{:S(2)}) %collective-permute-start.18) | collective-permute-done | bytes 491552 | tf_op jit(solution)/shard_map/ppermute | solution.py:460
  232.4 3.0 %update.3 = f32[64,32,128]{2,1,0:T(8,128)} custom-call(f32[6,64]{1,0:T(8,128)S(1)} %fusion.15.wz, f32[64,32,128]{2,1,0:T(8,128)S(1)} %get-tuple-element.57.est, f32[64,32,128]{2,1,0:T(8,128)S(1)} %get-tuple-element.62.midc, f32[30,32,128]{2,1,0:T(8,128)S(1)} %collective-permute-done.18.above, f32[30,32,128]{2,1,0:T(8,128)S(1)} %collective-permute-done.19.below, ...), custom_call_target="tpu_custom_call" | custom-call | tf_op jit(solution)/shard_map/update/pallas_call | solution.py:389
  (122 shorter events, 71.6 us)
Async XLA Ops:
  1.3 15.6 %collective-permute-start.1 = (f32[64,16,128]{2,1,0:T(8,128)S(1)}, f32[64,16,128]{2,1,0:T(8,128)S(1)}, u32[]{:S(2)}, u32[]{:S(2)}) collective-permute-start(f32[64,16,128]{2,1,0:T(8,128)S(1)} %get-tuple-element.77), channel_id=1, source_target_pairs={{8,0},{16,8},{24,16},{32,24},{40,32},{48,40},{56,48},{64,56},{72,6... | collective-permute-start | bytes 1572872 | tf_op jit(solution)/shard_map/ppermute | solution.py:460
  5.8 17.4 %collective-permute-start = (f32[64,16,128]{2,1,0:T(8,128)S(1)}, f32[64,16,128]{2,1,0:T(8,128)S(1)}, u32[]{:S(2)}, u32[]{:S(2)}) collective-permute-start(f32[64,16,128]{2,1,0:T(8,128)S(1)} %get-tuple-element.78), channel_id=1, source_target_pairs={{0,8},{8,16},{16,24},{24,32},{32,40},{40,48},{48,56},{56,64},{64,7... | collective-permute-start | bytes 1572872 | tf_op jit(solution)/shard_map/ppermute | solution.py:460
  23.1 65.5 %all-to-all-start = ((f32[16,520,128]{2,1,0:T(8,128)}), f32[16,520,128]{2,1,0:T(8,128)}, u32[]{:S(2)}, u32[]{:S(2)}) async-start(f32[16,520,128]{2,1,0:T(8,128)} %copy-done.2), calls=%async_computation | async-start | bytes 8519680 | tf_op jit(solution)/shard_map/all_to_all | solution.py:510
  29.9 16.7 %collective-permute-start.4 = (f32[30,32,128]{2,1,0:T(8,128)}, f32[30,32,128]{2,1,0:T(8,128)}, u32[]{:S(2)}, u32[]{:S(2)}) collective-permute-start(f32[30,32,128]{2,1,0:T(8,128)} %get-tuple-element.75), channel_id=1, source_target_pairs={{1,0},{2,1},{3,2},{4,3},{5,4},{6,5},{7,6},{9,8},{10,9},{11,10},{12... | collective-permute-start | bytes 1474568 | tf_op jit(solution)/shard_map/ppermute | solution.py:460
  31.8 14.8 %collective-permute-start.2 = (f32[30,32,128]{2,1,0:T(8,128)}, f32[30,32,128]{2,1,0:T(8,128)}, u32[]{:S(2)}, u32[]{:S(2)}) collective-permute-start(f32[30,32,128]{2,1,0:T(8,128)} %get-tuple-element.76), channel_id=1, source_target_pairs={{0,1},{1,2},{2,3},{3,4},{4,5},{5,6},{6,7},{8,9},{9,10},{10,11},{11... | collective-permute-start | bytes 1474568 | tf_op jit(solution)/shard_map/ppermute | solution.py:460
  35.7 11.9 %collective-permute-start.3 = (f32[30,32,128]{2,1,0:T(8,128)}, f32[30,32,128]{2,1,0:T(8,128)}, u32[]{:S(2)}, u32[]{:S(2)}) collective-permute-start(f32[30,32,128]{2,1,0:T(8,128)} %pad_maximum_fusion), channel_id=1, source_target_pairs={{0,1},{1,2},{2,3},{3,4},{4,5},{5,6},{6,7},{8,9},{9,10},{10,11},{11... | collective-permute-start | bytes 1474568 | tf_op jit(solution)/shard_map/ppermute | solution.py:460
  39.5 9.2 %collective-permute-start.5 = (f32[30,32,128]{2,1,0:T(8,128)}, f32[30,32,128]{2,1,0:T(8,128)}, u32[]{:S(2)}, u32[]{:S(2)}) collective-permute-start(f32[30,32,128]{2,1,0:T(8,128)} %pad_maximum_fusion.1), channel_id=1, source_target_pairs={{1,0},{2,1},{3,2},{4,3},{5,4},{6,5},{7,6},{9,8},{10,9},{11,10},{12... | collective-permute-start | bytes 1474568 | tf_op jit(solution)/shard_map/ppermute | solution.py:460
  106.4 26.9 %collective-permute-start.6 = (f32[30,32,128]{2,1,0:T(8,128)S(1)}, f32[30,32,128]{2,1,0:T(8,128)S(1)}, u32[]{:S(2)}, u32[]{:S(2)}) collective-permute-start(f32[30,32,128]{2,1,0:T(8,128)S(1)} %get-tuple-element.48), channel_id=1, source_target_pairs={{0,1},{1,2},{2,3},{3,4},{4,5},{5,6},{6,7},{8,9},{9,10},{10,11},{11... | collective-permute-start | bytes 1474568 | tf_op jit(solution)/shard_map/ppermute | solution.py:460
  108.3 25.0 %collective-permute-start.7 = (f32[30,32,128]{2,1,0:T(8,128)S(1)}, f32[30,32,128]{2,1,0:T(8,128)S(1)}, u32[]{:S(2)}, u32[]{:S(2)}) collective-permute-start(f32[30,32,128]{2,1,0:T(8,128)S(1)} %get-tuple-element.49), channel_id=1, source_target_pairs={{1,0},{2,1},{3,2},{4,3},{5,4},{6,5},{7,6},{9,8},{10,9},{11,10},{12... | collective-permute-start | bytes 1474568 | tf_op jit(solution)/shard_map/ppermute | solution.py:460
  112.0 10.1 %collective-permute-start.8 = (f32[30,32,128]{2,1,0:T(8,128)S(1)}, f32[30,32,128]{2,1,0:T(8,128)S(1)}, u32[]{:S(2)}, u32[]{:S(2)}) collective-permute-start(f32[30,32,128]{2,1,0:T(8,128)S(1)} %get-tuple-element.52), channel_id=1, source_target_pairs={{0,1},{1,2},{2,3},{3,4},{4,5},{5,6},{6,7},{8,9},{9,10},{10,11},{11... | collective-permute-start | bytes 1474568 | tf_op jit(solution)/shard_map/ppermute | solution.py:460
  113.9 10.0 %collective-permute-start.9 = (f32[30,32,128]{2,1,0:T(8,128)S(1)}, f32[30,32,128]{2,1,0:T(8,128)S(1)}, u32[]{:S(2)}, u32[]{:S(2)}) collective-permute-start(f32[30,32,128]{2,1,0:T(8,128)S(1)} %get-tuple-element.53), channel_id=1, source_target_pairs={{1,0},{2,1},{3,2},{4,3},{5,4},{6,5},{7,6},{9,8},{10,9},{11,10},{12... | collective-permute-start | bytes 1474568 | tf_op jit(solution)/shard_map/ppermute | solution.py:460
  124.0 18.0 %collective-permute-start.10 = (f32[64,16,128]{2,1,0:T(8,128)S(1)}, f32[64,16,128]{2,1,0:T(8,128)S(1)}, u32[]{:S(2)}, u32[]{:S(2)}) collective-permute-start(f32[64,16,128]{2,1,0:T(8,128)S(1)} %get-tuple-element.54), channel_id=1, source_target_pairs={{0,8},{8,16},{16,24},{24,32},{32,40},{40,48},{48,56},{56,64},{64,7... | collective-permute-start | bytes 1572872 | tf_op jit(solution)/shard_map/ppermute | solution.py:460
  125.9 17.8 %collective-permute-start.11 = (f32[64,16,128]{2,1,0:T(8,128)S(1)}, f32[64,16,128]{2,1,0:T(8,128)S(1)}, u32[]{:S(2)}, u32[]{:S(2)}) collective-permute-start(f32[64,16,128]{2,1,0:T(8,128)S(1)} %get-tuple-element.55), channel_id=1, source_target_pairs={{8,0},{16,8},{24,16},{32,24},{40,32},{48,40},{56,48},{64,56},{72,6... | collective-permute-start | bytes 1572872 | tf_op jit(solution)/shard_map/ppermute | solution.py:460
  145.8 18.9 %collective-permute-start.12 = (f32[64,16,128]{2,1,0:T(8,128)S(1)}, f32[64,16,128]{2,1,0:T(8,128)S(1)}, u32[]{:S(2)}, u32[]{:S(2)}) collective-permute-start(f32[64,16,128]{2,1,0:T(8,128)S(1)} %get-tuple-element.58), channel_id=1, source_target_pairs={{0,8},{8,16},{16,24},{24,32},{32,40},{40,48},{48,56},{56,64},{64,7... | collective-permute-start | bytes 1572872 | tf_op jit(solution)/shard_map/ppermute | solution.py:460
  147.7 18.2 %collective-permute-start.13 = (f32[64,16,128]{2,1,0:T(8,128)S(1)}, f32[64,16,128]{2,1,0:T(8,128)S(1)}, u32[]{:S(2)}, u32[]{:S(2)}) collective-permute-start(f32[64,16,128]{2,1,0:T(8,128)S(1)} %get-tuple-element.59), channel_id=1, source_target_pairs={{8,0},{16,8},{24,16},{32,24},{40,32},{48,40},{56,48},{64,56},{72,6... | collective-permute-start | bytes 1572872 | tf_op jit(solution)/shard_map/ppermute | solution.py:460
  154.2 17.4 %collective-permute-start.14 = (f32[30,32,128]{2,1,0:T(8,128)S(1)}, f32[30,32,128]{2,1,0:T(8,128)S(1)}, u32[]{:S(2)}, u32[]{:S(2)}) collective-permute-start(f32[30,32,128]{2,1,0:T(8,128)S(1)} %get-tuple-element.60), channel_id=1, source_target_pairs={{0,1},{1,2},{2,3},{3,4},{4,5},{5,6},{6,7},{8,9},{9,10},{10,11},{11... | collective-permute-start | bytes 1474568 | tf_op jit(solution)/shard_map/ppermute | solution.py:460
  156.2 15.4 %collective-permute-start.16 = (f32[30,32,128]{2,1,0:T(8,128)S(1)}, f32[30,32,128]{2,1,0:T(8,128)S(1)}, u32[]{:S(2)}, u32[]{:S(2)}) collective-permute-start(f32[30,32,128]{2,1,0:T(8,128)S(1)} %get-tuple-element.61), channel_id=1, source_target_pairs={{1,0},{2,1},{3,2},{4,3},{5,4},{6,5},{7,6},{9,8},{10,9},{11,10},{12... | collective-permute-start | bytes 1474568 | tf_op jit(solution)/shard_map/ppermute | solution.py:460
  166.0 10.1 %collective-permute-start.15 = (f32[30,32,128]{2,1,0:T(8,128)S(1)}, f32[30,32,128]{2,1,0:T(8,128)S(1)}, u32[]{:S(2)}, u32[]{:S(2)}) collective-permute-start(f32[30,32,128]{2,1,0:T(8,128)S(1)} %pad_maximum_fusion.2), channel_id=1, source_target_pairs={{0,1},{1,2},{2,3},{3,4},{4,5},{5,6},{6,7},{8,9},{9,10},{10,11},{11... | collective-permute-start | bytes 1474568 | tf_op jit(solution)/shard_map/ppermute | solution.py:460
  168.0 10.0 %collective-permute-start.17 = (f32[30,32,128]{2,1,0:T(8,128)S(1)}, f32[30,32,128]{2,1,0:T(8,128)S(1)}, u32[]{:S(2)}, u32[]{:S(2)}) collective-permute-start(f32[30,32,128]{2,1,0:T(8,128)S(1)} %pad_maximum_fusion.3), channel_id=1, source_target_pairs={{1,0},{2,1},{3,2},{4,3},{5,4},{6,5},{7,6},{9,8},{10,9},{11,10},{12... | collective-permute-start | bytes 1474568 | tf_op jit(solution)/shard_map/ppermute | solution.py:460
  195.3 10.3 %collective-permute-start.20 = (f32[30,32,128]{2,1,0:T(8,128)S(1)}, f32[30,32,128]{2,1,0:T(8,128)S(1)}, u32[]{:S(2)}, u32[]{:S(2)}) collective-permute-start(f32[30,32,128]{2,1,0:T(8,128)S(1)} %get-tuple-element.67), channel_id=1, source_target_pairs={{0,1},{1,2},{2,3},{3,4},{4,5},{5,6},{6,7},{8,9},{9,10},{10,11},{11... | collective-permute-start | bytes 1474568 | tf_op jit(solution)/shard_map/ppermute | solution.py:460
  207.5 24.9 %collective-permute-start.22 = (f32[64,16,128]{2,1,0:T(8,128)S(1)}, f32[64,16,128]{2,1,0:T(8,128)S(1)}, u32[]{:S(2)}, u32[]{:S(2)}) collective-permute-start(f32[64,16,128]{2,1,0:T(8,128)S(1)} %get-tuple-element.69), channel_id=1, source_target_pairs={{0,8},{8,16},{16,24},{24,32},{32,40},{40,48},{48,56},{56,64},{64,7... | collective-permute-start | bytes 1572872 | tf_op jit(solution)/shard_map/ppermute | solution.py:460
  209.4 23.0 %collective-permute-start.23 = (f32[64,16,128]{2,1,0:T(8,128)S(1)}, f32[64,16,128]{2,1,0:T(8,128)S(1)}, u32[]{:S(2)}, u32[]{:S(2)}) collective-permute-start(f32[64,16,128]{2,1,0:T(8,128)S(1)} %get-tuple-element.70), channel_id=1, source_target_pairs={{8,0},{16,8},{24,16},{32,24},{40,32},{48,40},{56,48},{64,56},{72,6... | collective-permute-start | bytes 1572872 | tf_op jit(solution)/shard_map/ppermute | solution.py:460
  220.3 10.3 %collective-permute-start.18 = (f32[30,32,128]{2,1,0:T(8,128)S(1)}, f32[30,32,128]{2,1,0:T(8,128)S(1)}, u32[]{:S(2)}, u32[]{:S(2)}) collective-permute-start(f32[30,32,128]{2,1,0:T(8,128)S(1)} %get-tuple-element.63), channel_id=1, source_target_pairs={{0,1},{1,2},{2,3},{3,4},{4,5},{5,6},{6,7},{8,9},{9,10},{10,11},{11... | collective-permute-start | bytes 1474568 | tf_op jit(solution)/shard_map/ppermute | solution.py:460
  223.7 8.7 %collective-permute-start.19 = (f32[30,32,128]{2,1,0:T(8,128)S(1)}, f32[30,32,128]{2,1,0:T(8,128)S(1)}, u32[]{:S(2)}, u32[]{:S(2)}) collective-permute-start(f32[30,32,128]{2,1,0:T(8,128)S(1)} %get-tuple-element.64), channel_id=1, source_target_pairs={{1,0},{2,1},{3,2},{4,3},{5,4},{6,5},{7,6},{9,8},{10,9},{11,10},{12... | collective-permute-start | bytes 1474568 | tf_op jit(solution)/shard_map/ppermute | solution.py:460
  (26 other events, 317.6 us)

commit v3 on v2

v3 whole, which is shorter than its diff:
```python
import functools

import jax
import jax.numpy as jnp
from jax import lax
from jax.experimental import pallas as pl
from jax.experimental.pallas import tpu as pltpu
from jax.sharding import PartitionSpec as P

BLK_DEV = 4
BX = 8
OFF = 8
ITERS = 2
V = 6
NY = 128
DZ = 64
DX = 32
RZ = 30
PZ = 32
RX = 16
EZ = DZ + 2 * PZ
EX = DX + 2 * RX
ROWS = V * DX
MIB = 1 << 20

exact_mode = lax.Precision.HIGHEST


def split(value):
    high = value.astype(jnp.bfloat16)
    low = (value - high.astype(jnp.float32)).astype(jnp.bfloat16)
    return high, low


def mul(a, b):
    return jnp.dot(a, b, preferred_element_type=jnp.float32)


def pair_columns(value, rows):
    return value[:, : value.shape[1] // 2], value[:, value.shape[1] // 2 :]


def blur_x(xf, planes, store):
    both = jnp.concatenate(planes, axis=1)
    high, low = split(both)
    out = mul(xf, jnp.concatenate([high, low, high], axis=0))
    store(out[:, :NY], out[:, NY:])


def starts(par, first, last):
    even = jnp.where(par[1] == 0, last, first)
    return even, first + last - even


def forward_x(par, s_ref, xf_ref, est, colse, colso, cene, ceno, side, sido):
    zeros = jnp.zeros((2, ROWS, NY), jnp.float32)
    s_ref[0:2, :ROWS] = zeros
    s_ref[EZ - 2 : EZ, :ROWS] = zeros
    plain = par[0] == 0

    def put(base):
        def store(first, second):
            s_ref[base, :ROWS] = first
            s_ref[base + 1, :ROWS] = second

        return store

    def rim(centre, sides, start):
        @pl.loop(0, RZ // 6)
        def _(group):
            for u in range(3):
                at = 6 * group + 2 * u
                planes = []
                for z in (at, at + 1):
                    planes.append(
                        jnp.concatenate([sides[z, :RX], centre[z], sides[z, RX:]], axis=0)
                    )
                blur_x(xf_ref[...], planes, put(start + at))

    @pl.loop(0, DZ // 8)
    def _(group):
        for u in range(4):
            at = 8 * group + 2 * u
            planes = []
            for z in (at, at + 1):
                even, odd = colse[z], colso[z]
                left, right = jnp.where(plain, odd, even), jnp.where(plain, even, odd)
                planes.append(jnp.concatenate([left, est[z], right], axis=0))
            blur_x(xf_ref[...], planes, put(PZ + at))

    even, odd = starts(par, PZ - RZ, PZ + DZ)
    rim(cene, side, even)
    rim(ceno, sido, odd)


def halves(value):
    middle = value.shape[1] // 2
    return value[:, :middle], value[:, middle:]


def forward_tile(s_ref, zf_ref, yf_ref, view, row):
    field = jnp.swapaxes(s_ref[:, pl.ds(row, BX), :], 0, 1)
    parts = []
    for p in range(BX // 2):
        high, low = split(jnp.concatenate([field[2 * p], field[2 * p + 1]], axis=1))
        out = mul(zf_ref[view], jnp.concatenate([high, low], axis=0))
        parts += halves(out[:DZ] + out[DZ:])
    high, low = split(jnp.concatenate(parts, axis=0))
    first, second = halves(mul(jnp.concatenate([high, low], axis=1), yf_ref[view]))
    return first + second


def backward_tile(zb_ref, yb_ref, view, ratio):
    high, low = split(ratio)
    first, second = halves(mul(jnp.concatenate([high, low], axis=1), yb_ref[view]))
    out = first + second
    parts = []
    for p in range(BX // 2):
        at = 2 * p * DZ
        high, low = split(jnp.concatenate([out[at : at + DZ], out[at + DZ : at + 2 * DZ]], axis=1))
        parts += halves(mul(zb_ref[view], jnp.concatenate([high, low, high], axis=0)))
    return jnp.swapaxes(jnp.stack(parts, axis=0), 0, 1)


def backward_x(par, s_ref, xb_ref, midc, midl, midr, cene, ceno, side, sido):
    def spread_pair(base):
        both = jnp.concatenate([s_ref[base, :ROWS], s_ref[base + 1, :ROWS]], axis=1)
        high, low = split(both)
        out = mul(xb_ref[...], jnp.concatenate([high, low], axis=0))
        return halves(out[:EX] + out[EX:])

    def rim(centre, sides, start):
        @pl.loop(0, RZ // 6)
        def _(group):
            for u in range(3):
                at = 6 * group + 2 * u
                for i, plane in enumerate(spread_pair(start + at)):
                    sides[at + i] = jnp.concatenate([plane[:RX], plane[RX + DX :]], axis=0)
                    centre[at + i] = plane[RX : RX + DX]

    even, odd = starts(par, PZ - RZ, PZ + DZ)
    rim(cene, side, even)
    rim(ceno, sido, odd)

    @pl.loop(0, DZ // 8)
    def _(group):
        for u in range(4):
            at = 8 * group + 2 * u
            for i, plane in enumerate(spread_pair(PZ + at)):
                midl[at + i] = plane[:RX]
                midc[at + i] = plane[RX : RX + DX]
                midr[at + i] = plane[RX + DX :]


def compact(slots, meta, order):
    count = jnp.int32(0)
    for slot in range(slots):
        order[count] = slot
        count = count + meta[slot]
    order[count] = slots
    return count


def clear_absent(slots, meta, s_ref):
    @pl.loop(0, V * BLK_DEV)
    def _(cell):
        @pl.when(meta[3 * (slots + 1) + cell] == 0)
        def _():
            s_ref[:, pl.ds(pl.multiple_of(cell * BX, BX), BX), :] = jnp.zeros(
                (EZ, BX, NY), jnp.float32
            )


def fetches(slots, meta, order, moves):
    count = compact(slots, meta, order)

    @pl.loop(0, count)
    def _(k):
        slot = order[k]
        for make in moves:
            make(slot, meta[2 * (slots + 1) + slot]).start()

    def arrive(slot):
        @pl.when(slot < slots)
        def _():
            for make in moves:
                make(slot, meta[2 * (slots + 1) + slot]).wait()

    return count, arrive


def visit_pairs(slots, meta, order, count, arrive, s_ref, data, zb, yb, predict):
    @pl.loop(0, (count + 1) // 2)
    def _(k):
        slot = (order[2 * k], order[2 * k + 1])
        for i in slot:
            arrive(i)
        view = [meta[slots + 1 + i] for i in slot]
        cell = [meta[2 * (slots + 1) + i] for i in slot]
        row = [pl.multiple_of(i * BX, BX) for i in cell]
        blurred = [predict(slot[i], view[i], row[i]) for i in (0, 1)]
        ratio = [data[slot[i]] / blurred[i] for i in (0, 1)]
        out = [backward_tile(zb, yb, view[i], ratio[i]) for i in (0, 1)]
        for i in (0, 1):
            s_ref[:, pl.ds(row[i], BX), :] = out[i]


def data_move(got, data, sem):
    def make(slot, cell):
        return pltpu.make_async_copy(
            got.at[slot, pl.ds(0, BX * DZ)], data.at[slot], sem.at[slot]
        )

    return make


def sweep_body(slots, par, meta, est, colse, colso, cene, ceno, side, sido, got, xf, xb, zf, zb, yf,
               yb, omidc, omidl, omidr, ocene, oceno, oside, osido, s_ref, order, data, sem):
    count, arrive = fetches(slots, meta, order, [data_move(got, data, sem)])
    forward_x(par, s_ref, xf, est, colse, colso, cene, ceno, side, sido)
    clear_absent(slots, meta, s_ref)

    def predict(slot, view, row):
        return forward_tile(s_ref, zf, yf, view, row)

    visit_pairs(slots, meta, order, count, arrive, s_ref, data, zb, yb, predict)
    backward_x(par, s_ref, xb, omidc, omidl, omidr, ocene, oceno, oside, osido)


def blur_body(par, est, colse, colso, cene, ceno, side, sido, xf, zf, yf, out, s_ref, staged, sem):
    forward_x(par, s_ref, xf, est, colse, colso, cene, ceno, side, sido)

    def push(k):
        return pltpu.make_async_copy(
            staged.at[pl.ds(2 * k, 2)], out.at[pl.ds(2 * k, 2)], sem.at[k]
        )

    @pl.loop(0, V * BLK_DEV // 2)
    def _(k):
        view = k // (BLK_DEV // 2)
        cells = (2 * k, 2 * k + 1)
        results = [
            forward_tile(s_ref, zf, yf, view, pl.multiple_of(cell * BX, BX)) for cell in cells
        ]
        for cell, result in zip(cells, results):
            staged[cell] = result
        push(k).start()

    @pl.loop(0, V * BLK_DEV // 2)
    def _(k):
        push(k).wait()


def spread_body(slots, par, meta, blurred, got, xb, zb, yb,
                omidc, omidl, omidr, ocene, oceno, oside, osido, s_ref, order, data, sem, held,
                held_sem):
    def make(slot, cell):
        return pltpu.make_async_copy(blurred.at[cell], held.at[slot], held_sem.at[slot])

    count, arrive = fetches(slots, meta, order, [make, data_move(got, data, sem)])
    clear_absent(slots, meta, s_ref)

    def predict(slot, view, row):
        return held[slot]

    visit_pairs(slots, meta, order, count, arrive, s_ref, data, zb, yb, predict)
    backward_x(par, s_ref, xb, omidc, omidl, omidr, ocene, oceno, oside, osido)


def f32(*shape):
    return jax.ShapeDtypeStruct(shape, jnp.float32)


VM = pl.BlockSpec(memory_space=pltpu.VMEM)
SM = pl.BlockSpec(memory_space=pltpu.SMEM)
PIECES = (
    f32(DZ, DX, NY),
    f32(DZ, RX, NY),
    f32(DZ, RX, NY),
    f32(RZ, DX, NY),
    f32(RZ, DX, NY),
    f32(RZ, 2 * RX, NY),
    f32(RZ, 2 * RX, NY),
)


def params(mib):
    return pltpu.CompilerParams(vmem_limit_bytes=mib * MIB)


FIELD = pltpu.VMEM((EZ, ROWS + BX, NY), jnp.float32)


def visit_scratch(slots):
    return [
        FIELD,
        pltpu.SMEM((slots + 1,), jnp.int32),
        pltpu.VMEM((slots + 1, BX * DZ, NY), jnp.float32),
        pltpu.SemaphoreType.DMA((slots + 1,)),
    ]


HB = pl.BlockSpec(memory_space=pltpu.HBM)


def in_hbm(value):
    return pltpu.with_memory_space_constraint(value, pltpu.HBM)


def sweep(par, meta, pieces, got, tables):
    slots = got.shape[0]
    return pl.pallas_call(
        functools.partial(sweep_body, slots),
        out_shape=PIECES,
        in_specs=[SM] * 2 + [VM] * 7 + [HB] + [VM] * 6,
        out_specs=[VM] * 7,
        scratch_shapes=visit_scratch(slots),
        compiler_params=params(36),
        name="sweep",
    )(par, meta, *pieces, in_hbm(got), *tables)


def blur_all(par, pieces, tables):
    xf, xb, zf, zb, yf, yb = tables
    cells = V * BLK_DEV
    return pl.pallas_call(
        blur_body,
        out_shape=pltpu.HBM((cells, BX * DZ, NY), jnp.float32),
        in_specs=[SM] + [VM] * 10,
        out_specs=HB,
        scratch_shapes=[
            FIELD,
            pltpu.VMEM((cells, BX * DZ, NY), jnp.float32),
            pltpu.SemaphoreType.DMA((cells // 2,)),
        ],
        compiler_params=params(34),
        name="blur_all",
    )(par, *pieces, xf, zf, yf)


def spread_ratio(par, meta, blurred, got, tables):
    slots = got.shape[0]
    xf, xb, zf, zb, yf, yb = tables
    return pl.pallas_call(
        functools.partial(spread_body, slots),
        out_shape=PIECES,
        in_specs=[SM] * 2 + [HB] * 2 + [VM] * 3,
        out_specs=[VM] * 7,
        scratch_shapes=visit_scratch(slots)
        + [
            pltpu.VMEM((slots + 1, BX * DZ, NY), jnp.float32),
            pltpu.SemaphoreType.DMA((slots + 1,)),
        ],
        compiler_params=params(36),
        name="spread_ratio",
    )(par, meta, in_hbm(blurred), in_hbm(got), xb, zb, yb)


def place_body(owner, pair, shift, tiles, out, staged, labels, sem, label_sem):
    count = tiles.shape[0]
    slots = out.shape[0]
    lane = lax.broadcasted_iota(jnp.int32, (8, NY), 1)
    values = jnp.zeros((8, NY), jnp.int32)
    for k in range(count):
        values = jnp.where(lane == k, pair[k], values)
        values = jnp.where(lane == count + k, shift[k], values)
    labels[...] = values.astype(jnp.float32)
    copies = []
    for slot in range(slots):
        copies.append(
            pltpu.make_async_copy(
                labels, out.at[slot, pl.ds(BX * DZ, 8)], label_sem.at[slot]
            )
        )
        copies[-1].start()
    column = lax.broadcasted_iota(jnp.int32, (DZ, BX, NY), 2)
    for k in range(count):
        moved = pltpu.roll(tiles[k], (shift[k] + NY) % NY, 2)
        source = column - shift[k]
        moved = jnp.where((source >= 0) & (source < NY), moved, 0.0)
        staged[k] = jnp.swapaxes(moved, 0, 1).reshape(BX * DZ, NY)
        copies.append(
            pltpu.make_async_copy(staged.at[k], out.at[owner[k], pl.ds(0, BX * DZ)], sem.at[k])
        )
        copies[-1].start()
    for copy in copies:
        copy.wait()


def place(owner, pair, shift, tiles, slots):
    count = tiles.shape[0]
    return pl.pallas_call(
        place_body,
        out_shape=pltpu.HBM((slots, BX * DZ + 8, NY), jnp.float32),
        in_specs=[SM, SM, SM, VM],
        out_specs=HB,
        scratch_shapes=[
            pltpu.VMEM((count, BX * DZ, NY), jnp.float32),
            pltpu.VMEM((8, NY), jnp.float32),
            pltpu.SemaphoreType.DMA((count,)),
            pltpu.SemaphoreType.DMA((slots,)),
        ],
        compiler_params=params(32),
        name="place",
    )(owner, pair, shift, tiles)


def pick(par, even_if_plain, other):
    plain = par[0] == 0
    return jnp.where(plain, even_if_plain, other), jnp.where(plain, other, even_if_plain)


def first_body(par, est, colse, colso, cene, ceno):
    @pl.loop(0, DZ // 4)
    def _(group):
        for u in range(4):
            z = 4 * group + u
            colse[z], colso[z] = pick(par, est[z, RX:], est[z, :RX])

    even, odd = starts(par, 0, DZ - RZ)

    @pl.loop(0, RZ // 6)
    def _(group):
        for u in range(6):
            k = 6 * group + u
            cene[k] = est[even + k]
            ceno[k] = est[odd + k]


COLUMNS = f32(DZ, RX, NY)
PLANES = f32(RZ, DX, NY)


def first_rims(par, est):
    return pl.pallas_call(
        first_body,
        out_shape=(COLUMNS, COLUMNS, PLANES, PLANES),
        in_specs=[SM, VM],
        out_specs=[VM] * 4,
        compiler_params=params(16),
        name="first_rims",
    )(par, est)


def rims_body(par, midl, midr, side, sido, outl, outr):
    even, odd = starts(par, 0, DZ - RZ)

    @pl.loop(0, DZ // 4)
    def _(group):
        for u in range(4):
            z = 4 * group + u
            outl[z], outr[z] = pick(par, midr[z], midl[z])

    for start, sides in ((even, side), (odd, sido)):

        @pl.loop(0, RZ // 6)
        def _(group):
            for u in range(6):
                k = 6 * group + u
                add, other = pick(par, sides[k, RX:], sides[k, :RX])
                outl[start + k] += add
                outr[start + k] += other


def fold_rims(par, midl, midr, side, sido):
    return pl.pallas_call(
        rims_body,
        out_shape=(COLUMNS, COLUMNS),
        in_specs=[SM] + [VM] * 4,
        out_specs=[VM] * 2,
        compiler_params=params(16),
        name="fold_rims",
    )(par, midl, midr, side, sido)


def corner_body(par, colse, colso, side, sido):
    even, odd = starts(par, 0, DZ - RZ)
    for start, out in ((even, side), (odd, sido)):

        @pl.loop(0, RZ // 6)
        def _(group):
            for u in range(6):
                k = 6 * group + u
                right, left = pick(par, colse[start + k], colso[start + k])
                out[k] = jnp.concatenate([left, right], axis=0)


def corners(par, colse, colso):
    return pl.pallas_call(
        corner_body,
        out_shape=(PLANES, PLANES),
        in_specs=[SM] + [VM] * 2,
        out_specs=[VM] * 2,
        compiler_params=params(16),
        name="corners",
    )(par, colse, colso)


def weigh_body(planes, blocks, at, labels, kz, kx, yb, out, along_x, inside, views):
    held = labels.shape[1] // 2
    lane = lax.broadcasted_iota(jnp.int32, (1, NY), 1)
    boxes = kx[...]
    for i in range(1, BX):
        boxes = boxes + pltpu.roll(kx[...], i, 1)
    along_x[...] = jnp.zeros(along_x.shape, jnp.float32)
    inside[...] = jnp.zeros(inside.shape, jnp.float32)
    views[...] = jnp.full(views.shape, -1, jnp.int32)

    @pl.loop(0, labels.shape[0])
    def _(holder):
        for k in range(held):
            pair = labels[holder, k]
            shift = labels[holder, held + k]
            view = pair // blocks
            beside = pair % blocks - at[0] * BLK_DEV

            @pl.when((beside >= -2) & (beside < BLK_DEV + 2))
            def _():
                row = holder * held + k
                box = jnp.zeros((1, NY), jnp.float32)
                for v in range(V):
                    box = jnp.where(view == v, boxes[v : v + 1], box)
                step = (BX * beside - 15 + NY) % NY
                moved = pltpu.roll(jnp.broadcast_to(box, (8, NY)), step, 1)
                along_x[pl.ds(row, 1), :] = moved[:1]
                seen = (lane >= shift) & (lane < NY + shift)
                inside[pl.ds(row, 1), :] = jnp.where(seen, 1.0, 0.0)
                views[pl.ds(row, 1), :] = jnp.full((1, NY), view, jnp.int32)

    z = at[1] * DZ + lax.broadcasted_iota(jnp.int32, (DZ, NY), 0)
    tap = lax.broadcasted_iota(jnp.int32, (DZ, NY), 1)
    reached = (z - tap + RZ >= 0) & (z - tap + RZ < planes)
    seen = inside[...].astype(jnp.bfloat16)
    gains, slopes = [], []
    for v in range(V):
        first, second = halves(mul(seen, yb[v, :NY]))
        member = jnp.where(views[...] == v, along_x[...], 0.0)
        gains.append(
            lax.dot_general(
                member.T[:DX],
                first + second,
                (((1,), (0,)), ((), ())),
                precision=exact_mode,
                preferred_element_type=jnp.float32,
            )
        )
        row = jnp.where(reached, jnp.broadcast_to(kz[v : v + 1], (DZ, NY)), 0.0)
        slopes.append(jnp.broadcast_to(jnp.sum(row, axis=1, keepdims=True), (DZ, NY)))
    for i in range(DZ):
        total = slopes[0][i : i + 1] * gains[0]
        for v in range(1, V):
            total = total + slopes[v][i : i + 1] * gains[v]
        out[i] = jnp.maximum(total, 1.0)


def weigh(planes, blocks, at, labels, kz, kx, yb):
    count = labels.shape[0] * labels.shape[1] // 2
    return pl.pallas_call(
        functools.partial(weigh_body, planes, blocks),
        out_shape=f32(DZ, DX, NY),
        in_specs=[SM] * 2 + [VM] * 3,
        out_specs=VM,
        scratch_shapes=[
            pltpu.VMEM((count, NY), jnp.float32),
            pltpu.VMEM((count, NY), jnp.float32),
            pltpu.VMEM((count, NY), jnp.int32),
        ],
        compiler_params=params(16),
        name="weigh",
    )(at, labels, kz, kx, yb)


def update_body(par, est, weight, midc, cene, ceno, colse, colso, new, *outs):
    even, odd = starts(par, 0, DZ - RZ)

    @pl.loop(0, DZ // 4)
    def _(group):
        for u in range(4):
            z = 4 * group + u
            right, left = pick(par, colse[z], colso[z])
            new[z] = midc[z] + jnp.concatenate([left, right], axis=0)

    for start, centre in ((even, cene), (odd, ceno)):

        @pl.loop(0, RZ // 6)
        def _(group):
            for u in range(6):
                new[start + 6 * group + u] += centre[6 * group + u]

    @pl.loop(0, DZ // 4)
    def _(group):
        for u in range(4):
            z = 4 * group + u
            value = est[z] * new[z] / weight[z]
            new[z] = value
            if outs:
                outs[0][z], outs[1][z] = pick(par, value[RX:], value[:RX])

    if outs:

        @pl.loop(0, RZ // 6)
        def _(group):
            for u in range(6):
                k = 6 * group + u
                outs[2][k] = new[even + k]
                outs[3][k] = new[odd + k]


def update(par, est, weight, midc, cene, ceno, colse, colso, last):
    shapes = [f32(DZ, DX, NY)]
    if not last:
        shapes += [COLUMNS, COLUMNS, PLANES, PLANES]
    return pl.pallas_call(
        update_body,
        out_shape=tuple(shapes),
        in_specs=[SM] + [VM] * 7,
        out_specs=[VM] * len(shapes),
        compiler_params=params(16),
        name="update",
    )(par, est, weight, midc, cene, ceno, colse, colso)


def band(row, rows, first):
    table = jnp.broadcast_to(row, (rows, row.shape[1]))
    return pltpu.roll(table, first % row.shape[1], 1, stride=1, stride_axis=0)


def tables_body(kz, kx, ky, xf, xb, zf, zb, yf, yb):
    for view in range(V):
        full = band(kz[view : view + 1], DZ, PZ - RZ)
        high, low = split(full)
        zf[view] = jnp.concatenate(
            [jnp.concatenate([high, high], axis=1), jnp.concatenate([low, low], axis=1)], axis=0
        )
        high, low = split(full.T)
        zb[view] = jnp.concatenate([high, high, low], axis=1)
        full = band(ky[view : view + 1], NY, -15)[:, :NY]
        high, low = split(full)
        half = jnp.concatenate([high, low], axis=1)
        yb[view] = jnp.concatenate([half, half], axis=0)
        high, low = split(full.T)
        half = jnp.concatenate([high, low], axis=1)
        yf[view] = jnp.concatenate([half, half], axis=0)
    full = jnp.concatenate([band(kx[v : v + 1], DX, RX - 15) for v in range(V)], axis=0)
    high, low = split(full[:, :EX])
    xf[...] = jnp.concatenate([high, high, low], axis=1)
    high, low = split(full.T[:EX])
    both = jnp.concatenate([high, low], axis=0)
    xb[...] = jnp.concatenate([both, both], axis=1)


def padded(kernel, lanes):
    return jnp.pad(kernel, ((0, 8 - V), (0, lanes - kernel.shape[1])))


def make_tables(kernel_z, kernel_x, kernel_y):
    def bf16(*shape):
        return jax.ShapeDtypeStruct(shape, jnp.bfloat16)

    return pl.pallas_call(
        tables_body,
        out_shape=(
            bf16(ROWS, 3 * EX),
            bf16(2 * EX, 2 * ROWS),
            bf16(V, 2 * DZ, 2 * EZ),
            bf16(V, EZ, 3 * DZ),
            bf16(V, 2 * NY, 2 * NY),
            bf16(V, 2 * NY, 2 * NY),
        ),
        in_specs=[VM] * 3,
        out_specs=[VM] * 6,
        compiler_params=params(32),
        name="tables",
    )(kernel_z, kernel_x, kernel_y)


def swap(even, odd, axis):
    count = lax.axis_size(axis)
    out = []
    for value, first in ((even, 0), (odd, 1)):
        pairs = []
        for i in range(first, count - 1, 2):
            pairs += [(i, i + 1), (i + 1, i)]
        out.append(lax.ppermute(value, axis, pairs))
    return out


def local(estimate0, tiles, psf_z, psf_x, psf_y, tile_pair, tile_shift):
    owners = lax.axis_size("blocks")
    all_blocks = BLK_DEV * owners
    me = lax.axis_index("blocks")
    kernel_z = padded(psf_z / jnp.sum(psf_z, axis=1, keepdims=True), 128)
    kernel_x = padded(psf_x / jnp.sum(psf_x, axis=1, keepdims=True), 128)
    kernel_y = padded(psf_y / jnp.sum(psf_y, axis=1, keepdims=True), 256)

    held = tile_pair % all_blocks // BLK_DEV
    est = estimate0
    par = jnp.stack([me % 2, lax.axis_index("depth") % 2]).astype(jnp.int32)
    *columns, cene, ceno = first_rims(par, est)
    columns = swap(*columns, "blocks")
    sent = place(held, tile_pair, tile_shift, tiles, owners)
    sent, *columns = lax.optimization_barrier((sent, *columns))
    got = lax.all_to_all(sent, "blocks", split_axis=0, concat_axis=0, tiled=True)
    tables = make_tables(kernel_z, kernel_x, kernel_y)

    count = tiles.shape[0]
    labels = got[:, BX * DZ, : 2 * count].astype(jnp.int32)
    pairs, shifts = labels[:, :count], labels[:, count:]
    mine = pairs % all_blocks // BLK_DEV == me
    live = jnp.max(mine.astype(jnp.int32), axis=1)
    got_pair = jnp.sum(jnp.where(mine, pairs, 0), axis=1)
    view = got_pair // all_blocks
    cell = jnp.where(live > 0, view * BLK_DEV + got_pair % all_blocks - me * BLK_DEV, V * BLK_DEV)
    hit = cell[None, :] == jnp.arange(V * BLK_DEV)[:, None]
    present = jnp.max(hit.astype(jnp.int32), axis=1)
    end = lambda value: jnp.full((1,), value, jnp.int32)
    meta = jnp.concatenate([live, end(0), view, end(0), cell, end(V * BLK_DEV), present])
    meta = meta.astype(jnp.int32)
    at = jnp.stack([me, lax.axis_index("depth")]).astype(jnp.int32)
    planes = lax.axis_size("depth") * DZ
    weight = weigh(planes, all_blocks, at, labels, kernel_z, kernel_x, tables[5])

    for iteration in range(ITERS):
        centre = swap(cene, ceno, "depth")
        sides = swap(*corners(par, *columns), "depth")
        pieces = (est, *columns, *centre, *sides)
        if iteration == 0:
            spread = spread_ratio(par, meta, blur_all(par, pieces, tables), got, tables)
        else:
            spread = sweep(par, meta, pieces, got, tables)
        midc, midl, midr, cene, ceno, side, sido = spread
        side, sido = swap(side, sido, "depth")
        rims = fold_rims(par, midl, midr, side, sido)
        cene, ceno, *rims = lax.optimization_barrier((cene, ceno, *rims))
        columns = swap(*rims, "blocks")
        cene, ceno = swap(cene, ceno, "depth")
        last = iteration == ITERS - 1
        est, *rest = update(par, est, weight, midc, cene, ceno, *columns, last)
        if not last:
            *columns, cene, ceno = rest
            columns = swap(*columns, "blocks")
    return est


def solution(mesh):
    in_specs = (
        P("depth", "blocks", None),
        P("blocks", "depth", None, None),
        P(),
        P(),
        P(),
        P("blocks"),
        P("blocks"),
    )
    out_specs = P("depth", "blocks", None)
    return jax.shard_map(local, mesh=mesh, in_specs=in_specs, out_specs=out_specs, check_vma=False)
```

time: 239 us -> 216 us (0.904); the launches traced: 235 us -> 217 us
  starting transfers between devices: 84.9 us -> 39.3 us
  waiting for transfers between devices: 71.9 us -> 97.1 us
  Pallas kernels: 52.5 us -> 67.3 us
  local copies, waits for them, and re-layouts: 18.9 us -> 10.5 us
    ppermute x24, starting transfers between devices: 79.1 us -> 32.4 us  [swap(): out.append(lax.ppermute(value, axis, pairs))]
    ppermute x24, waiting for transfers between devices: 51 us -> 70.4 us  [swap(): out.append(lax.ppermute(value, axis, pairs))]
    pallas_call x4 -> x8, Pallas kernels: 17.1 us -> 28.4 us  [the longest x1 15.7 us: blur_all(): pl.pallas_call(blur_body, out_shape=pltpu.HBM((cells, BX * DZ, NY), jnp.f...]
    unnamed x50 -> x34, local copies, waits for them, and re-layouts: 16.2 us -> 9.81 us
    all_to_all x1, waiting for transfers between devices: 20.9 us -> 26.7 us  [local(): lax.all_to_all(sent, 'blocks', split_axis=0, concat_axis=0, tiled=True)]
    pallas_call x1, Pallas kernels: 17.3 us -> 20.3 us  [sweep(): pl.pallas_call(functools.partial(sweep_body, slots), out_shape=PIECES, in...]
    slice x5 -> x0, local copies, waits for them, and re-layouts: 2.44 us -> none  [the longest x1 1.28 us: local(): left, right = halo_columns(est[:, :RX], est[:, DX - RX:])]
  transfers between devices with their start and end apart: 25 -> 25, of which waited for: 17 -> 15; matrix products, arithmetic and copies ran while one was open for 3% -> 1% of each run, Pallas kernels for 8% -> 12%
where the time goes in v3:
time: 216 us; the launch traced here: 217 us
  waiting for transfers between devices  97.1 us (45%)
  Pallas kernels  67.3 us (31%)
  starting transfers between devices  39.3 us (18%)
  local copies, waits for them, and re-layouts  10.5 us (5%)
  other arithmetic  2.49 us (1%)
    ppermute x24, waiting for transfers between devices, swap(): out.append(lax.ppermute(value, axis, pairs))  70.4 us
    ppermute x24, starting transfers between devices, swap(): out.append(lax.ppermute(value, axis, pairs))  32.4 us
    all_to_all x1, waiting for transfers between devices, local(): lax.all_to_all(sent, 'blocks', split_axis=0, concat_axis=0, tiled=True)  26.7 us
    pallas_call x1, Pallas kernels, sweep(): pl.pallas_call(functools.partial(sweep_body, slots), out_shape=PIECES, in...  20.3 us
    pallas_call x1, Pallas kernels, blur_all(): pl.pallas_call(blur_body, out_shape=pltpu.HBM((cells, BX * DZ, NY), jnp.f...  15.7 us
    pallas_call x1, Pallas kernels, spread_ratio(): pl.pallas_call(functools.partial(spread_body, slots), out_shape=PIECES, i...  13.9 us
    unnamed x34, local copies, waits for them, and re-layouts  9.81 us
    all_to_all x1, starting transfers between devices, local(): lax.all_to_all(sent, 'blocks', split_axis=0, concat_axis=0, tiled=True)  6.89 us
  transfers between devices with their start and end apart: 25, of which 15 were waited for; matrix products, arithmetic and copies ran while one was open for 1% of the time, Pallas kernels for 12%

profile of v3, /device:TPU:34, one launch (start us, length us, event | category | flops | bytes accessed | tf_op | source)
XLA Modules:
  0.0 217.1 jit_solution(14672005463431446489)
XLA Ops:
  4.6 3.6 %collective-permute-start.1 = (f32[64,16,128]{2,1,0:T(8,128)S(1)}, f32[64,16,128]{2,1,0:T(8,128)S(1)}, u32[]{:S(2)}, u32[]{:S(2)}) collective-permute-start(f32[64,16,128]{2,1,0:T(8,128)S(1)} %get-tuple-element.54), channel_id=1, source_target_pairs={{8,16},{16,8},{24,32},{32,24},{40,48},{48,40},{56,64},{64,56},{72,... | collective-permute-start | bytes 1572872 | tf_op jit(solution)/shard_map/ppermute | solution.py:684
  11.8 2.3 %place.1 = f32[16,520,128]{2,1,0:T(8,128)} custom-call(s32[8]{0:T(128)S(1)} %and_select_fusion.2.owner, s32[8]{0:T(128)S(1)} %copy-done.12, s32[8]{0:T(128)S(1)} %copy-done.13, f32[8,64,8,128]{3,2,1,0:T(8,128)S(1)} %copy-done.4), custom_call_target="tpu_custom_call" | custom-call | tf_op jit(solution)/shard_map/place/pallas_call | solution.py:392
  14.2 2.6 %collective-permute-done.colse = f32[64,16,128]{2,1,0:T(8,128)S(1)} collective-permute-done((f32[64,16,128]{2,1,0:T(8,128)S(1)}, f32[64,16,128]{2,1,0:T(8,128)S(1)}, u32[]{:S(2)}, u32[]{:S(2)}) %collective-permute-start) | collective-permute-done | bytes 524320 | tf_op jit(solution)/shard_map/ppermute | solution.py:684
  16.7 5.3 %collective-permute-done.1.colso = f32[64,16,128]{2,1,0:T(8,128)S(1)} collective-permute-done((f32[64,16,128]{2,1,0:T(8,128)S(1)}, f32[64,16,128]{2,1,0:T(8,128)S(1)}, u32[]{:S(2)}, u32[]{:S(2)}) %collective-permute-start.1) | collective-permute-done | bytes 524320 | tf_op jit(solution)/shard_map/ppermute | solution.py:684
  22.0 6.9 %all-to-all-start = ((f32[16,520,128]{2,1,0:T(8,128)}), f32[16,520,128]{2,1,0:T(8,128)}, u32[]{:S(2)}, u32[]{:S(2)}) async-start(f32[16,520,128]{2,1,0:T(8,128)} %place.1), calls=%async_computation | async-start | bytes 8519680 | tf_op jit(solution)/shard_map/all_to_all | solution.py:703
  28.9 2.5 %collective-permute-start.3 = (f32[30,32,128]{2,1,0:T(8,128)}, f32[30,32,128]{2,1,0:T(8,128)}, u32[]{:S(2)}, u32[]{:S(2)}) collective-permute-start(f32[30,32,128]{2,1,0:T(8,128)} %get-tuple-element.60), channel_id=1, source_target_pairs={{1,2},{2,1},{3,4},{4,3},{5,6},{6,5},{9,10},{10,9},{11,12},{12,11},... | collective-permute-start | bytes 1474568 | tf_op jit(solution)/shard_map/ppermute | solution.py:684
  40.8 3.8 %collective-permute-done.5.sido = f32[30,32,128]{2,1,0:T(8,128)} collective-permute-done((f32[30,32,128]{2,1,0:T(8,128)}, f32[30,32,128]{2,1,0:T(8,128)}, u32[]{:S(2)}, u32[]{:S(2)}) %collective-permute-start.5) | collective-permute-done | bytes 491552 | tf_op jit(solution)/shard_map/ppermute | solution.py:684
  45.7 15.7 %blur_all.1.blurred = f32[24,512,128]{2,1,0:T(8,128)} custom-call(s32[2]{0:T(128)S(1)} %pad_add_fusion.par, f32[64,32,128]{2,1,0:T(8,128)S(1)} %copy-done.1, f32[64,16,128]{2,1,0:T(8,128)S(1)} %collective-permute-done.colse, f32[64,16,128]{2,1,0:T(8,128)S(1)} %copy-done.3, f32[30,32,128]{2,1,0:T(8,128)} %collective-permute-done.2.cene, ...), custom_call_target="tpu_custom_call" | custom-call | tf_op jit(solution)/shard_map/blur_all/pallas_call | solution.py:326
  62.0 26.7 %all-to-all-done.got = f32[16,520,128]{2,1,0:T(8,128)} async-done(((f32[16,520,128]{2,1,0:T(8,128)}), f32[16,520,128]{2,1,0:T(8,128)}, u32[]{:S(2)}, u32[]{:S(2)}) %all-to-all-start) | async-done | bytes 4259872 | tf_op jit(solution)/shard_map/all_to_all | solution.py:703
  91.7 13.9 %spread_ratio.1 = (f32[64,32,128]{2,1,0:T(8,128)S(1)}, f32[64,16,128]{2,1,0:T(8,128)S(1)}, f32[64,16,128]{2,1,0:T(8,128)S(1)}, f32[30,32,128]{2,1,0:T(8,128)S(1)...) custom-call(s32[2]{0:T(128)S(1)} %pad_add_fusion.par, ...), custom_call_target="tpu_custom_call" | custom-call | tf_op jit(solution)/shard_map/spread_ratio/pallas_call | solution.py:344
  105.7 2.5 %collective-permute-start.7 = (f32[30,32,128]{2,1,0:T(8,128)S(1)}, f32[30,32,128]{2,1,0:T(8,128)S(1)}, u32[]{:S(2)}, u32[]{:S(2)}) collective-permute-start(f32[30,32,128]{2,1,0:T(8,128)S(1)} %get-tuple-element.74), channel_id=1, source_target_pairs={{1,2},{2,1},{3,4},{4,3},{5,6},{6,5},{9,10},{10,9},{11,12},{12,11},... | collective-permute-start | bytes 1474568 | tf_op jit(solution)/shard_map/ppermute | solution.py:684
  108.3 7.6 %collective-permute-done.7.sido = f32[30,32,128]{2,1,0:T(8,128)S(1)} collective-permute-done((f32[30,32,128]{2,1,0:T(8,128)S(1)}, f32[30,32,128]{2,1,0:T(8,128)S(1)}, u32[]{:S(2)}, u32[]{:S(2)}) %collective-permute-start.7) | collective-permute-done | bytes 491552 | tf_op jit(solution)/shard_map/ppermute | solution.py:684
  119.4 2.4 %collective-permute-start.9 = (f32[30,32,128]{2,1,0:T(8,128)S(1)}, f32[30,32,128]{2,1,0:T(8,128)S(1)}, u32[]{:S(2)}, u32[]{:S(2)}) collective-permute-start(f32[30,32,128]{2,1,0:T(8,128)S(1)} %get-tuple-element.78), channel_id=1, source_target_pairs={{1,2},{2,1},{3,4},{4,3},{5,6},{6,5},{9,10},{10,9},{11,12},{12,11},... | collective-permute-start | bytes 1474568 | tf_op jit(solution)/shard_map/ppermute | solution.py:684
  121.8 4.7 %weigh.1.weight = f32[64,32,128]{2,1,0:T(8,128)S(1)} custom-call(s32[2]{0:T(128)S(1)} %pad_add_fusion.1.at, s32[16,16]{1,0:T(8,128)S(1)} %bitcast.6, f32[8,128]{1,0:T(8,128)S(1)} %pad.12.kz, f32[8,128]{1,0:T(8,128)S(1)} %pad.13.kx, bf16[6,256,256]{2,1,0:T(8,128)(2,1)S(1)} %get-tuple-element.56.yb), custom_call_target="tpu_custom_call" | custom-call | tf_op jit(solution)/shard_map/weigh/pallas_call | solution.py:558
  126.5 3.0 %collective-permute-done.9.ceno = f32[30,32,128]{2,1,0:T(8,128)S(1)} collective-permute-done((f32[30,32,128]{2,1,0:T(8,128)S(1)}, f32[30,32,128]{2,1,0:T(8,128)S(1)}, u32[]{:S(2)}, u32[]{:S(2)}) %collective-permute-start.9) | collective-permute-done | bytes 491552 | tf_op jit(solution)/shard_map/ppermute | solution.py:684
  131.2 4.0 %collective-permute-done.11.colso = f32[64,16,128]{2,1,0:T(8,128)S(1)} collective-permute-done((f32[64,16,128]{2,1,0:T(8,128)S(1)}, f32[64,16,128]{2,1,0:T(8,128)S(1)}, u32[]{:S(2)}, u32[]{:S(2)}) %collective-permute-start.11) | collective-permute-done | bytes 524320 | tf_op jit(solution)/shard_map/ppermute | solution.py:684
  136.6 3.2 %collective-permute-start.13 = (f32[64,16,128]{2,1,0:T(8,128)S(1)}, f32[64,16,128]{2,1,0:T(8,128)S(1)}, u32[]{:S(2)}, u32[]{:S(2)}) collective-permute-start(f32[64,16,128]{2,1,0:T(8,128)S(1)} %get-tuple-element.83), channel_id=1, source_target_pairs={{8,16},{16,8},{24,32},{32,24},{40,48},{48,40},{56,64},{64,56},{72,... | collective-permute-start | bytes 1572872 | tf_op jit(solution)/shard_map/ppermute | solution.py:684
  141.8 8.3 %collective-permute-done.12.colse = f32[64,16,128]{2,1,0:T(8,128)S(1)} collective-permute-done((f32[64,16,128]{2,1,0:T(8,128)S(1)}, f32[64,16,128]{2,1,0:T(8,128)S(1)}, u32[]{:S(2)}, u32[]{:S(2)}) %collective-permute-start.12) | collective-permute-done | bytes 524320 | tf_op jit(solution)/shard_map/ppermute | solution.py:684
  150.1 4.0 %collective-permute-done.13.colso = f32[64,16,128]{2,1,0:T(8,128)S(1)} collective-permute-done((f32[64,16,128]{2,1,0:T(8,128)S(1)}, f32[64,16,128]{2,1,0:T(8,128)S(1)}, u32[]{:S(2)}, u32[]{:S(2)}) %collective-permute-start.13) | collective-permute-done | bytes 524320 | tf_op jit(solution)/shard_map/ppermute | solution.py:684
  156.8 8.2 %collective-permute-done.17.sido = f32[30,32,128]{2,1,0:T(8,128)S(1)} collective-permute-done((f32[30,32,128]{2,1,0:T(8,128)S(1)}, f32[30,32,128]{2,1,0:T(8,128)S(1)}, u32[]{:S(2)}, u32[]{:S(2)}) %collective-permute-start.17) | collective-permute-done | bytes 491552 | tf_op jit(solution)/shard_map/ppermute | solution.py:684
  165.0 20.3 %sweep.1 = (f32[64,32,128]{2,1,0:T(8,128)S(1)}, f32[64,16,128]{2,1,0:T(8,128)S(1)}, f32[64,16,128]{2,1,0:T(8,128)S(1)}, f32[30,32,128]{2,1,0:T(8,128)S(1)}, f32[...) custom-call(s32[2]{0:T(128)S(1)} %pad_add_fusion.par, s32[75]{0:T(128)S(1)} %concatenate.3.meta, ...), custom_call_target="tpu_custom_call" | custom-call | tf_op jit(solution)/shard_map/sweep/pallas_call | solution.py:312
  187.8 8.2 %collective-permute-done.19.sido = f32[30,32,128]{2,1,0:T(8,128)S(1)} collective-permute-done((f32[30,32,128]{2,1,0:T(8,128)S(1)}, f32[30,32,128]{2,1,0:T(8,128)S(1)}, u32[]{:S(2)}, u32[]{:S(2)}) %collective-permute-start.19) | collective-permute-done | bytes 491552 | tf_op jit(solution)/shard_map/ppermute | solution.py:684
  201.2 8.0 %collective-permute-done.21.ceno = f32[30,32,128]{2,1,0:T(8,128)S(1)} collective-permute-done((f32[30,32,128]{2,1,0:T(8,128)S(1)}, f32[30,32,128]{2,1,0:T(8,128)S(1)}, u32[]{:S(2)}, u32[]{:S(2)}) %collective-permute-start.21) | collective-permute-done | bytes 491552 | tf_op jit(solution)/shard_map/ppermute | solution.py:684
  210.9 4.0 %collective-permute-done.23.colso = f32[64,16,128]{2,1,0:T(8,128)S(1)} collective-permute-done((f32[64,16,128]{2,1,0:T(8,128)S(1)}, f32[64,16,128]{2,1,0:T(8,128)S(1)}, u32[]{:S(2)}, u32[]{:S(2)}) %collective-permute-start.23) | collective-permute-done | bytes 524320 | tf_op jit(solution)/shard_map/ppermute | solution.py:684
  (90 shorter events, 45.1 us)
Async XLA Ops:
  3.1 13.7 %collective-permute-start = (f32[64,16,128]{2,1,0:T(8,128)S(1)}, f32[64,16,128]{2,1,0:T(8,128)S(1)}, u32[]{:S(2)}, u32[]{:S(2)}) collective-permute-start(f32[64,16,128]{2,1,0:T(8,128)S(1)} %get-tuple-element.53), channel_id=1, source_target_pairs={{0,8},{8,0},{16,24},{24,16},{32,40},{40,32},{48,56},{56,48},{64,72... | collective-permute-start | bytes 1572872 | tf_op jit(solution)/shard_map/ppermute | solution.py:684
  4.6 17.4 %collective-permute-start.1 = (f32[64,16,128]{2,1,0:T(8,128)S(1)}, f32[64,16,128]{2,1,0:T(8,128)S(1)}, u32[]{:S(2)}, u32[]{:S(2)}) collective-permute-start(f32[64,16,128]{2,1,0:T(8,128)S(1)} %get-tuple-element.54), channel_id=1, source_target_pairs={{8,16},{16,8},{24,32},{32,24},{40,48},{48,40},{56,64},{64,56},{72,... | collective-permute-start | bytes 1572872 | tf_op jit(solution)/shard_map/ppermute | solution.py:684
  22.0 66.7 %all-to-all-start = ((f32[16,520,128]{2,1,0:T(8,128)}), f32[16,520,128]{2,1,0:T(8,128)}, u32[]{:S(2)}, u32[]{:S(2)}) async-start(f32[16,520,128]{2,1,0:T(8,128)} %place.1), calls=%async_computation | async-start | bytes 8519680 | tf_op jit(solution)/shard_map/all_to_all | solution.py:703
  28.9 11.9 %collective-permute-start.2 = (f32[30,32,128]{2,1,0:T(8,128)}, f32[30,32,128]{2,1,0:T(8,128)}, u32[]{:S(2)}, u32[]{:S(2)}) collective-permute-start(f32[30,32,128]{2,1,0:T(8,128)} %get-tuple-element.59), channel_id=1, source_target_pairs={{0,1},{1,0},{2,3},{3,2},{4,5},{5,4},{6,7},{7,6},{8,9},{9,8},{10,11... | collective-permute-start | bytes 1474568 | tf_op jit(solution)/shard_map/ppermute | solution.py:684
  28.9 11.9 %collective-permute-start.3 = (f32[30,32,128]{2,1,0:T(8,128)}, f32[30,32,128]{2,1,0:T(8,128)}, u32[]{:S(2)}, u32[]{:S(2)}) collective-permute-start(f32[30,32,128]{2,1,0:T(8,128)} %get-tuple-element.60), channel_id=1, source_target_pairs={{1,2},{2,1},{3,4},{4,3},{5,6},{6,5},{9,10},{10,9},{11,12},{12,11},... | collective-permute-start | bytes 1474568 | tf_op jit(solution)/shard_map/ppermute | solution.py:684
  33.2 7.6 %collective-permute-start.4 = (f32[30,32,128]{2,1,0:T(8,128)}, f32[30,32,128]{2,1,0:T(8,128)}, u32[]{:S(2)}, u32[]{:S(2)}) collective-permute-start(f32[30,32,128]{2,1,0:T(8,128)} %get-tuple-element.61), channel_id=1, source_target_pairs={{0,1},{1,0},{2,3},{3,2},{4,5},{5,4},{6,7},{7,6},{8,9},{9,8},{10,11... | collective-permute-start | bytes 1474568 | tf_op jit(solution)/shard_map/ppermute | solution.py:684
  34.2 10.5 %collective-permute-start.5 = (f32[30,32,128]{2,1,0:T(8,128)}, f32[30,32,128]{2,1,0:T(8,128)}, u32[]{:S(2)}, u32[]{:S(2)}) collective-permute-start(f32[30,32,128]{2,1,0:T(8,128)} %get-tuple-element.62), channel_id=1, source_target_pairs={{1,2},{2,1},{3,4},{4,3},{5,6},{6,5},{9,10},{10,9},{11,12},{12,11},... | collective-permute-start | bytes 1474568 | tf_op jit(solution)/shard_map/ppermute | solution.py:684
  105.6 2.6 %collective-permute-start.6 = (f32[30,32,128]{2,1,0:T(8,128)S(1)}, f32[30,32,128]{2,1,0:T(8,128)S(1)}, u32[]{:S(2)}, u32[]{:S(2)}) collective-permute-start(f32[30,32,128]{2,1,0:T(8,128)S(1)} %get-tuple-element.73), channel_id=1, source_target_pairs={{0,1},{1,0},{2,3},{3,2},{4,5},{5,4},{6,7},{7,6},{8,9},{9,8},{10,11... | collective-permute-start | bytes 1474568 | tf_op jit(solution)/shard_map/ppermute | solution.py:684
  105.7 10.1 %collective-permute-start.7 = (f32[30,32,128]{2,1,0:T(8,128)S(1)}, f32[30,32,128]{2,1,0:T(8,128)S(1)}, u32[]{:S(2)}, u32[]{:S(2)}) collective-permute-start(f32[30,32,128]{2,1,0:T(8,128)S(1)} %get-tuple-element.74), channel_id=1, source_target_pairs={{1,2},{2,1},{3,4},{4,3},{5,6},{6,5},{9,10},{10,9},{11,12},{12,11},... | collective-permute-start | bytes 1474568 | tf_op jit(solution)/shard_map/ppermute | solution.py:684
  116.8 14.4 %collective-permute-start.10 = (f32[64,16,128]{2,1,0:T(8,128)S(1)}, f32[64,16,128]{2,1,0:T(8,128)S(1)}, u32[]{:S(2)}, u32[]{:S(2)}) collective-permute-start(f32[64,16,128]{2,1,0:T(8,128)S(1)} %get-tuple-element.79), channel_id=1, source_target_pairs={{0,8},{8,0},{16,24},{24,16},{32,40},{40,32},{48,56},{56,48},{64,72... | collective-permute-start | bytes 1572872 | tf_op jit(solution)/shard_map/ppermute | solution.py:684
  116.9 18.3 %collective-permute-start.11 = (f32[64,16,128]{2,1,0:T(8,128)S(1)}, f32[64,16,128]{2,1,0:T(8,128)S(1)}, u32[]{:S(2)}, u32[]{:S(2)}) collective-permute-start(f32[64,16,128]{2,1,0:T(8,128)S(1)} %get-tuple-element.80), channel_id=1, source_target_pairs={{8,16},{16,8},{24,32},{32,24},{40,48},{48,40},{56,64},{64,56},{72,... | collective-permute-start | bytes 1572872 | tf_op jit(solution)/shard_map/ppermute | solution.py:684
  118.9 7.7 %collective-permute-start.8 = (f32[30,32,128]{2,1,0:T(8,128)S(1)}, f32[30,32,128]{2,1,0:T(8,128)S(1)}, u32[]{:S(2)}, u32[]{:S(2)}) collective-permute-start(f32[30,32,128]{2,1,0:T(8,128)S(1)} %get-tuple-element.77), channel_id=1, source_target_pairs={{0,1},{1,0},{2,3},{3,2},{4,5},{5,4},{6,7},{7,6},{8,9},{9,8},{10,11... | collective-permute-start | bytes 1474568 | tf_op jit(solution)/shard_map/ppermute | solution.py:684
  119.4 10.1 %collective-permute-start.9 = (f32[30,32,128]{2,1,0:T(8,128)S(1)}, f32[30,32,128]{2,1,0:T(8,128)S(1)}, u32[]{:S(2)}, u32[]{:S(2)}) collective-permute-start(f32[30,32,128]{2,1,0:T(8,128)S(1)} %get-tuple-element.78), channel_id=1, source_target_pairs={{1,2},{2,1},{3,4},{4,3},{5,6},{6,5},{9,10},{10,9},{11,12},{12,11},... | collective-permute-start | bytes 1474568 | tf_op jit(solution)/shard_map/ppermute | solution.py:684
  136.5 13.6 %collective-permute-start.12 = (f32[64,16,128]{2,1,0:T(8,128)S(1)}, f32[64,16,128]{2,1,0:T(8,128)S(1)}, u32[]{:S(2)}, u32[]{:S(2)}) collective-permute-start(f32[64,16,128]{2,1,0:T(8,128)S(1)} %get-tuple-element.82), channel_id=1, source_target_pairs={{0,8},{8,0},{16,24},{24,16},{32,40},{40,32},{48,56},{56,48},{64,72... | collective-permute-start | bytes 1572872 | tf_op jit(solution)/shard_map/ppermute | solution.py:684
  136.6 17.5 %collective-permute-start.13 = (f32[64,16,128]{2,1,0:T(8,128)S(1)}, f32[64,16,128]{2,1,0:T(8,128)S(1)}, u32[]{:S(2)}, u32[]{:S(2)}) collective-permute-start(f32[64,16,128]{2,1,0:T(8,128)S(1)} %get-tuple-element.83), channel_id=1, source_target_pairs={{8,16},{16,8},{24,32},{32,24},{40,48},{48,40},{56,64},{64,56},{72,... | collective-permute-start | bytes 1572872 | tf_op jit(solution)/shard_map/ppermute | solution.py:684
  139.7 17.1 %collective-permute-start.14 = (f32[30,32,128]{2,1,0:T(8,128)S(1)}, f32[30,32,128]{2,1,0:T(8,128)S(1)}, u32[]{:S(2)}, u32[]{:S(2)}) collective-permute-start(f32[30,32,128]{2,1,0:T(8,128)S(1)} %get-tuple-element.84), channel_id=1, source_target_pairs={{0,1},{1,0},{2,3},{3,2},{4,5},{5,4},{6,7},{7,6},{8,9},{9,8},{10,11... | collective-permute-start | bytes 1474568 | tf_op jit(solution)/shard_map/ppermute | solution.py:684
  139.8 17.0 %collective-permute-start.15 = (f32[30,32,128]{2,1,0:T(8,128)S(1)}, f32[30,32,128]{2,1,0:T(8,128)S(1)}, u32[]{:S(2)}, u32[]{:S(2)}) collective-permute-start(f32[30,32,128]{2,1,0:T(8,128)S(1)} %get-tuple-element.85), channel_id=1, source_target_pairs={{1,2},{2,1},{3,4},{4,3},{5,6},{6,5},{9,10},{10,9},{11,12},{12,11},... | collective-permute-start | bytes 1474568 | tf_op jit(solution)/shard_map/ppermute | solution.py:684
  154.9 10.1 %collective-permute-start.17 = (f32[30,32,128]{2,1,0:T(8,128)S(1)}, f32[30,32,128]{2,1,0:T(8,128)S(1)}, u32[]{:S(2)}, u32[]{:S(2)}) collective-permute-start(f32[30,32,128]{2,1,0:T(8,128)S(1)} %get-tuple-element.87), channel_id=1, source_target_pairs={{1,2},{2,1},{3,4},{4,3},{5,6},{6,5},{9,10},{10,9},{11,12},{12,11},... | collective-permute-start | bytes 1474568 | tf_op jit(solution)/shard_map/ppermute | solution.py:684
  185.3 2.5 %collective-permute-start.18 = (f32[30,32,128]{2,1,0:T(8,128)S(1)}, f32[30,32,128]{2,1,0:T(8,128)S(1)}, u32[]{:S(2)}, u32[]{:S(2)}) collective-permute-start(f32[30,32,128]{2,1,0:T(8,128)S(1)} %get-tuple-element.93), channel_id=1, source_target_pairs={{0,1},{1,0},{2,3},{3,2},{4,5},{5,4},{6,7},{7,6},{8,9},{9,8},{10,11... | collective-permute-start | bytes 1474568 | tf_op jit(solution)/shard_map/ppermute | solution.py:684
  185.9 10.1 %collective-permute-start.19 = (f32[30,32,128]{2,1,0:T(8,128)S(1)}, f32[30,32,128]{2,1,0:T(8,128)S(1)}, u32[]{:S(2)}, u32[]{:S(2)}) collective-permute-start(f32[30,32,128]{2,1,0:T(8,128)S(1)} %get-tuple-element.94), channel_id=1, source_target_pairs={{1,2},{2,1},{3,4},{4,3},{5,6},{6,5},{9,10},{10,9},{11,12},{12,11},... | collective-permute-start | bytes 1474568 | tf_op jit(solution)/shard_map/ppermute | solution.py:684
  196.9 14.0 %collective-permute-start.22 = (f32[64,16,128]{2,1,0:T(8,128)S(1)}, f32[64,16,128]{2,1,0:T(8,128)S(1)}, u32[]{:S(2)}, u32[]{:S(2)}) collective-permute-start(f32[64,16,128]{2,1,0:T(8,128)S(1)} %get-tuple-element.99), channel_id=1, source_target_pairs={{0,8},{8,0},{16,24},{24,16},{32,40},{40,32},{48,56},{56,48},{64,72... | collective-permute-start | bytes 1572872 | tf_op jit(solution)/shard_map/ppermute | solution.py:684
  197.0 17.9 %collective-permute-start.23 = (f32[64,16,128]{2,1,0:T(8,128)S(1)}, f32[64,16,128]{2,1,0:T(8,128)S(1)}, u32[]{:S(2)}, u32[]{:S(2)}) collective-permute-start(f32[64,16,128]{2,1,0:T(8,128)S(1)} %get-tuple-element.100), channel_id=1, source_target_pairs={{8,16},{16,8},{24,32},{32,24},{40,48},{48,40},{56,64},{64,56},{72,... | collective-permute-start | bytes 1572872 | tf_op jit(solution)/shard_map/ppermute | solution.py:684
  198.9 2.3 %collective-permute-start.20 = (f32[30,32,128]{2,1,0:T(8,128)S(1)}, f32[30,32,128]{2,1,0:T(8,128)S(1)}, u32[]{:S(2)}, u32[]{:S(2)}) collective-permute-start(f32[30,32,128]{2,1,0:T(8,128)S(1)} %get-tuple-element.97), channel_id=1, source_target_pairs={{0,1},{1,0},{2,3},{3,2},{4,5},{5,4},{6,7},{7,6},{8,9},{9,8},{10,11... | collective-permute-start | bytes 1474568 | tf_op jit(solution)/shard_map/ppermute | solution.py:684
  199.1 10.1 %collective-permute-start.21 = (f32[30,32,128]{2,1,0:T(8,128)S(1)}, f32[30,32,128]{2,1,0:T(8,128)S(1)}, u32[]{:S(2)}, u32[]{:S(2)}) collective-permute-start(f32[30,32,128]{2,1,0:T(8,128)S(1)} %get-tuple-element.98), channel_id=1, source_target_pairs={{1,2},{2,1},{3,4},{4,3},{5,6},{6,5},{9,10},{10,9},{11,12},{12,11},... | collective-permute-start | bytes 1474568 | tf_op jit(solution)/shard_map/ppermute | solution.py:684
  (18 other events, 162.1 us)

commit v4 on v3

--- a/solution.py
+++ b/solution.py
@@ -53,23 +53,23 @@
 
 
 def forward_x(par, s_ref, xf_ref, est, colse, colso, cene, ceno, side, sido):
-    zeros = jnp.zeros((2, ROWS, NY), jnp.float32)
-    s_ref[0:2, :ROWS] = zeros
-    s_ref[EZ - 2 : EZ, :ROWS] = zeros
+    zeros = jnp.zeros((2,) + s_ref.shape[1:], jnp.float32)
+    s_ref[0:2] = zeros
+    s_ref[EZ - 2 : EZ] = zeros
     plain = par[0] == 0
 
     def put(base):
         def store(first, second):
-            s_ref[base, :ROWS] = first
-            s_ref[base + 1, :ROWS] = second
+            s_ref[base] = first
+            s_ref[base + 1] = second
 
         return store
 
     def rim(centre, sides, start):
-        @pl.loop(0, RZ // 6)
+        @pl.loop(0, RZ // 30)
         def _(group):
-            for u in range(3):
-                at = 6 * group + 2 * u
+            for u in range(15):
+                at = 30 * group + 2 * u
                 planes = []
                 for z in (at, at + 1):
                     planes.append(
@@ -77,10 +77,10 @@
                     )
                 blur_x(xf_ref[...], planes, put(start + at))
 
-    @pl.loop(0, DZ // 8)
+    @pl.loop(0, DZ // 64)
     def _(group):
-        for u in range(4):
-            at = 8 * group + 2 * u
+        for u in range(32):
+            at = 64 * group + 2 * u
             planes = []
             for z in (at, at + 1):
                 even, odd = colse[z], colso[z]
@@ -124,16 +124,16 @@
 
 def backward_x(par, s_ref, xb_ref, midc, midl, midr, cene, ceno, side, sido):
     def spread_pair(base):
-        both = jnp.concatenate([s_ref[base, :ROWS], s_ref[base + 1, :ROWS]], axis=1)
+        both = jnp.concatenate([s_ref[base], s_ref[base + 1]], axis=1)
         high, low = split(both)
         out = mul(xb_ref[...], jnp.concatenate([high, low], axis=0))
         return halves(out[:EX] + out[EX:])
 
     def rim(centre, sides, start):
-        @pl.loop(0, RZ // 6)
+        @pl.loop(0, RZ // 30)
         def _(group):
-            for u in range(3):
-                at = 6 * group + 2 * u
+            for u in range(15):
+                at = 30 * group + 2 * u
                 for i, plane in enumerate(spread_pair(start + at)):
                     sides[at + i] = jnp.concatenate([plane[:RX], plane[RX + DX :]], axis=0)
                     centre[at + i] = plane[RX : RX + DX]
@@ -142,10 +142,10 @@
     rim(cene, side, even)
     rim(ceno, sido, odd)
 
-    @pl.loop(0, DZ // 8)
+    @pl.loop(0, DZ // 64)
     def _(group):
-        for u in range(4):
-            at = 8 * group + 2 * u
+        for u in range(32):
+            at = 64 * group + 2 * u
             for i, plane in enumerate(spread_pair(PZ + at)):
                 midl[at + i] = plane[:RX]
                 midc[at + i] = plane[RX : RX + DX]
@@ -161,14 +161,25 @@
     return count
 
 
-def clear_absent(slots, meta, s_ref):
-    @pl.loop(0, V * BLK_DEV)
-    def _(cell):
-        @pl.when(meta[3 * (slots + 1) + cell] == 0)
-        def _():
-            s_ref[:, pl.ds(pl.multiple_of(cell * BX, BX), BX), :] = jnp.zeros(
-                (EZ, BX, NY), jnp.float32
-            )
+def gather_x(slots, meta, order, count, fx, picked, xf, xb):
+    for n in range(slots):
+        slot = jnp.where(n < count, order[n], slots)
+        cell = jnp.where(n < count, meta[2 * (slots + 1) + slot], 0)
+        scale = jnp.where(n < count, 1.0, 0.0)
+        picked[n * BX : (n + 1) * BX] = fx[cell] * scale
+    table = picked[...]
+    if xf is not None:
+        high, low = split(table[:, :EX])
+        xf[...] = jnp.concatenate([high, high, low], axis=1)
+    high, low = split(table.T[:EX])
+    both = jnp.concatenate([high, low], axis=0)
+    xb[...] = jnp.concatenate([both, both], axis=1)
+
+
+def clear_rest(slots, count, s_ref):
+    @pl.loop(count, slots)
+    def _(n):
+        s_ref[:, pl.ds(pl.multiple_of(n * BX, BX), BX), :] = jnp.zeros((EZ, BX, NY), jnp.float32)
 
 
 def fetches(slots, meta, order, moves):
@@ -189,19 +200,21 @@
     return count, arrive
 
 
-def visit_pairs(slots, meta, order, count, arrive, s_ref, data, zb, yb, predict):
-    @pl.loop(0, (count + 1) // 2)
+def visit_tiles(step, slots, meta, order, count, arrive, s_ref, data, zb, yb, predict):
+    @pl.loop(0, (count + step - 1) // step)
     def _(k):
-        slot = (order[2 * k], order[2 * k + 1])
+        slot = [
+            jnp.where(step * k + i < count, order[step * k + i], slots) for i in range(step)
+        ]
         for i in slot:
             arrive(i)
         view = [meta[slots + 1 + i] for i in slot]
-        cell = [meta[2 * (slots + 1) + i] for i in slot]
-        row = [pl.multiple_of(i * BX, BX) for i in cell]
-        blurred = [predict(slot[i], view[i], row[i]) for i in (0, 1)]
-        ratio = [data[slot[i]] / blurred[i] for i in (0, 1)]
-        out = [backward_tile(zb, yb, view[i], ratio[i]) for i in (0, 1)]
-        for i in (0, 1):
+        row = [pl.multiple_of((step * k + i) * BX, BX) for i in range(step)]
+        blurred = [predict(slot[i], view[i], row[i]) for i in range(step)]
+        out = [
+            backward_tile(zb, yb, view[i], data[slot[i]] / blurred[i]) for i in range(step)
+        ]
+        for i in range(step):
             s_ref[:, pl.ds(row[i], BX), :] = out[i]
 
 
@@ -214,16 +227,18 @@
     return make
 
 
-def sweep_body(slots, par, meta, est, colse, colso, cene, ceno, side, sido, got, xf, xb, zf, zb, yf,
-               yb, omidc, omidl, omidr, ocene, oceno, oside, osido, s_ref, order, data, sem):
+def sweep_body(slots, par, meta, est, colse, colso, cene, ceno, side, sido, got, fx, zf, zb, yf,
+               yb, omidc, omidl, omidr, ocene, oceno, oside, osido, s_ref, order, data, sem, picked,
+               xb, xf):
     count, arrive = fetches(slots, meta, order, [data_move(got, data, sem)])
+    gather_x(slots, meta, order, count, fx, picked, xf, xb)
     forward_x(par, s_ref, xf, est, colse, colso, cene, ceno, side, sido)
-    clear_absent(slots, meta, s_ref)
 
     def predict(slot, view, row):
         return forward_tile(s_ref, zf, yf, view, row)
 
-    visit_pairs(slots, meta, order, count, arrive, s_ref, data, zb, yb, predict)
+    visit_tiles(2, slots, meta, order, count, arrive, s_ref, data, zb, yb, predict)
+    clear_rest(slots, count, s_ref)
     backward_x(par, s_ref, xb, omidc, omidl, omidr, ocene, oceno, oside, osido)
 
 
@@ -251,19 +266,20 @@
         push(k).wait()
 
 
-def spread_body(slots, par, meta, blurred, got, xb, zb, yb,
-                omidc, omidl, omidr, ocene, oceno, oside, osido, s_ref, order, data, sem, held,
-                held_sem):
+def spread_body(slots, par, meta, blurred, got, fx, zb, yb,
+                omidc, omidl, omidr, ocene, oceno, oside, osido, s_ref, order, data, sem, picked,
+                xb, held, held_sem):
     def make(slot, cell):
         return pltpu.make_async_copy(blurred.at[cell], held.at[slot], held_sem.at[slot])
 
     count, arrive = fetches(slots, meta, order, [make, data_move(got, data, sem)])
-    clear_absent(slots, meta, s_ref)
+    gather_x(slots, meta, order, count, fx, picked, None, xb)
 
     def predict(slot, view, row):
         return held[slot]
 
-    visit_pairs(slots, meta, order, count, arrive, s_ref, data, zb, yb, predict)
+    visit_tiles(4, slots, meta, order, count, arrive, s_ref, data, zb, yb, predict)
+    clear_rest(slots, count, s_ref)
     backward_x(par, s_ref, xb, omidc, omidl, omidr, ocene, oceno, oside, osido)
 
 
@@ -288,15 +304,15 @@
     return pltpu.CompilerParams(vmem_limit_bytes=mib * MIB)
 
 
-FIELD = pltpu.VMEM((EZ, ROWS + BX, NY), jnp.float32)
-
-
 def visit_scratch(slots):
+    rows = slots * BX
     return [
-        FIELD,
+        pltpu.VMEM((EZ, rows, NY), jnp.float32),
         pltpu.SMEM((slots + 1,), jnp.int32),
         pltpu.VMEM((slots + 1, BX * DZ, NY), jnp.float32),
         pltpu.SemaphoreType.DMA((slots + 1,)),
+        pltpu.VMEM((rows, NY), jnp.float32),
+        pltpu.VMEM((2 * EX, 2 * rows), jnp.bfloat16),
     ]
 
 
@@ -312,16 +328,16 @@
     return pl.pallas_call(
         functools.partial(sweep_body, slots),
         out_shape=PIECES,
-        in_specs=[SM] * 2 + [VM] * 7 + [HB] + [VM] * 6,
+        in_specs=[SM] * 2 + [VM] * 7 + [HB] + [VM] * 5,
         out_specs=[VM] * 7,
-        scratch_shapes=visit_scratch(slots),
+        scratch_shapes=visit_scratch(slots) + [pltpu.VMEM((slots * BX, 3 * EX), jnp.bfloat16)],
         compiler_params=params(36),
         name="sweep",
-    )(par, meta, *pieces, in_hbm(got), *tables)
+    )(par, meta, *pieces, in_hbm(got), *tables[1:])
 
 
 def blur_all(par, pieces, tables):
-    xf, xb, zf, zb, yf, yb = tables
+    xf, fx, zf, zb, yf, yb = tables
     cells = V * BLK_DEV
     return pl.pallas_call(
         blur_body,
@@ -329,7 +345,7 @@
         in_specs=[SM] + [VM] * 10,
         out_specs=HB,
         scratch_shapes=[
-            FIELD,
+            pltpu.VMEM((EZ, ROWS, NY), jnp.float32),
             pltpu.VMEM((cells, BX * DZ, NY), jnp.float32),
             pltpu.SemaphoreType.DMA((cells // 2,)),
         ],
@@ -340,7 +356,7 @@
 
 def spread_ratio(par, meta, blurred, got, tables):
     slots = got.shape[0]
-    xf, xb, zf, zb, yf, yb = tables
+    xf, fx, zf, zb, yf, yb = tables
     return pl.pallas_call(
         functools.partial(spread_body, slots),
         out_shape=PIECES,
@@ -353,7 +369,7 @@
         ],
         compiler_params=params(36),
         name="spread_ratio",
-    )(par, meta, in_hbm(blurred), in_hbm(got), xb, zb, yb)
+    )(par, meta, in_hbm(blurred), in_hbm(got), fx, zb, yb)
 
 
 def place_body(owner, pair, shift, tiles, out, staged, labels, sem, label_sem):
@@ -625,7 +641,7 @@
     return pltpu.roll(table, first % row.shape[1], 1, stride=1, stride_axis=0)
 
 
-def tables_body(kz, kx, ky, xf, xb, zf, zb, yf, yb):
+def tables_body(kz, kx, ky, xf, fx, zf, zb, yf, yb):
     for view in range(V):
         full = band(kz[view : view + 1], DZ, PZ - RZ)
         high, low = split(full)
@@ -642,11 +658,9 @@
         half = jnp.concatenate([high, low], axis=1)
         yf[view] = jnp.concatenate([half, half], axis=0)
     full = jnp.concatenate([band(kx[v : v + 1], DX, RX - 15) for v in range(V)], axis=0)
+    fx[...] = full.reshape(V * BLK_DEV, BX, NY)
     high, low = split(full[:, :EX])
     xf[...] = jnp.concatenate([high, high, low], axis=1)
-    high, low = split(full.T[:EX])
-    both = jnp.concatenate([high, low], axis=0)
-    xb[...] = jnp.concatenate([both, both], axis=1)
 
 
 def padded(kernel, lanes):
@@ -661,7 +675,7 @@
         tables_body,
         out_shape=(
             bf16(ROWS, 3 * EX),
-            bf16(2 * EX, 2 * ROWS),
+            f32(V * BLK_DEV, BX, NY),
             bf16(V, 2 * DZ, 2 * EZ),
             bf16(V, EZ, 3 * DZ),
             bf16(V, 2 * NY, 2 * NY),
@@ -711,10 +725,8 @@
     got_pair = jnp.sum(jnp.where(mine, pairs, 0), axis=1)
     view = got_pair // all_blocks
     cell = jnp.where(live > 0, view * BLK_DEV + got_pair % all_blocks - me * BLK_DEV, V * BLK_DEV)
-    hit = cell[None, :] == jnp.arange(V * BLK_DEV)[:, None]
-    present = jnp.max(hit.astype(jnp.int32), axis=1)
     end = lambda value: jnp.full((1,), value, jnp.int32)
-    meta = jnp.concatenate([live, end(0), view, end(0), cell, end(V * BLK_DEV), present])
+    meta = jnp.concatenate([live, end(0), view, end(0), cell, end(V * BLK_DEV)])
     meta = meta.astype(jnp.int32)
     at = jnp.stack([me, lax.axis_index("depth")]).astype(jnp.int32)
     planes = lax.axis_size("depth") * DZ

time: 216 us -> 205 us (0.949); the launches traced: 217 us -> 203 us
  Pallas kernels: 67.3 us -> 44.1 us
  starting transfers between devices: 39.3 us -> 56.5 us
  waiting for transfers between devices: 97.1 us -> 89.5 us
    ppermute x24, starting transfers between devices: 32.4 us -> 49.6 us  [swap(): out.append(lax.ppermute(value, axis, pairs))]
    pallas_call x1, Pallas kernels: 20.3 us -> 6.86 us  [sweep(): pl.pallas_call(functools.partial(sweep_body, slots), out_shape=PIECES, in...]
    ppermute x24, waiting for transfers between devices: 70.4 us -> 60.9 us  [swap(): out.append(lax.ppermute(value, axis, pairs))]
    pallas_call x1, Pallas kernels: 13.9 us -> 5.75 us  [spread_ratio(): pl.pallas_call(functools.partial(spread_body, slots), out_shape=PIECES, i...]
    unnamed x34 -> x30, local copies, waits for them, and re-layouts: 9.81 us -> 9.18 us
  transfers between devices with their start and end apart: 25 -> 25, of which waited for: 15 -> 13; matrix products, arithmetic and copies ran while one was open for 1% -> 1% of each run, Pallas kernels for 12% -> 12%
where the time goes in v4:
time: 205 us; the launch traced here: 203 us
  waiting for transfers between devices  89.5 us (44%)
  starting transfers between devices  56.5 us (28%)
  Pallas kernels  44.1 us (22%)
  local copies, waits for them, and re-layouts  9.88 us (5%)
  other arithmetic  2.4 us (1%)
    ppermute x24, waiting for transfers between devices, swap(): out.append(lax.ppermute(value, axis, pairs))  60.9 us
    ppermute x24, starting transfers between devices, swap(): out.append(lax.ppermute(value, axis, pairs))  49.6 us
    all_to_all x1, waiting for transfers between devices, local(): lax.all_to_all(sent, 'blocks', split_axis=0, concat_axis=0, tiled=True)  28.6 us
    pallas_call x1, Pallas kernels, blur_all(): pl.pallas_call(blur_body, out_shape=pltpu.HBM((cells, BX * DZ, NY), jnp.f...  14.4 us
    unnamed x30, local copies, waits for them, and re-layouts  9.18 us
    all_to_all x1, starting transfers between devices, local(): lax.all_to_all(sent, 'blocks', split_axis=0, concat_axis=0, tiled=True)  6.89 us
    pallas_call x1, Pallas kernels, sweep(): pl.pallas_call(functools.partial(sweep_body, slots), out_shape=PIECES, in...  6.86 us
    pallas_call x1, Pallas kernels, spread_ratio(): pl.pallas_call(functools.partial(spread_body, slots), out_shape=PIECES, i...  5.75 us
  transfers between devices with their start and end apart: 25, of which 13 were waited for; matrix products, arithmetic and copies ran while one was open for 1% of the time, Pallas kernels for 12%

profile of v4, /device:TPU:34, one launch (start us, length us, event | category | flops | bytes accessed | tf_op | source)
XLA Modules:
  0.0 202.8 jit_solution(17441128410662206532)
XLA Ops:
  4.6 3.6 %collective-permute-start.1 = (f32[64,16,128]{2,1,0:T(8,128)S(1)}, f32[64,16,128]{2,1,0:T(8,128)S(1)}, u32[]{:S(2)}, u32[]{:S(2)}) collective-permute-start(f32[64,16,128]{2,1,0:T(8,128)S(1)} %get-tuple-element.54), channel_id=1, source_target_pairs={{8,16},{16,8},{24,32},{32,24},{40,48},{48,40},{56,64},{64,56},{72,... | collective-permute-start | bytes 1572872 | tf_op jit(solution)/shard_map/ppermute | solution.py:698
  11.8 2.3 %place.1 = f32[16,520,128]{2,1,0:T(8,128)} custom-call(s32[8]{0:T(128)S(1)} %and_select_fusion.2.owner, s32[8]{0:T(128)S(1)} %copy-done.10, s32[8]{0:T(128)S(1)} %copy-done.11, f32[8,64,8,128]{3,2,1,0:T(8,128)S(1)} %copy-done.4), custom_call_target="tpu_custom_call" | custom-call | tf_op jit(solution)/shard_map/place/pallas_call | solution.py:408
  14.2 2.5 %collective-permute-done.colse = f32[64,16,128]{2,1,0:T(8,128)S(1)} collective-permute-done((f32[64,16,128]{2,1,0:T(8,128)S(1)}, f32[64,16,128]{2,1,0:T(8,128)S(1)}, u32[]{:S(2)}, u32[]{:S(2)}) %collective-permute-start) | collective-permute-done | bytes 524320 | tf_op jit(solution)/shard_map/ppermute | solution.py:698
  16.7 5.3 %collective-permute-done.1.colso = f32[64,16,128]{2,1,0:T(8,128)S(1)} collective-permute-done((f32[64,16,128]{2,1,0:T(8,128)S(1)}, f32[64,16,128]{2,1,0:T(8,128)S(1)}, u32[]{:S(2)}, u32[]{:S(2)}) %collective-permute-start.1) | collective-permute-done | bytes 524320 | tf_op jit(solution)/shard_map/ppermute | solution.py:698
  22.0 6.9 %all-to-all-start = ((f32[16,520,128]{2,1,0:T(8,128)}), f32[16,520,128]{2,1,0:T(8,128)}, u32[]{:S(2)}, u32[]{:S(2)}) async-start(f32[16,520,128]{2,1,0:T(8,128)} %place.1), calls=%async_computation | async-start | bytes 8519680 | tf_op jit(solution)/shard_map/all_to_all | solution.py:717
  28.9 2.5 %collective-permute-start.3 = (f32[30,32,128]{2,1,0:T(8,128)}, f32[30,32,128]{2,1,0:T(8,128)}, u32[]{:S(2)}, u32[]{:S(2)}) collective-permute-start(f32[30,32,128]{2,1,0:T(8,128)} %get-tuple-element.60), channel_id=1, source_target_pairs={{1,2},{2,1},{3,4},{4,3},{5,6},{6,5},{9,10},{10,9},{11,12},{12,11},... | collective-permute-start | bytes 1474568 | tf_op jit(solution)/shard_map/ppermute | solution.py:698
  40.8 3.9 %collective-permute-done.5.sido = f32[30,32,128]{2,1,0:T(8,128)} collective-permute-done((f32[30,32,128]{2,1,0:T(8,128)}, f32[30,32,128]{2,1,0:T(8,128)}, u32[]{:S(2)}, u32[]{:S(2)}) %collective-permute-start.5) | collective-permute-done | bytes 491552 | tf_op jit(solution)/shard_map/ppermute | solution.py:698
  45.7 14.4 %blur_all.1.blurred = f32[24,512,128]{2,1,0:T(8,128)} custom-call(s32[2]{0:T(128)S(1)} %pad_add_fusion.par, f32[64,32,128]{2,1,0:T(8,128)S(1)} %copy-done.1, f32[64,16,128]{2,1,0:T(8,128)S(1)} %collective-permute-done.colse, f32[64,16,128]{2,1,0:T(8,128)S(1)} %copy-done.3, f32[30,32,128]{2,1,0:T(8,128)} %collective-permute-done.2.cene, ...), custom_call_target="tpu_custom_call" | custom-call | tf_op jit(solution)/shard_map/blur_all/pallas_call | solution.py:342
  60.1 28.6 %all-to-all-done.got = f32[16,520,128]{2,1,0:T(8,128)} async-done(((f32[16,520,128]{2,1,0:T(8,128)}), f32[16,520,128]{2,1,0:T(8,128)}, u32[]{:S(2)}, u32[]{:S(2)}) %all-to-all-start) | async-done | bytes 4259872 | tf_op jit(solution)/shard_map/all_to_all | solution.py:717
  91.6 5.7 %spread_ratio.1 = (f32[64,32,128]{2,1,0:T(8,128)S(1)}, f32[64,16,128]{2,1,0:T(8,128)S(1)}, f32[64,16,128]{2,1,0:T(8,128)S(1)}, f32[30,32,128]{2,1,0:T(8,128)S(1)...) custom-call(s32[2]{0:T(128)S(1)} %pad_add_fusion.par, ...), custom_call_target="tpu_custom_call" | custom-call | tf_op jit(solution)/shard_map/spread_ratio/pallas_call | solution.py:360
  97.5 2.5 %collective-permute-start.7 = (f32[30,32,128]{2,1,0:T(8,128)S(1)}, f32[30,32,128]{2,1,0:T(8,128)S(1)}, u32[]{:S(2)}, u32[]{:S(2)}) collective-permute-start(f32[30,32,128]{2,1,0:T(8,128)S(1)} %get-tuple-element.74), channel_id=1, source_target_pairs={{1,2},{2,1},{3,4},{4,3},{5,6},{6,5},{9,10},{10,9},{11,12},{12,11},... | collective-permute-start | bytes 1474568 | tf_op jit(solution)/shard_map/ppermute | solution.py:698
  100.1 7.6 %collective-permute-done.7.sido = f32[30,32,128]{2,1,0:T(8,128)S(1)} collective-permute-done((f32[30,32,128]{2,1,0:T(8,128)S(1)}, f32[30,32,128]{2,1,0:T(8,128)S(1)}, u32[]{:S(2)}, u32[]{:S(2)}) %collective-permute-start.7) | collective-permute-done | bytes 491552 | tf_op jit(solution)/shard_map/ppermute | solution.py:698
  108.6 5.8 %collective-permute-start.11 = (f32[64,16,128]{2,1,0:T(8,128)S(1)}, f32[64,16,128]{2,1,0:T(8,128)S(1)}, u32[]{:S(2)}, u32[]{:S(2)}) collective-permute-start(f32[64,16,128]{2,1,0:T(8,128)S(1)} %get-tuple-element.80), channel_id=1, source_target_pairs={{8,16},{16,8},{24,32},{32,24},{40,48},{48,40},{56,64},{64,56},{72,... | collective-permute-start | bytes 1572872 | tf_op jit(solution)/shard_map/ppermute | solution.py:698
  114.7 2.4 %collective-permute-start.9 = (f32[30,32,128]{2,1,0:T(8,128)S(1)}, f32[30,32,128]{2,1,0:T(8,128)S(1)}, u32[]{:S(2)}, u32[]{:S(2)}) collective-permute-start(f32[30,32,128]{2,1,0:T(8,128)S(1)} %get-tuple-element.78), channel_id=1, source_target_pairs={{1,2},{2,1},{3,4},{4,3},{5,6},{6,5},{9,10},{10,9},{11,12},{12,11},... | collective-permute-start | bytes 1474568 | tf_op jit(solution)/shard_map/ppermute | solution.py:698
  117.1 4.3 %weigh.1.weight = f32[64,32,128]{2,1,0:T(8,128)S(1)} custom-call(s32[2]{0:T(128)S(1)} %pad_add_fusion.1.at, s32[16,16]{1,0:T(8,128)S(1)} %bitcast.6, f32[8,128]{1,0:T(8,128)S(1)} %pad.12.kz, f32[8,128]{1,0:T(8,128)S(1)} %pad.13.kx, bf16[6,256,256]{2,1,0:T(8,128)(2,1)S(1)} %get-tuple-element.56.yb), custom_call_target="tpu_custom_call" | custom-call | tf_op jit(solution)/shard_map/weigh/pallas_call | solution.py:574
  121.4 3.4 %collective-permute-done.9.ceno = f32[30,32,128]{2,1,0:T(8,128)S(1)} collective-permute-done((f32[30,32,128]{2,1,0:T(8,128)S(1)}, f32[30,32,128]{2,1,0:T(8,128)S(1)}, u32[]{:S(2)}, u32[]{:S(2)}) %collective-permute-start.9) | collective-permute-done | bytes 491552 | tf_op jit(solution)/shard_map/ppermute | solution.py:698
  128.3 5.8 %collective-permute-start.13 = (f32[64,16,128]{2,1,0:T(8,128)S(1)}, f32[64,16,128]{2,1,0:T(8,128)S(1)}, u32[]{:S(2)}, u32[]{:S(2)}) collective-permute-start(f32[64,16,128]{2,1,0:T(8,128)S(1)} %get-tuple-element.83), channel_id=1, source_target_pairs={{8,16},{16,8},{24,32},{32,24},{40,48},{48,40},{56,64},{64,56},{72,... | collective-permute-start | bytes 1572872 | tf_op jit(solution)/shard_map/ppermute | solution.py:698
  136.3 5.6 %collective-permute-done.12.colse = f32[64,16,128]{2,1,0:T(8,128)S(1)} collective-permute-done((f32[64,16,128]{2,1,0:T(8,128)S(1)}, f32[64,16,128]{2,1,0:T(8,128)S(1)}, u32[]{:S(2)}, u32[]{:S(2)}) %collective-permute-start.12) | collective-permute-done | bytes 524320 | tf_op jit(solution)/shard_map/ppermute | solution.py:698
  141.8 4.0 %collective-permute-done.13.colso = f32[64,16,128]{2,1,0:T(8,128)S(1)} collective-permute-done((f32[64,16,128]{2,1,0:T(8,128)S(1)}, f32[64,16,128]{2,1,0:T(8,128)S(1)}, u32[]{:S(2)}, u32[]{:S(2)}) %collective-permute-start.13) | collective-permute-done | bytes 524320 | tf_op jit(solution)/shard_map/ppermute | solution.py:698
  148.6 8.2 %collective-permute-done.17.sido = f32[30,32,128]{2,1,0:T(8,128)S(1)} collective-permute-done((f32[30,32,128]{2,1,0:T(8,128)S(1)}, f32[30,32,128]{2,1,0:T(8,128)S(1)}, u32[]{:S(2)}, u32[]{:S(2)}) %collective-permute-start.17) | collective-permute-done | bytes 491552 | tf_op jit(solution)/shard_map/ppermute | solution.py:698
  156.8 6.9 %sweep.1 = (f32[64,32,128]{2,1,0:T(8,128)S(1)}, f32[64,16,128]{2,1,0:T(8,128)S(1)}, f32[64,16,128]{2,1,0:T(8,128)S(1)}, f32[30,32,128]{2,1,0:T(8,128)S(1)}, f32[...) custom-call(s32[2]{0:T(128)S(1)} %pad_add_fusion.par, s32[51]{0:T(128)S(1)} %concatenate.3.meta, ...), custom_call_target="tpu_custom_call" | custom-call | tf_op jit(solution)/shard_map/sweep/pallas_call | solution.py:328
  166.2 8.2 %collective-permute-done.19.sido = f32[30,32,128]{2,1,0:T(8,128)S(1)} collective-permute-done((f32[30,32,128]{2,1,0:T(8,128)S(1)}, f32[30,32,128]{2,1,0:T(8,128)S(1)}, u32[]{:S(2)}, u32[]{:S(2)}) %collective-permute-start.19) | collective-permute-done | bytes 491552 | tf_op jit(solution)/shard_map/ppermute | solution.py:698
  175.3 13.1 %collective-permute-start.23 = (f32[64,16,128]{2,1,0:T(8,128)S(1)}, f32[64,16,128]{2,1,0:T(8,128)S(1)}, u32[]{:S(2)}, u32[]{:S(2)}) collective-permute-start(f32[64,16,128]{2,1,0:T(8,128)S(1)} %get-tuple-element.100), channel_id=1, source_target_pairs={{8,16},{16,8},{24,32},{32,24},{40,48},{48,40},{56,64},{64,56},{72,... | collective-permute-start | bytes 1572872 | tf_op jit(solution)/shard_map/ppermute | solution.py:698
  190.5 8.2 %collective-permute-done.21.ceno = f32[30,32,128]{2,1,0:T(8,128)S(1)} collective-permute-done((f32[30,32,128]{2,1,0:T(8,128)S(1)}, f32[30,32,128]{2,1,0:T(8,128)S(1)}, u32[]{:S(2)}, u32[]{:S(2)}) %collective-permute-start.21) | collective-permute-done | bytes 491552 | tf_op jit(solution)/shard_map/ppermute | solution.py:698
  (85 shorter events, 40.8 us)
Async XLA Ops:
  3.1 13.7 %collective-permute-start = (f32[64,16,128]{2,1,0:T(8,128)S(1)}, f32[64,16,128]{2,1,0:T(8,128)S(1)}, u32[]{:S(2)}, u32[]{:S(2)}) collective-permute-start(f32[64,16,128]{2,1,0:T(8,128)S(1)} %get-tuple-element.53), channel_id=1, source_target_pairs={{0,8},{8,0},{16,24},{24,16},{32,40},{40,32},{48,56},{56,48},{64,72... | collective-permute-start | bytes 1572872 | tf_op jit(solution)/shard_map/ppermute | solution.py:698
  4.6 17.4 %collective-permute-start.1 = (f32[64,16,128]{2,1,0:T(8,128)S(1)}, f32[64,16,128]{2,1,0:T(8,128)S(1)}, u32[]{:S(2)}, u32[]{:S(2)}) collective-permute-start(f32[64,16,128]{2,1,0:T(8,128)S(1)} %get-tuple-element.54), channel_id=1, source_target_pairs={{8,16},{16,8},{24,32},{32,24},{40,48},{48,40},{56,64},{64,56},{72,... | collective-permute-start | bytes 1572872 | tf_op jit(solution)/shard_map/ppermute | solution.py:698
  22.0 66.7 %all-to-all-start = ((f32[16,520,128]{2,1,0:T(8,128)}), f32[16,520,128]{2,1,0:T(8,128)}, u32[]{:S(2)}, u32[]{:S(2)}) async-start(f32[16,520,128]{2,1,0:T(8,128)} %place.1), calls=%async_computation | async-start | bytes 8519680 | tf_op jit(solution)/shard_map/all_to_all | solution.py:717
  28.9 11.9 %collective-permute-start.2 = (f32[30,32,128]{2,1,0:T(8,128)}, f32[30,32,128]{2,1,0:T(8,128)}, u32[]{:S(2)}, u32[]{:S(2)}) collective-permute-start(f32[30,32,128]{2,1,0:T(8,128)} %get-tuple-element.59), channel_id=1, source_target_pairs={{0,1},{1,0},{2,3},{3,2},{4,5},{5,4},{6,7},{7,6},{8,9},{9,8},{10,11... | collective-permute-start | bytes 1474568 | tf_op jit(solution)/shard_map/ppermute | solution.py:698
  28.9 11.9 %collective-permute-start.3 = (f32[30,32,128]{2,1,0:T(8,128)}, f32[30,32,128]{2,1,0:T(8,128)}, u32[]{:S(2)}, u32[]{:S(2)}) collective-permute-start(f32[30,32,128]{2,1,0:T(8,128)} %get-tuple-element.60), channel_id=1, source_target_pairs={{1,2},{2,1},{3,4},{4,3},{5,6},{6,5},{9,10},{10,9},{11,12},{12,11},... | collective-permute-start | bytes 1474568 | tf_op jit(solution)/shard_map/ppermute | solution.py:698
  33.2 7.6 %collective-permute-start.4 = (f32[30,32,128]{2,1,0:T(8,128)}, f32[30,32,128]{2,1,0:T(8,128)}, u32[]{:S(2)}, u32[]{:S(2)}) collective-permute-start(f32[30,32,128]{2,1,0:T(8,128)} %get-tuple-element.61), channel_id=1, source_target_pairs={{0,1},{1,0},{2,3},{3,2},{4,5},{5,4},{6,7},{7,6},{8,9},{9,8},{10,11... | collective-permute-start | bytes 1474568 | tf_op jit(solution)/shard_map/ppermute | solution.py:698
  34.2 10.5 %collective-permute-start.5 = (f32[30,32,128]{2,1,0:T(8,128)}, f32[30,32,128]{2,1,0:T(8,128)}, u32[]{:S(2)}, u32[]{:S(2)}) collective-permute-start(f32[30,32,128]{2,1,0:T(8,128)} %get-tuple-element.62), channel_id=1, source_target_pairs={{1,2},{2,1},{3,4},{4,3},{5,6},{6,5},{9,10},{10,9},{11,12},{12,11},... | collective-permute-start | bytes 1474568 | tf_op jit(solution)/shard_map/ppermute | solution.py:698
  97.4 2.6 %collective-permute-start.6 = (f32[30,32,128]{2,1,0:T(8,128)S(1)}, f32[30,32,128]{2,1,0:T(8,128)S(1)}, u32[]{:S(2)}, u32[]{:S(2)}) collective-permute-start(f32[30,32,128]{2,1,0:T(8,128)S(1)} %get-tuple-element.73), channel_id=1, source_target_pairs={{0,1},{1,0},{2,3},{3,2},{4,5},{5,4},{6,7},{7,6},{8,9},{9,8},{10,11... | collective-permute-start | bytes 1474568 | tf_op jit(solution)/shard_map/ppermute | solution.py:698
  97.5 10.1 %collective-permute-start.7 = (f32[30,32,128]{2,1,0:T(8,128)S(1)}, f32[30,32,128]{2,1,0:T(8,128)S(1)}, u32[]{:S(2)}, u32[]{:S(2)}) collective-permute-start(f32[30,32,128]{2,1,0:T(8,128)S(1)} %get-tuple-element.74), channel_id=1, source_target_pairs={{1,2},{2,1},{3,4},{4,3},{5,6},{6,5},{9,10},{10,9},{11,12},{12,11},... | collective-permute-start | bytes 1474568 | tf_op jit(solution)/shard_map/ppermute | solution.py:698
  108.5 16.3 %collective-permute-start.10 = (f32[64,16,128]{2,1,0:T(8,128)S(1)}, f32[64,16,128]{2,1,0:T(8,128)S(1)}, u32[]{:S(2)}, u32[]{:S(2)}) collective-permute-start(f32[64,16,128]{2,1,0:T(8,128)S(1)} %get-tuple-element.79), channel_id=1, source_target_pairs={{0,8},{8,0},{16,24},{24,16},{32,40},{40,32},{48,56},{56,48},{64,72... | collective-permute-start | bytes 1572872 | tf_op jit(solution)/shard_map/ppermute | solution.py:698
  108.6 18.3 %collective-permute-start.11 = (f32[64,16,128]{2,1,0:T(8,128)S(1)}, f32[64,16,128]{2,1,0:T(8,128)S(1)}, u32[]{:S(2)}, u32[]{:S(2)}) collective-permute-start(f32[64,16,128]{2,1,0:T(8,128)S(1)} %get-tuple-element.80), channel_id=1, source_target_pairs={{8,16},{16,8},{24,32},{32,24},{40,48},{48,40},{56,64},{64,56},{72,... | collective-permute-start | bytes 1572872 | tf_op jit(solution)/shard_map/ppermute | solution.py:698
  114.4 7.0 %collective-permute-start.8 = (f32[30,32,128]{2,1,0:T(8,128)S(1)}, f32[30,32,128]{2,1,0:T(8,128)S(1)}, u32[]{:S(2)}, u32[]{:S(2)}) collective-permute-start(f32[30,32,128]{2,1,0:T(8,128)S(1)} %get-tuple-element.77), channel_id=1, source_target_pairs={{0,1},{1,0},{2,3},{3,2},{4,5},{5,4},{6,7},{7,6},{8,9},{9,8},{10,11... | collective-permute-start | bytes 1474568 | tf_op jit(solution)/shard_map/ppermute | solution.py:698
  114.7 10.1 %collective-permute-start.9 = (f32[30,32,128]{2,1,0:T(8,128)S(1)}, f32[30,32,128]{2,1,0:T(8,128)S(1)}, u32[]{:S(2)}, u32[]{:S(2)}) collective-permute-start(f32[30,32,128]{2,1,0:T(8,128)S(1)} %get-tuple-element.78), channel_id=1, source_target_pairs={{1,2},{2,1},{3,4},{4,3},{5,6},{6,5},{9,10},{10,9},{11,12},{12,11},... | collective-permute-start | bytes 1474568 | tf_op jit(solution)/shard_map/ppermute | solution.py:698
  128.2 13.6 %collective-permute-start.12 = (f32[64,16,128]{2,1,0:T(8,128)S(1)}, f32[64,16,128]{2,1,0:T(8,128)S(1)}, u32[]{:S(2)}, u32[]{:S(2)}) collective-permute-start(f32[64,16,128]{2,1,0:T(8,128)S(1)} %get-tuple-element.82), channel_id=1, source_target_pairs={{0,8},{8,0},{16,24},{24,16},{32,40},{40,32},{48,56},{56,48},{64,72... | collective-permute-start | bytes 1572872 | tf_op jit(solution)/shard_map/ppermute | solution.py:698
  128.3 17.5 %collective-permute-start.13 = (f32[64,16,128]{2,1,0:T(8,128)S(1)}, f32[64,16,128]{2,1,0:T(8,128)S(1)}, u32[]{:S(2)}, u32[]{:S(2)}) collective-permute-start(f32[64,16,128]{2,1,0:T(8,128)S(1)} %get-tuple-element.83), channel_id=1, source_target_pairs={{8,16},{16,8},{24,32},{32,24},{40,48},{48,40},{56,64},{64,56},{72,... | collective-permute-start | bytes 1572872 | tf_op jit(solution)/shard_map/ppermute | solution.py:698
  134.1 14.5 %collective-permute-start.14 = (f32[30,32,128]{2,1,0:T(8,128)S(1)}, f32[30,32,128]{2,1,0:T(8,128)S(1)}, u32[]{:S(2)}, u32[]{:S(2)}) collective-permute-start(f32[30,32,128]{2,1,0:T(8,128)S(1)} %get-tuple-element.84), channel_id=1, source_target_pairs={{0,1},{1,0},{2,3},{3,2},{4,5},{5,4},{6,7},{7,6},{8,9},{9,8},{10,11... | collective-permute-start | bytes 1474568 | tf_op jit(solution)/shard_map/ppermute | solution.py:698
  134.4 14.2 %collective-permute-start.15 = (f32[30,32,128]{2,1,0:T(8,128)S(1)}, f32[30,32,128]{2,1,0:T(8,128)S(1)}, u32[]{:S(2)}, u32[]{:S(2)}) collective-permute-start(f32[30,32,128]{2,1,0:T(8,128)S(1)} %get-tuple-element.85), channel_id=1, source_target_pairs={{1,2},{2,1},{3,4},{4,3},{5,6},{6,5},{9,10},{10,9},{11,12},{12,11},... | collective-permute-start | bytes 1474568 | tf_op jit(solution)/shard_map/ppermute | solution.py:698
  146.5 2.0 %collective-permute-start.16 = (f32[30,32,128]{2,1,0:T(8,128)S(1)}, f32[30,32,128]{2,1,0:T(8,128)S(1)}, u32[]{:S(2)}, u32[]{:S(2)}) collective-permute-start(f32[30,32,128]{2,1,0:T(8,128)S(1)} %get-tuple-element.86), channel_id=1, source_target_pairs={{0,1},{1,0},{2,3},{3,2},{4,5},{5,4},{6,7},{7,6},{8,9},{9,8},{10,11... | collective-permute-start | bytes 1474568 | tf_op jit(solution)/shard_map/ppermute | solution.py:698
  146.6 10.1 %collective-permute-start.17 = (f32[30,32,128]{2,1,0:T(8,128)S(1)}, f32[30,32,128]{2,1,0:T(8,128)S(1)}, u32[]{:S(2)}, u32[]{:S(2)}) collective-permute-start(f32[30,32,128]{2,1,0:T(8,128)S(1)} %get-tuple-element.87), channel_id=1, source_target_pairs={{1,2},{2,1},{3,4},{4,3},{5,6},{6,5},{9,10},{10,9},{11,12},{12,11},... | collective-permute-start | bytes 1474568 | tf_op jit(solution)/shard_map/ppermute | solution.py:698
  163.7 2.5 %collective-permute-start.18 = (f32[30,32,128]{2,1,0:T(8,128)S(1)}, f32[30,32,128]{2,1,0:T(8,128)S(1)}, u32[]{:S(2)}, u32[]{:S(2)}) collective-permute-start(f32[30,32,128]{2,1,0:T(8,128)S(1)} %get-tuple-element.93), channel_id=1, source_target_pairs={{0,1},{1,0},{2,3},{3,2},{4,5},{5,4},{6,7},{7,6},{8,9},{9,8},{10,11... | collective-permute-start | bytes 1474568 | tf_op jit(solution)/shard_map/ppermute | solution.py:698
  164.2 10.1 %collective-permute-start.19 = (f32[30,32,128]{2,1,0:T(8,128)S(1)}, f32[30,32,128]{2,1,0:T(8,128)S(1)}, u32[]{:S(2)}, u32[]{:S(2)}) collective-permute-start(f32[30,32,128]{2,1,0:T(8,128)S(1)} %get-tuple-element.94), channel_id=1, source_target_pairs={{1,2},{2,1},{3,4},{4,3},{5,6},{6,5},{9,10},{10,9},{11,12},{12,11},... | collective-permute-start | bytes 1474568 | tf_op jit(solution)/shard_map/ppermute | solution.py:698
  175.2 23.5 %collective-permute-start.22 = (f32[64,16,128]{2,1,0:T(8,128)S(1)}, f32[64,16,128]{2,1,0:T(8,128)S(1)}, u32[]{:S(2)}, u32[]{:S(2)}) collective-permute-start(f32[64,16,128]{2,1,0:T(8,128)S(1)} %get-tuple-element.99), channel_id=1, source_target_pairs={{0,8},{8,0},{16,24},{24,16},{32,40},{40,32},{48,56},{56,48},{64,72... | collective-permute-start | bytes 1572872 | tf_op jit(solution)/shard_map/ppermute | solution.py:698
  175.3 25.3 %collective-permute-start.23 = (f32[64,16,128]{2,1,0:T(8,128)S(1)}, f32[64,16,128]{2,1,0:T(8,128)S(1)}, u32[]{:S(2)}, u32[]{:S(2)}) collective-permute-start(f32[64,16,128]{2,1,0:T(8,128)S(1)} %get-tuple-element.100), channel_id=1, source_target_pairs={{8,16},{16,8},{24,32},{32,24},{40,48},{48,40},{56,64},{64,56},{72,... | collective-permute-start | bytes 1572872 | tf_op jit(solution)/shard_map/ppermute | solution.py:698
  188.6 10.1 %collective-permute-start.21 = (f32[30,32,128]{2,1,0:T(8,128)S(1)}, f32[30,32,128]{2,1,0:T(8,128)S(1)}, u32[]{:S(2)}, u32[]{:S(2)}) collective-permute-start(f32[30,32,128]{2,1,0:T(8,128)S(1)} %get-tuple-element.98), channel_id=1, source_target_pairs={{1,2},{2,1},{3,4},{4,3},{5,6},{6,5},{9,10},{10,9},{11,12},{12,11},... | collective-permute-start | bytes 1474568 | tf_op jit(solution)/shard_map/ppermute | solution.py:698
  (16 other events, 113.1 us)

commit v5 on v4

--- a/solution.py
+++ b/solution.py
@@ -200,12 +200,26 @@
     return count, arrive
 
 
+def slots_of(step, k, slots, order, count):
+    return [jnp.where(step * k + i < count, order[step * k + i], slots) for i in range(step)]
+
+
+def blur_tiles(step, slots, meta, order, count, s_ref, zf, yf, held):
+    @pl.loop(0, (count + step - 1) // step)
+    def _(k):
+        slot = slots_of(step, k, slots, order, count)
+        out = []
+        for i in range(step):
+            row = pl.multiple_of((step * k + i) * BX, BX)
+            out.append(forward_tile(s_ref, zf, yf, meta[slots + 1 + slot[i]], row))
+        for i in range(step):
+            held[slot[i]] = out[i]
+
+
 def visit_tiles(step, slots, meta, order, count, arrive, s_ref, data, zb, yb, predict):
     @pl.loop(0, (count + step - 1) // step)
     def _(k):
-        slot = [
-            jnp.where(step * k + i < count, order[step * k + i], slots) for i in range(step)
-        ]
+        slot = slots_of(step, k, slots, order, count)
         for i in slot:
             arrive(i)
         view = [meta[slots + 1 + i] for i in slot]
@@ -229,15 +243,17 @@
 
 def sweep_body(slots, par, meta, est, colse, colso, cene, ceno, side, sido, got, fx, zf, zb, yf,
                yb, omidc, omidl, omidr, ocene, oceno, oside, osido, s_ref, order, data, sem, picked,
-               xb, xf):
+               xb, xf, held):
     count, arrive = fetches(slots, meta, order, [data_move(got, data, sem)])
     gather_x(slots, meta, order, count, fx, picked, xf, xb)
     forward_x(par, s_ref, xf, est, colse, colso, cene, ceno, side, sido)
 
+    blur_tiles(4, slots, meta, order, count, s_ref, zf, yf, held)
+
     def predict(slot, view, row):
-        return forward_tile(s_ref, zf, yf, view, row)
-
-    visit_tiles(2, slots, meta, order, count, arrive, s_ref, data, zb, yb, predict)
+        return held[slot]
+
+    visit_tiles(4, slots, meta, order, count, arrive, s_ref, data, zb, yb, predict)
     clear_rest(slots, count, s_ref)
     backward_x(par, s_ref, xb, omidc, omidl, omidr, ocene, oceno, oside, osido)
 
@@ -250,29 +266,35 @@
             staged.at[pl.ds(2 * k, 2)], out.at[pl.ds(2 * k, 2)], sem.at[k]
         )
 
-    @pl.loop(0, V * BLK_DEV // 2)
-    def _(k):
-        view = k // (BLK_DEV // 2)
-        cells = (2 * k, 2 * k + 1)
-        results = [
-            forward_tile(s_ref, zf, yf, view, pl.multiple_of(cell * BX, BX)) for cell in cells
-        ]
-        for cell, result in zip(cells, results):
-            staged[cell] = result
-        push(k).start()
+    @pl.loop(0, V)
+    def _(view):
+        for i in range(BLK_DEV):
+            cell = view * BLK_DEV + i
+            staged[cell] = forward_tile(s_ref, zf, yf, view, pl.multiple_of(cell * BX, BX))
+        push(2 * view).start()
+        push(2 * view + 1).start()
 
     @pl.loop(0, V * BLK_DEV // 2)
     def _(k):
         push(k).wait()
 
 
-def spread_body(slots, par, meta, blurred, got, fx, zb, yb,
+def spread_body(slots, par, meta, blurred, got, far_fx, far_zb, far_yb,
                 omidc, omidl, omidr, ocene, oceno, oside, osido, s_ref, order, data, sem, picked,
-                xb, held, held_sem):
+                xb, held, held_sem, fx, zb, yb, table_sem):
+    tables = [
+        pltpu.make_async_copy(far, close, table_sem.at[i])
+        for i, (far, close) in enumerate(((far_fx, fx), (far_zb, zb), (far_yb, yb)))
+    ]
+    for copy in tables:
+        copy.start()
+
     def make(slot, cell):
         return pltpu.make_async_copy(blurred.at[cell], held.at[slot], held_sem.at[slot])
 
     count, arrive = fetches(slots, meta, order, [make, data_move(got, data, sem)])
+    for copy in tables:
+        copy.wait()
     gather_x(slots, meta, order, count, fx, picked, None, xb)
 
     def predict(slot, view, row):
@@ -330,7 +352,11 @@
         out_shape=PIECES,
         in_specs=[SM] * 2 + [VM] * 7 + [HB] + [VM] * 5,
         out_specs=[VM] * 7,
-        scratch_shapes=visit_scratch(slots) + [pltpu.VMEM((slots * BX, 3 * EX), jnp.bfloat16)],
+        scratch_shapes=visit_scratch(slots)
+        + [
+            pltpu.VMEM((slots * BX, 3 * EX), jnp.bfloat16),
+            pltpu.VMEM((slots + 1, BX * DZ, NY), jnp.float32),
+        ],
         compiler_params=params(36),
         name="sweep",
     )(par, meta, *pieces, in_hbm(got), *tables[1:])
@@ -360,16 +386,18 @@
     return pl.pallas_call(
         functools.partial(spread_body, slots),
         out_shape=PIECES,
-        in_specs=[SM] * 2 + [HB] * 2 + [VM] * 3,
+        in_specs=[SM] * 2 + [HB] * 5,
         out_specs=[VM] * 7,
         scratch_shapes=visit_scratch(slots)
         + [
             pltpu.VMEM((slots + 1, BX * DZ, NY), jnp.float32),
             pltpu.SemaphoreType.DMA((slots + 1,)),
-        ],
+        ]
+        + [pltpu.VMEM(table.shape, table.dtype) for table in (fx, zb, yb)]
+        + [pltpu.SemaphoreType.DMA((3,))],
         compiler_params=params(36),
         name="spread_ratio",
-    )(par, meta, in_hbm(blurred), in_hbm(got), fx, zb, yb)
+    )(par, meta, *[in_hbm(value) for value in (blurred, got, fx, zb, yb)])
 
 
 def place_body(owner, pair, shift, tiles, out, staged, labels, sem, label_sem):
@@ -691,12 +719,12 @@
 def swap(even, odd, axis):
     count = lax.axis_size(axis)
     out = []
-    for value, first in ((even, 0), (odd, 1)):
+    for value, first in ((odd, 1), (even, 0)):
         pairs = []
         for i in range(first, count - 1, 2):
             pairs += [(i, i + 1), (i + 1, i)]
         out.append(lax.ppermute(value, axis, pairs))
-    return out
+    return out[::-1]
 
 
 def local(estimate0, tiles, psf_z, psf_x, psf_y, tile_pair, tile_shift):

time: 205 us -> 203 us (level); the launches traced: 203 us -> 204 us
  starting transfers between devices: 56.5 us -> 38.6 us
  waiting for transfers between devices: 89.5 us -> 103 us
  Pallas kernels: 44.1 us -> 52.9 us
  local copies, waits for them, and re-layouts: 9.88 us -> 6.53 us
    ppermute x24, starting transfers between devices: 49.6 us -> 31.7 us  [swap(): out.append(lax.ppermute(value, axis, pairs))]
    ppermute x24, waiting for transfers between devices: 60.9 us -> 71.7 us  [swap(): out.append(lax.ppermute(value, axis, pairs))]
    pallas_call x1, Pallas kernels: 6.86 us -> 13.8 us  [sweep(): pl.pallas_call(functools.partial(sweep_body, slots), out_shape=PIECES, in...]
    pallas_call x1, Pallas kernels: 5.75 us -> 9.13 us  [spread_ratio(): pl.pallas_call(functools.partial(spread_body, slots), out_shape=PIECES, i...]
    all_to_all x1, waiting for transfers between devices: 28.6 us -> 31.6 us  [local(): lax.all_to_all(sent, 'blocks', split_axis=0, concat_axis=0, tiled=True)]
    unnamed x30 -> x28, local copies, waits for them, and re-layouts: 9.18 us -> 6.43 us
  transfers between devices with their start and end apart: 25 -> 25, of which waited for: 13 -> 15; matrix products, arithmetic and copies ran while one was open for 1% -> 1% of each run, Pallas kernels for 12% -> 11%
where the time goes in v5:
time: 203 us; the launch traced here: 204 us
  waiting for transfers between devices  103 us (51%)
  Pallas kernels  52.9 us (26%)
  starting transfers between devices  38.6 us (19%)
  local copies, waits for them, and re-layouts  6.53 us (3%)
  other arithmetic  2.4 us (1%)
    ppermute x24, waiting for transfers between devices, swap(): out.append(lax.ppermute(value, axis, pairs))  71.7 us
    ppermute x24, starting transfers between devices, swap(): out.append(lax.ppermute(value, axis, pairs))  31.7 us
    all_to_all x1, waiting for transfers between devices, local(): lax.all_to_all(sent, 'blocks', split_axis=0, concat_axis=0, tiled=True)  31.6 us
    pallas_call x1, Pallas kernels, sweep(): pl.pallas_call(functools.partial(sweep_body, slots), out_shape=PIECES, in...  13.8 us
    pallas_call x1, Pallas kernels, blur_all(): pl.pallas_call(blur_body, out_shape=pltpu.HBM((cells, BX * DZ, NY), jnp.f...  12.4 us
    pallas_call x1, Pallas kernels, spread_ratio(): pl.pallas_call(functools.partial(spread_body, slots), out_shape=PIECES, i...  9.13 us
    all_to_all x1, starting transfers between devices, local(): lax.all_to_all(sent, 'blocks', split_axis=0, concat_axis=0, tiled=True)  6.89 us
    unnamed x28, local copies, waits for them, and re-layouts  6.43 us
  transfers between devices with their start and end apart: 25, of which 15 were waited for; matrix products, arithmetic and copies ran while one was open for 1% of the time, Pallas kernels for 11%

profile of v5, /device:TPU:34, one launch (start us, length us, event | category | flops | bytes accessed | tf_op | source)
XLA Modules:
  0.0 204.1 jit_solution(10607510507197619801)
XLA Ops:
  4.6 3.6 %collective-permute-start.1 = (f32[64,16,128]{2,1,0:T(8,128)S(1)}, f32[64,16,128]{2,1,0:T(8,128)S(1)}, u32[]{:S(2)}, u32[]{:S(2)}) collective-permute-start(f32[64,16,128]{2,1,0:T(8,128)S(1)} %get-tuple-element.54), channel_id=1, source_target_pairs={{8,16},{16,8},{24,32},{32,24},{40,48},{48,40},{56,64},{64,56},{72,... | collective-permute-start | bytes 1572872 | tf_op jit(solution)/shard_map/ppermute | solution.py:726
  11.8 2.2 %place.1 = f32[16,520,128]{2,1,0:T(8,128)} custom-call(s32[8]{0:T(128)S(1)} %and_select_fusion.2.owner, s32[8]{0:T(128)S(1)} %copy-done.9, s32[8]{0:T(128)S(1)} %copy-done.10, f32[8,64,8,128]{3,2,1,0:T(8,128)S(1)} %copy-done.4), custom_call_target="tpu_custom_call" | custom-call | tf_op jit(solution)/shard_map/place/pallas_call | solution.py:436
  14.1 2.6 %collective-permute-done.colse = f32[64,16,128]{2,1,0:T(8,128)S(1)} collective-permute-done((f32[64,16,128]{2,1,0:T(8,128)S(1)}, f32[64,16,128]{2,1,0:T(8,128)S(1)}, u32[]{:S(2)}, u32[]{:S(2)}) %collective-permute-start) | collective-permute-done | bytes 524320 | tf_op jit(solution)/shard_map/ppermute | solution.py:726
  16.7 5.3 %collective-permute-done.1.colso = f32[64,16,128]{2,1,0:T(8,128)S(1)} collective-permute-done((f32[64,16,128]{2,1,0:T(8,128)S(1)}, f32[64,16,128]{2,1,0:T(8,128)S(1)}, u32[]{:S(2)}, u32[]{:S(2)}) %collective-permute-start.1) | collective-permute-done | bytes 524320 | tf_op jit(solution)/shard_map/ppermute | solution.py:726
  22.0 6.9 %all-to-all-start = ((f32[16,520,128]{2,1,0:T(8,128)}), f32[16,520,128]{2,1,0:T(8,128)}, u32[]{:S(2)}, u32[]{:S(2)}) async-start(f32[16,520,128]{2,1,0:T(8,128)} %place.1), calls=%async_computation | async-start | bytes 8519680 | tf_op jit(solution)/shard_map/all_to_all | solution.py:745
  28.9 2.5 %collective-permute-start.3 = (f32[30,32,128]{2,1,0:T(8,128)}, f32[30,32,128]{2,1,0:T(8,128)}, u32[]{:S(2)}, u32[]{:S(2)}) collective-permute-start(f32[30,32,128]{2,1,0:T(8,128)} %get-tuple-element.60), channel_id=1, source_target_pairs={{1,2},{2,1},{3,4},{4,3},{5,6},{6,5},{9,10},{10,9},{11,12},{12,11},... | collective-permute-start | bytes 1474568 | tf_op jit(solution)/shard_map/ppermute | solution.py:726
  40.4 4.3 %collective-permute-done.5.sido = f32[30,32,128]{2,1,0:T(8,128)} collective-permute-done((f32[30,32,128]{2,1,0:T(8,128)}, f32[30,32,128]{2,1,0:T(8,128)}, u32[]{:S(2)}, u32[]{:S(2)}) %collective-permute-start.5) | collective-permute-done | bytes 491552 | tf_op jit(solution)/shard_map/ppermute | solution.py:726
  44.7 12.4 %blur_all.1.blurred = f32[24,512,128]{2,1,0:T(8,128)} custom-call(s32[2]{0:T(128)S(1)} %pad_add_fusion.par, f32[64,32,128]{2,1,0:T(8,128)S(1)} %copy-done.1, f32[64,16,128]{2,1,0:T(8,128)S(1)} %collective-permute-done.colse, f32[64,16,128]{2,1,0:T(8,128)S(1)} %collective-permute-done.1.colso, f32[30,32,128]{2,1,0:T(8,128)} %collective-permute-done.2.cene, ...), custom_call_target="tpu_custom_call" | custom-call | tf_op jit(solution)/shard_map/blur_all/pallas_call | solution.py:368
  57.1 31.6 %all-to-all-done.got = f32[16,520,128]{2,1,0:T(8,128)} async-done(((f32[16,520,128]{2,1,0:T(8,128)}), f32[16,520,128]{2,1,0:T(8,128)}, u32[]{:S(2)}, u32[]{:S(2)}) %all-to-all-start) | async-done | bytes 4259872 | tf_op jit(solution)/shard_map/all_to_all | solution.py:745
  89.8 9.1 %spread_ratio.1 = (f32[64,32,128]{2,1,0:T(8,128)S(1)}, f32[64,16,128]{2,1,0:T(8,128)S(1)}, f32[64,16,128]{2,1,0:T(8,128)S(1)}, f32[30,32,128]{2,1,0:T(8,128)S(1)...) custom-call(s32[2]{0:T(128)S(1)} %pad_add_fusion.par, ...), custom_call_target="tpu_custom_call" | custom-call | tf_op jit(solution)/shard_map/spread_ratio/pallas_call | solution.py:386
  99.0 2.5 %collective-permute-start.7 = (f32[30,32,128]{2,1,0:T(8,128)S(1)}, f32[30,32,128]{2,1,0:T(8,128)S(1)}, u32[]{:S(2)}, u32[]{:S(2)}) collective-permute-start(f32[30,32,128]{2,1,0:T(8,128)S(1)} %get-tuple-element.74), channel_id=1, source_target_pairs={{1,2},{2,1},{3,4},{4,3},{5,6},{6,5},{9,10},{10,9},{11,12},{12,11},... | collective-permute-start | bytes 1474568 | tf_op jit(solution)/shard_map/ppermute | solution.py:726
  101.5 7.6 %collective-permute-done.7.sido = f32[30,32,128]{2,1,0:T(8,128)S(1)} collective-permute-done((f32[30,32,128]{2,1,0:T(8,128)S(1)}, f32[30,32,128]{2,1,0:T(8,128)S(1)}, u32[]{:S(2)}, u32[]{:S(2)}) %collective-permute-start.7) | collective-permute-done | bytes 491552 | tf_op jit(solution)/shard_map/ppermute | solution.py:726
  112.8 2.4 %collective-permute-start.9 = (f32[30,32,128]{2,1,0:T(8,128)S(1)}, f32[30,32,128]{2,1,0:T(8,128)S(1)}, u32[]{:S(2)}, u32[]{:S(2)}) collective-permute-start(f32[30,32,128]{2,1,0:T(8,128)S(1)} %get-tuple-element.78), channel_id=1, source_target_pairs={{1,2},{2,1},{3,4},{4,3},{5,6},{6,5},{9,10},{10,9},{11,12},{12,11},... | collective-permute-start | bytes 1474568 | tf_op jit(solution)/shard_map/ppermute | solution.py:726
  115.2 4.8 %weigh.1.weight = f32[64,32,128]{2,1,0:T(8,128)S(1)} custom-call(s32[2]{0:T(128)S(1)} %pad_add_fusion.1.at, s32[16,16]{1,0:T(8,128)S(1)} %bitcast.6, f32[8,128]{1,0:T(8,128)S(1)} %pad.12.kz, f32[8,128]{1,0:T(8,128)S(1)} %pad.13.kx, bf16[6,256,256]{2,1,0:T(8,128)(2,1)S(1)} %copy-done.3), custom_call_target="tpu_custom_call" | custom-call | tf_op jit(solution)/shard_map/weigh/pallas_call | solution.py:602
  120.0 2.9 %collective-permute-done.9.ceno = f32[30,32,128]{2,1,0:T(8,128)S(1)} collective-permute-done((f32[30,32,128]{2,1,0:T(8,128)S(1)}, f32[30,32,128]{2,1,0:T(8,128)S(1)}, u32[]{:S(2)}, u32[]{:S(2)}) %collective-permute-start.9) | collective-permute-done | bytes 491552 | tf_op jit(solution)/shard_map/ppermute | solution.py:726
  124.4 4.1 %collective-permute-done.11.colso = f32[64,16,128]{2,1,0:T(8,128)S(1)} collective-permute-done((f32[64,16,128]{2,1,0:T(8,128)S(1)}, f32[64,16,128]{2,1,0:T(8,128)S(1)}, u32[]{:S(2)}, u32[]{:S(2)}) %collective-permute-start.11) | collective-permute-done | bytes 524320 | tf_op jit(solution)/shard_map/ppermute | solution.py:726
  130.1 2.2 %collective-permute-start.13 = (f32[64,16,128]{2,1,0:T(8,128)S(1)}, f32[64,16,128]{2,1,0:T(8,128)S(1)}, u32[]{:S(2)}, u32[]{:S(2)}) collective-permute-start(f32[64,16,128]{2,1,0:T(8,128)S(1)} %get-tuple-element.83), channel_id=1, source_target_pairs={{8,16},{16,8},{24,32},{32,24},{40,48},{48,40},{56,64},{64,56},{72,... | collective-permute-start | bytes 1572872 | tf_op jit(solution)/shard_map/ppermute | solution.py:726
  134.4 9.3 %collective-permute-done.12.colse = f32[64,16,128]{2,1,0:T(8,128)S(1)} collective-permute-done((f32[64,16,128]{2,1,0:T(8,128)S(1)}, f32[64,16,128]{2,1,0:T(8,128)S(1)}, u32[]{:S(2)}, u32[]{:S(2)}) %collective-permute-start.12) | collective-permute-done | bytes 524320 | tf_op jit(solution)/shard_map/ppermute | solution.py:726
  143.6 4.0 %collective-permute-done.13.colso = f32[64,16,128]{2,1,0:T(8,128)S(1)} collective-permute-done((f32[64,16,128]{2,1,0:T(8,128)S(1)}, f32[64,16,128]{2,1,0:T(8,128)S(1)}, u32[]{:S(2)}, u32[]{:S(2)}) %collective-permute-start.13) | collective-permute-done | bytes 524320 | tf_op jit(solution)/shard_map/ppermute | solution.py:726
  150.4 8.2 %collective-permute-done.17.sido = f32[30,32,128]{2,1,0:T(8,128)S(1)} collective-permute-done((f32[30,32,128]{2,1,0:T(8,128)S(1)}, f32[30,32,128]{2,1,0:T(8,128)S(1)}, u32[]{:S(2)}, u32[]{:S(2)}) %collective-permute-start.17) | collective-permute-done | bytes 491552 | tf_op jit(solution)/shard_map/ppermute | solution.py:726
  158.6 13.8 %sweep.1 = (f32[64,32,128]{2,1,0:T(8,128)S(1)}, f32[64,16,128]{2,1,0:T(8,128)S(1)}, f32[64,16,128]{2,1,0:T(8,128)S(1)}, f32[30,32,128]{2,1,0:T(8,128)S(1)}, f32[...) custom-call(s32[2]{0:T(128)S(1)} %pad_add_fusion.par, s32[51]{0:T(128)S(1)} %concatenate.3.meta, ...), custom_call_target="tpu_custom_call" | custom-call | tf_op jit(solution)/shard_map/sweep/pallas_call | solution.py:350
  174.9 8.2 %collective-permute-done.19.sido = f32[30,32,128]{2,1,0:T(8,128)S(1)} collective-permute-done((f32[30,32,128]{2,1,0:T(8,128)S(1)}, f32[30,32,128]{2,1,0:T(8,128)S(1)}, u32[]{:S(2)}, u32[]{:S(2)}) %collective-permute-start.19) | collective-permute-done | bytes 491552 | tf_op jit(solution)/shard_map/ppermute | solution.py:726
  188.3 8.0 %collective-permute-done.21.ceno = f32[30,32,128]{2,1,0:T(8,128)S(1)} collective-permute-done((f32[30,32,128]{2,1,0:T(8,128)S(1)}, f32[30,32,128]{2,1,0:T(8,128)S(1)}, u32[]{:S(2)}, u32[]{:S(2)}) %collective-permute-start.21) | collective-permute-done | bytes 491552 | tf_op jit(solution)/shard_map/ppermute | solution.py:726
  198.0 4.0 %collective-permute-done.23.colso = f32[64,16,128]{2,1,0:T(8,128)S(1)} collective-permute-done((f32[64,16,128]{2,1,0:T(8,128)S(1)}, f32[64,16,128]{2,1,0:T(8,128)S(1)}, u32[]{:S(2)}, u32[]{:S(2)}) %collective-permute-start.23) | collective-permute-done | bytes 524320 | tf_op jit(solution)/shard_map/ppermute | solution.py:726
  (83 shorter events, 41.2 us)
Async XLA Ops:
  3.1 13.7 %collective-permute-start = (f32[64,16,128]{2,1,0:T(8,128)S(1)}, f32[64,16,128]{2,1,0:T(8,128)S(1)}, u32[]{:S(2)}, u32[]{:S(2)}) collective-permute-start(f32[64,16,128]{2,1,0:T(8,128)S(1)} %get-tuple-element.53), channel_id=1, source_target_pairs={{0,8},{8,0},{16,24},{24,16},{32,40},{40,32},{48,56},{56,48},{64,72... | collective-permute-start | bytes 1572872 | tf_op jit(solution)/shard_map/ppermute | solution.py:726
  4.6 17.4 %collective-permute-start.1 = (f32[64,16,128]{2,1,0:T(8,128)S(1)}, f32[64,16,128]{2,1,0:T(8,128)S(1)}, u32[]{:S(2)}, u32[]{:S(2)}) collective-permute-start(f32[64,16,128]{2,1,0:T(8,128)S(1)} %get-tuple-element.54), channel_id=1, source_target_pairs={{8,16},{16,8},{24,32},{32,24},{40,48},{48,40},{56,64},{64,56},{72,... | collective-permute-start | bytes 1572872 | tf_op jit(solution)/shard_map/ppermute | solution.py:726
  22.0 66.7 %all-to-all-start = ((f32[16,520,128]{2,1,0:T(8,128)}), f32[16,520,128]{2,1,0:T(8,128)}, u32[]{:S(2)}, u32[]{:S(2)}) async-start(f32[16,520,128]{2,1,0:T(8,128)} %place.1), calls=%async_computation | async-start | bytes 8519680 | tf_op jit(solution)/shard_map/all_to_all | solution.py:745
  28.9 11.5 %collective-permute-start.2 = (f32[30,32,128]{2,1,0:T(8,128)}, f32[30,32,128]{2,1,0:T(8,128)}, u32[]{:S(2)}, u32[]{:S(2)}) collective-permute-start(f32[30,32,128]{2,1,0:T(8,128)} %get-tuple-element.59), channel_id=1, source_target_pairs={{0,1},{1,0},{2,3},{3,2},{4,5},{5,4},{6,7},{7,6},{8,9},{9,8},{10,11... | collective-permute-start | bytes 1474568 | tf_op jit(solution)/shard_map/ppermute | solution.py:726
  28.9 11.5 %collective-permute-start.3 = (f32[30,32,128]{2,1,0:T(8,128)}, f32[30,32,128]{2,1,0:T(8,128)}, u32[]{:S(2)}, u32[]{:S(2)}) collective-permute-start(f32[30,32,128]{2,1,0:T(8,128)} %get-tuple-element.60), channel_id=1, source_target_pairs={{1,2},{2,1},{3,4},{4,3},{5,6},{6,5},{9,10},{10,9},{11,12},{12,11},... | collective-permute-start | bytes 1474568 | tf_op jit(solution)/shard_map/ppermute | solution.py:726
  33.2 7.2 %collective-permute-start.4 = (f32[30,32,128]{2,1,0:T(8,128)}, f32[30,32,128]{2,1,0:T(8,128)}, u32[]{:S(2)}, u32[]{:S(2)}) collective-permute-start(f32[30,32,128]{2,1,0:T(8,128)} %get-tuple-element.61), channel_id=1, source_target_pairs={{0,1},{1,0},{2,3},{3,2},{4,5},{5,4},{6,7},{7,6},{8,9},{9,8},{10,11... | collective-permute-start | bytes 1474568 | tf_op jit(solution)/shard_map/ppermute | solution.py:726
  34.2 10.5 %collective-permute-start.5 = (f32[30,32,128]{2,1,0:T(8,128)}, f32[30,32,128]{2,1,0:T(8,128)}, u32[]{:S(2)}, u32[]{:S(2)}) collective-permute-start(f32[30,32,128]{2,1,0:T(8,128)} %get-tuple-element.62), channel_id=1, source_target_pairs={{1,2},{2,1},{3,4},{4,3},{5,6},{6,5},{9,10},{10,9},{11,12},{12,11},... | collective-permute-start | bytes 1474568 | tf_op jit(solution)/shard_map/ppermute | solution.py:726
  98.9 2.6 %collective-permute-start.6 = (f32[30,32,128]{2,1,0:T(8,128)S(1)}, f32[30,32,128]{2,1,0:T(8,128)S(1)}, u32[]{:S(2)}, u32[]{:S(2)}) collective-permute-start(f32[30,32,128]{2,1,0:T(8,128)S(1)} %get-tuple-element.73), channel_id=1, source_target_pairs={{0,1},{1,0},{2,3},{3,2},{4,5},{5,4},{6,7},{7,6},{8,9},{9,8},{10,11... | collective-permute-start | bytes 1474568 | tf_op jit(solution)/shard_map/ppermute | solution.py:726
  99.0 10.1 %collective-permute-start.7 = (f32[30,32,128]{2,1,0:T(8,128)S(1)}, f32[30,32,128]{2,1,0:T(8,128)S(1)}, u32[]{:S(2)}, u32[]{:S(2)}) collective-permute-start(f32[30,32,128]{2,1,0:T(8,128)S(1)} %get-tuple-element.74), channel_id=1, source_target_pairs={{1,2},{2,1},{3,4},{4,3},{5,6},{6,5},{9,10},{10,9},{11,12},{12,11},... | collective-permute-start | bytes 1474568 | tf_op jit(solution)/shard_map/ppermute | solution.py:726
  110.0 14.4 %collective-permute-start.10 = (f32[64,16,128]{2,1,0:T(8,128)S(1)}, f32[64,16,128]{2,1,0:T(8,128)S(1)}, u32[]{:S(2)}, u32[]{:S(2)}) collective-permute-start(f32[64,16,128]{2,1,0:T(8,128)S(1)} %get-tuple-element.79), channel_id=1, source_target_pairs={{0,8},{8,0},{16,24},{24,16},{32,40},{40,32},{48,56},{56,48},{64,72... | collective-permute-start | bytes 1572872 | tf_op jit(solution)/shard_map/ppermute | solution.py:726
  110.1 18.4 %collective-permute-start.11 = (f32[64,16,128]{2,1,0:T(8,128)S(1)}, f32[64,16,128]{2,1,0:T(8,128)S(1)}, u32[]{:S(2)}, u32[]{:S(2)}) collective-permute-start(f32[64,16,128]{2,1,0:T(8,128)S(1)} %get-tuple-element.80), channel_id=1, source_target_pairs={{8,16},{16,8},{24,32},{32,24},{40,48},{48,40},{56,64},{64,56},{72,... | collective-permute-start | bytes 1572872 | tf_op jit(solution)/shard_map/ppermute | solution.py:726
  112.2 7.8 %collective-permute-start.8 = (f32[30,32,128]{2,1,0:T(8,128)S(1)}, f32[30,32,128]{2,1,0:T(8,128)S(1)}, u32[]{:S(2)}, u32[]{:S(2)}) collective-permute-start(f32[30,32,128]{2,1,0:T(8,128)S(1)} %get-tuple-element.77), channel_id=1, source_target_pairs={{0,1},{1,0},{2,3},{3,2},{4,5},{5,4},{6,7},{7,6},{8,9},{9,8},{10,11... | collective-permute-start | bytes 1474568 | tf_op jit(solution)/shard_map/ppermute | solution.py:726
  112.8 10.1 %collective-permute-start.9 = (f32[30,32,128]{2,1,0:T(8,128)S(1)}, f32[30,32,128]{2,1,0:T(8,128)S(1)}, u32[]{:S(2)}, u32[]{:S(2)}) collective-permute-start(f32[30,32,128]{2,1,0:T(8,128)S(1)} %get-tuple-element.78), channel_id=1, source_target_pairs={{1,2},{2,1},{3,4},{4,3},{5,6},{6,5},{9,10},{10,9},{11,12},{12,11},... | collective-permute-start | bytes 1474568 | tf_op jit(solution)/shard_map/ppermute | solution.py:726
  129.9 13.8 %collective-permute-start.12 = (f32[64,16,128]{2,1,0:T(8,128)S(1)}, f32[64,16,128]{2,1,0:T(8,128)S(1)}, u32[]{:S(2)}, u32[]{:S(2)}) collective-permute-start(f32[64,16,128]{2,1,0:T(8,128)S(1)} %get-tuple-element.82), channel_id=1, source_target_pairs={{0,8},{8,0},{16,24},{24,16},{32,40},{40,32},{48,56},{56,48},{64,72... | collective-permute-start | bytes 1572872 | tf_op jit(solution)/shard_map/ppermute | solution.py:726
  130.1 17.5 %collective-permute-start.13 = (f32[64,16,128]{2,1,0:T(8,128)S(1)}, f32[64,16,128]{2,1,0:T(8,128)S(1)}, u32[]{:S(2)}, u32[]{:S(2)}) collective-permute-start(f32[64,16,128]{2,1,0:T(8,128)S(1)} %get-tuple-element.83), channel_id=1, source_target_pairs={{8,16},{16,8},{24,32},{32,24},{40,48},{48,40},{56,64},{64,56},{72,... | collective-permute-start | bytes 1572872 | tf_op jit(solution)/shard_map/ppermute | solution.py:726
  132.3 18.0 %collective-permute-start.14 = (f32[30,32,128]{2,1,0:T(8,128)S(1)}, f32[30,32,128]{2,1,0:T(8,128)S(1)}, u32[]{:S(2)}, u32[]{:S(2)}) collective-permute-start(f32[30,32,128]{2,1,0:T(8,128)S(1)} %get-tuple-element.84), channel_id=1, source_target_pairs={{0,1},{1,0},{2,3},{3,2},{4,5},{5,4},{6,7},{7,6},{8,9},{9,8},{10,11... | collective-permute-start | bytes 1474568 | tf_op jit(solution)/shard_map/ppermute | solution.py:726
  132.4 18.0 %collective-permute-start.15 = (f32[30,32,128]{2,1,0:T(8,128)S(1)}, f32[30,32,128]{2,1,0:T(8,128)S(1)}, u32[]{:S(2)}, u32[]{:S(2)}) collective-permute-start(f32[30,32,128]{2,1,0:T(8,128)S(1)} %get-tuple-element.85), channel_id=1, source_target_pairs={{1,2},{2,1},{3,4},{4,3},{5,6},{6,5},{9,10},{10,9},{11,12},{12,11},... | collective-permute-start | bytes 1474568 | tf_op jit(solution)/shard_map/ppermute | solution.py:726
  148.4 10.1 %collective-permute-start.17 = (f32[30,32,128]{2,1,0:T(8,128)S(1)}, f32[30,32,128]{2,1,0:T(8,128)S(1)}, u32[]{:S(2)}, u32[]{:S(2)}) collective-permute-start(f32[30,32,128]{2,1,0:T(8,128)S(1)} %get-tuple-element.87), channel_id=1, source_target_pairs={{1,2},{2,1},{3,4},{4,3},{5,6},{6,5},{9,10},{10,9},{11,12},{12,11},... | collective-permute-start | bytes 1474568 | tf_op jit(solution)/shard_map/ppermute | solution.py:726
  172.4 2.5 %collective-permute-start.18 = (f32[30,32,128]{2,1,0:T(8,128)S(1)}, f32[30,32,128]{2,1,0:T(8,128)S(1)}, u32[]{:S(2)}, u32[]{:S(2)}) collective-permute-start(f32[30,32,128]{2,1,0:T(8,128)S(1)} %get-tuple-element.93), channel_id=1, source_target_pairs={{0,1},{1,0},{2,3},{3,2},{4,5},{5,4},{6,7},{7,6},{8,9},{9,8},{10,11... | collective-permute-start | bytes 1474568 | tf_op jit(solution)/shard_map/ppermute | solution.py:726
  172.9 10.1 %collective-permute-start.19 = (f32[30,32,128]{2,1,0:T(8,128)S(1)}, f32[30,32,128]{2,1,0:T(8,128)S(1)}, u32[]{:S(2)}, u32[]{:S(2)}) collective-permute-start(f32[30,32,128]{2,1,0:T(8,128)S(1)} %get-tuple-element.94), channel_id=1, source_target_pairs={{1,2},{2,1},{3,4},{4,3},{5,6},{6,5},{9,10},{10,9},{11,12},{12,11},... | collective-permute-start | bytes 1474568 | tf_op jit(solution)/shard_map/ppermute | solution.py:726
  183.9 14.0 %collective-permute-start.22 = (f32[64,16,128]{2,1,0:T(8,128)S(1)}, f32[64,16,128]{2,1,0:T(8,128)S(1)}, u32[]{:S(2)}, u32[]{:S(2)}) collective-permute-start(f32[64,16,128]{2,1,0:T(8,128)S(1)} %get-tuple-element.99), channel_id=1, source_target_pairs={{0,8},{8,0},{16,24},{24,16},{32,40},{40,32},{48,56},{56,48},{64,72... | collective-permute-start | bytes 1572872 | tf_op jit(solution)/shard_map/ppermute | solution.py:726
  184.0 17.9 %collective-permute-start.23 = (f32[64,16,128]{2,1,0:T(8,128)S(1)}, f32[64,16,128]{2,1,0:T(8,128)S(1)}, u32[]{:S(2)}, u32[]{:S(2)}) collective-permute-start(f32[64,16,128]{2,1,0:T(8,128)S(1)} %get-tuple-element.100), channel_id=1, source_target_pairs={{8,16},{16,8},{24,32},{32,24},{40,48},{48,40},{56,64},{64,56},{72,... | collective-permute-start | bytes 1572872 | tf_op jit(solution)/shard_map/ppermute | solution.py:726
  186.0 2.3 %collective-permute-start.20 = (f32[30,32,128]{2,1,0:T(8,128)S(1)}, f32[30,32,128]{2,1,0:T(8,128)S(1)}, u32[]{:S(2)}, u32[]{:S(2)}) collective-permute-start(f32[30,32,128]{2,1,0:T(8,128)S(1)} %get-tuple-element.97), channel_id=1, source_target_pairs={{0,1},{1,0},{2,3},{3,2},{4,5},{5,4},{6,7},{7,6},{8,9},{9,8},{10,11... | collective-permute-start | bytes 1474568 | tf_op jit(solution)/shard_map/ppermute | solution.py:726
  186.2 10.1 %collective-permute-start.21 = (f32[30,32,128]{2,1,0:T(8,128)S(1)}, f32[30,32,128]{2,1,0:T(8,128)S(1)}, u32[]{:S(2)}, u32[]{:S(2)}) collective-permute-start(f32[30,32,128]{2,1,0:T(8,128)S(1)} %get-tuple-element.98), channel_id=1, source_target_pairs={{1,2},{2,1},{3,4},{4,3},{5,6},{6,5},{9,10},{10,9},{11,12},{12,11},... | collective-permute-start | bytes 1474568 | tf_op jit(solution)/shard_map/ppermute | solution.py:726
  (15 other events, 223.5 us)

commit v6 on v5

--- a/solution.py
+++ b/solution.py
@@ -454,36 +454,42 @@
     return jnp.where(plain, even_if_plain, other), jnp.where(plain, other, even_if_plain)
 
 
-def first_body(par, est, colse, colso, cene, ceno):
-    @pl.loop(0, DZ // 4)
-    def _(group):
-        for u in range(4):
-            z = 4 * group + u
-            colse[z], colso[z] = pick(par, est[z, RX:], est[z, :RX])
-
+def pull(pairs, sem):
+    copies = [
+        pltpu.make_async_copy(source, target, sem.at[i])
+        for i, (source, target) in enumerate(pairs)
+    ]
+    for copy in copies:
+        copy.start()
+    for copy in copies:
+        copy.wait()
+
+
+def columns_body(par, est, colse, colso, sem):
+    even = pl.multiple_of(jnp.where(par[0] == 0, RX, 0), RX)
+    odd = pl.multiple_of(RX - even, RX)
+    pull([(est.at[:, pl.ds(even, RX)], colse), (est.at[:, pl.ds(odd, RX)], colso)], sem)
+
+
+def planes_body(par, est, cene, ceno, sem):
     even, odd = starts(par, 0, DZ - RZ)
-
-    @pl.loop(0, RZ // 6)
-    def _(group):
-        for u in range(6):
-            k = 6 * group + u
-            cene[k] = est[even + k]
-            ceno[k] = est[odd + k]
+    pull([(est.at[pl.ds(even, RZ)], cene), (est.at[pl.ds(odd, RZ)], ceno)], sem)
 
 
 COLUMNS = f32(DZ, RX, NY)
 PLANES = f32(RZ, DX, NY)
 
 
-def first_rims(par, est):
+def first(body, name, shape, par, est):
     return pl.pallas_call(
-        first_body,
-        out_shape=(COLUMNS, COLUMNS, PLANES, PLANES),
-        in_specs=[SM, VM],
-        out_specs=[VM] * 4,
+        body,
+        out_shape=(shape, shape),
+        in_specs=[SM, HB],
+        out_specs=[VM] * 2,
+        scratch_shapes=[pltpu.SemaphoreType.DMA((2,))],
         compiler_params=params(16),
-        name="first_rims",
-    )(par, est)
+        name=name,
+    )(par, in_hbm(est))
 
 
 def rims_body(par, midl, midr, side, sido, outl, outr):
@@ -614,7 +620,7 @@
     )(at, labels, kz, kx, yb)
 
 
-def update_body(par, est, weight, midc, cene, ceno, colse, colso, new, *outs):
+def gather_total(par, midc, cene, ceno, colse, colso, new):
     even, odd = starts(par, 0, DZ - RZ)
 
     @pl.loop(0, DZ // 4)
@@ -631,37 +637,74 @@
             for u in range(6):
                 new[start + 6 * group + u] += centre[6 * group + u]
 
+
+def update_body(par, est, weight, midc, cene, ceno, colse, colso, new, *outs):
+    gather_total(par, midc, cene, ceno, colse, colso, new)
+
     @pl.loop(0, DZ // 4)
     def _(group):
         for u in range(4):
             z = 4 * group + u
             value = est[z] * new[z] / weight[z]
             new[z] = value
-            if outs:
-                outs[0][z], outs[1][z] = pick(par, value[RX:], value[:RX])
-
-    if outs:
-
-        @pl.loop(0, RZ // 6)
+            outs[0][z], outs[1][z] = pick(par, value[RX:], value[:RX])
+
+    even, odd = starts(par, 0, DZ - RZ)
+
+    @pl.loop(0, RZ // 6)
+    def _(group):
+        for u in range(6):
+            k = 6 * group + u
+            outs[2][k] = new[even + k]
+            outs[3][k] = new[odd + k]
+
+
+def finish_body(par, est, weight, midc, cene, ceno, colse, colso, out, new, sem):
+    gather_total(par, midc, cene, ceno, colse, colso, new)
+    chunk = 16
+
+    def push(k):
+        part = pl.ds(chunk * k, chunk)
+        return pltpu.make_async_copy(new.at[part], out.at[part], sem.at[k])
+
+    for k in range(DZ // chunk):
+
+        @pl.loop(0, chunk // 4)
         def _(group):
-            for u in range(6):
-                k = 6 * group + u
-                outs[2][k] = new[even + k]
-                outs[3][k] = new[odd + k]
+            for u in range(4):
+                z = chunk * k + 4 * group + u
+                new[z] = est[z] * new[z] / weight[z]
+
+        push(k).start()
+    for k in range(DZ // chunk):
+        push(k).wait()
 
 
 def update(par, est, weight, midc, cene, ceno, colse, colso, last):
-    shapes = [f32(DZ, DX, NY)]
-    if not last:
-        shapes += [COLUMNS, COLUMNS, PLANES, PLANES]
-    return pl.pallas_call(
-        update_body,
-        out_shape=tuple(shapes),
-        in_specs=[SM] + [VM] * 7,
-        out_specs=[VM] * len(shapes),
-        compiler_params=params(16),
-        name="update",
-    )(par, est, weight, midc, cene, ceno, colse, colso)
+    whole = f32(DZ, DX, NY)
+    if last:
+        call = pl.pallas_call(
+            finish_body,
+            out_shape=whole,
+            in_specs=[SM] + [VM] * 7,
+            out_specs=HB,
+            scratch_shapes=[
+                pltpu.VMEM((DZ, DX, NY), jnp.float32),
+                pltpu.SemaphoreType.DMA((DZ // 16,)),
+            ],
+            compiler_params=params(16),
+            name="finish",
+        )
+    else:
+        call = pl.pallas_call(
+            update_body,
+            out_shape=(whole, COLUMNS, COLUMNS, PLANES, PLANES),
+            in_specs=[SM] + [VM] * 7,
+            out_specs=[VM] * 5,
+            compiler_params=params(16),
+            name="update",
+        )
+    return call(par, est, weight, midc, cene, ceno, colse, colso)
 
 
 def band(row, rows, first):
@@ -738,8 +781,8 @@
     held = tile_pair % all_blocks // BLK_DEV
     est = estimate0
     par = jnp.stack([me % 2, lax.axis_index("depth") % 2]).astype(jnp.int32)
-    *columns, cene, ceno = first_rims(par, est)
-    columns = swap(*columns, "blocks")
+    columns = swap(*first(columns_body, "first_columns", COLUMNS, par, est), "blocks")
+    cene, ceno = first(planes_body, "first_planes", PLANES, par, est)
     sent = place(held, tile_pair, tile_shift, tiles, owners)
     sent, *columns = lax.optimization_barrier((sent, *columns))
     got = lax.all_to_all(sent, "blocks", split_axis=0, concat_axis=0, tiled=True)
@@ -775,11 +818,11 @@
         columns = swap(*rims, "blocks")
         cene, ceno = swap(cene, ceno, "depth")
         last = iteration == ITERS - 1
-        est, *rest = update(par, est, weight, midc, cene, ceno, *columns, last)
-        if not last:
-            *columns, cene, ceno = rest
-            columns = swap(*columns, "blocks")
-    return est
+        new = update(par, est, weight, midc, cene, ceno, *columns, last)
+        if last:
+            return new
+        est, *columns, cene, ceno = new
+        columns = swap(*columns, "blocks")
 
 
 def solution(mesh):

time: 203 us -> 203 us (level)
  waiting for transfers between devices: 103 us -> 98.7 us
  Pallas kernels: 52.9 us -> 55.6 us
    all_to_all x1, waiting for transfers between devices: 31.6 us -> 28.8 us  [local(): lax.all_to_all(sent, 'blocks', split_axis=0, concat_axis=0, tiled=True)]
    pallas_call x3 -> x4, Pallas kernels: 5.17 us -> 7.69 us  [the longest x2 4.46 us: first(): pl.pallas_call(body, out_shape=(shape, shape), in_specs=[SM, HB], out_spe...]
    unnamed x28 -> x26, local copies, waits for them, and re-layouts: 6.43 us -> 5.2 us
  transfers between devices with their start and end apart: 25 -> 25, of which waited for: 15 -> 15; matrix products, arithmetic and copies ran while one was open for 1% -> 1% of each run, Pallas kernels for 11% -> 13%
where the time goes in v6:
time: 203 us
  waiting for transfers between devices  98.7 us (49%)
  Pallas kernels  55.6 us (27%)
  starting transfers between devices  40.4 us (20%)
  local copies, waits for them, and re-layouts  5.31 us (3%)
  other arithmetic  2.4 us (1%)
    ppermute x24, waiting for transfers between devices, swap(): out.append(lax.ppermute(value, axis, pairs))  69.9 us
    ppermute x24, starting transfers between devices, swap(): out.append(lax.ppermute(value, axis, pairs))  33.5 us
    all_to_all x1, waiting for transfers between devices, local(): lax.all_to_all(sent, 'blocks', split_axis=0, concat_axis=0, tiled=True)  28.8 us
    pallas_call x1, Pallas kernels, sweep(): pl.pallas_call(functools.partial(sweep_body, slots), out_shape=PIECES, in...  13.8 us
    pallas_call x1, Pallas kernels, blur_all(): pl.pallas_call(blur_body, out_shape=pltpu.HBM((cells, BX * DZ, NY), jnp.f...  12.4 us
    pallas_call x1, Pallas kernels, spread_ratio(): pl.pallas_call(functools.partial(spread_body, slots), out_shape=PIECES, i...  9.13 us
    all_to_all x1, starting transfers between devices, local(): lax.all_to_all(sent, 'blocks', split_axis=0, concat_axis=0, tiled=True)  6.89 us
    unnamed x26, local copies, waits for them, and re-layouts  5.2 us
  transfers between devices with their start and end apart: 25, of which 15 were waited for; matrix products, arithmetic and copies ran while one was open for 1% of the time, Pallas kernels for 13%

profile of v6, /device:TPU:34, one launch (start us, length us, event | category | flops | bytes accessed | tf_op | source)
XLA Modules:
  0.0 203.0 jit_solution(9992243042047579997)
XLA Ops:
  3.5 3.6 %collective-permute-start.1 = (f32[64,16,128]{2,1,0:T(8,128)S(1)}, f32[64,16,128]{2,1,0:T(8,128)S(1)}, u32[]{:S(2)}, u32[]{:S(2)}) collective-permute-start(f32[64,16,128]{2,1,0:T(8,128)S(1)} %get-tuple-element.54), channel_id=1, source_target_pairs={{8,16},{16,8},{24,32},{32,24},{40,48},{48,40},{56,64},{64,56},{72,... | collective-permute-start | bytes 1572872 | tf_op jit(solution)/shard_map/ppermute | solution.py:769
  15.6 5.3 %collective-permute-done.1.colso = f32[64,16,128]{2,1,0:T(8,128)S(1)} collective-permute-done((f32[64,16,128]{2,1,0:T(8,128)S(1)}, f32[64,16,128]{2,1,0:T(8,128)S(1)}, u32[]{:S(2)}, u32[]{:S(2)}) %collective-permute-start.1) | collective-permute-done | bytes 524320 | tf_op jit(solution)/shard_map/ppermute | solution.py:769
  20.9 6.9 %all-to-all-start = ((f32[16,520,128]{2,1,0:T(8,128)}), f32[16,520,128]{2,1,0:T(8,128)}, u32[]{:S(2)}, u32[]{:S(2)}) async-start(f32[16,520,128]{2,1,0:T(8,128)} %place.1), calls=%async_computation | async-start | bytes 8519680 | tf_op jit(solution)/shard_map/all_to_all | solution.py:788
  27.8 2.7 %first_planes.1 = (f32[30,32,128]{2,1,0:T(8,128)}, f32[30,32,128]{2,1,0:T(8,128)}) custom-call(s32[2]{0:T(128)S(1)} %pad_add_fusion.par, f32[64,32,128]{2,1,0:T(8,128)} %est.7), custom_call_target="tpu_custom_call" | custom-call | tf_op jit(solution)/shard_map/first_planes/pallas_call | solution.py:484
  30.6 2.5 %collective-permute-start.3 = (f32[30,32,128]{2,1,0:T(8,128)}, f32[30,32,128]{2,1,0:T(8,128)}, u32[]{:S(2)}, u32[]{:S(2)}) collective-permute-start(f32[30,32,128]{2,1,0:T(8,128)} %get-tuple-element.60), channel_id=1, source_target_pairs={{1,2},{2,1},{3,4},{4,3},{5,6},{6,5},{9,10},{10,9},{11,12},{12,11},... | collective-permute-start | bytes 1474568 | tf_op jit(solution)/shard_map/ppermute | solution.py:769
  42.0 4.3 %collective-permute-done.5.sido = f32[30,32,128]{2,1,0:T(8,128)} collective-permute-done((f32[30,32,128]{2,1,0:T(8,128)}, f32[30,32,128]{2,1,0:T(8,128)}, u32[]{:S(2)}, u32[]{:S(2)}) %collective-permute-start.5) | collective-permute-done | bytes 491552 | tf_op jit(solution)/shard_map/ppermute | solution.py:769
  46.3 12.4 %blur_all.1.blurred = f32[24,512,128]{2,1,0:T(8,128)} custom-call(s32[2]{0:T(128)S(1)} %pad_add_fusion.par, f32[64,32,128]{2,1,0:T(8,128)S(1)} %copy-done, f32[64,16,128]{2,1,0:T(8,128)S(1)} %collective-permute-done.colse, f32[64,16,128]{2,1,0:T(8,128)S(1)} %collective-permute-done.1.colso, f32[30,32,128]{2,1,0:T(8,128)} %collective-permute-done.2.cene, ...), custom_call_target="tpu_custom_call" | custom-call | tf_op jit(solution)/shard_map/blur_all/pallas_call | solution.py:368
  58.8 28.8 %all-to-all-done.got = f32[16,520,128]{2,1,0:T(8,128)} async-done(((f32[16,520,128]{2,1,0:T(8,128)}), f32[16,520,128]{2,1,0:T(8,128)}, u32[]{:S(2)}, u32[]{:S(2)}) %all-to-all-start) | async-done | bytes 4259872 | tf_op jit(solution)/shard_map/all_to_all | solution.py:788
  88.6 9.1 %spread_ratio.1 = (f32[64,32,128]{2,1,0:T(8,128)S(1)}, f32[64,16,128]{2,1,0:T(8,128)S(1)}, f32[64,16,128]{2,1,0:T(8,128)S(1)}, f32[30,32,128]{2,1,0:T(8,128)S(1)...) custom-call(s32[2]{0:T(128)S(1)} %pad_add_fusion.par, ...), custom_call_target="tpu_custom_call" | custom-call | tf_op jit(solution)/shard_map/spread_ratio/pallas_call | solution.py:386
  97.8 2.5 %collective-permute-start.7 = (f32[30,32,128]{2,1,0:T(8,128)S(1)}, f32[30,32,128]{2,1,0:T(8,128)S(1)}, u32[]{:S(2)}, u32[]{:S(2)}) collective-permute-start(f32[30,32,128]{2,1,0:T(8,128)S(1)} %get-tuple-element.74), channel_id=1, source_target_pairs={{1,2},{2,1},{3,4},{4,3},{5,6},{6,5},{9,10},{10,9},{11,12},{12,11},... | collective-permute-start | bytes 1474568 | tf_op jit(solution)/shard_map/ppermute | solution.py:769
  100.4 7.6 %collective-permute-done.7.sido = f32[30,32,128]{2,1,0:T(8,128)S(1)} collective-permute-done((f32[30,32,128]{2,1,0:T(8,128)S(1)}, f32[30,32,128]{2,1,0:T(8,128)S(1)}, u32[]{:S(2)}, u32[]{:S(2)}) %collective-permute-start.7) | collective-permute-done | bytes 491552 | tf_op jit(solution)/shard_map/ppermute | solution.py:769
  109.0 2.9 %collective-permute-start.11 = (f32[64,16,128]{2,1,0:T(8,128)S(1)}, f32[64,16,128]{2,1,0:T(8,128)S(1)}, u32[]{:S(2)}, u32[]{:S(2)}) collective-permute-start(f32[64,16,128]{2,1,0:T(8,128)S(1)} %get-tuple-element.80), channel_id=1, source_target_pairs={{8,16},{16,8},{24,32},{32,24},{40,48},{48,40},{56,64},{64,56},{72,... | collective-permute-start | bytes 1572872 | tf_op jit(solution)/shard_map/ppermute | solution.py:769
  114.6 4.8 %weigh.1.weight = f32[64,32,128]{2,1,0:T(8,128)S(1)} custom-call(s32[2]{0:T(128)S(1)} %pad_add_fusion.1.at, s32[16,16]{1,0:T(8,128)S(1)} %bitcast.6, f32[8,128]{1,0:T(8,128)S(1)} %pad.12.kz, f32[8,128]{1,0:T(8,128)S(1)} %pad.13.kx, bf16[6,256,256]{2,1,0:T(8,128)(2,1)S(1)} %copy-done.2), custom_call_target="tpu_custom_call" | custom-call | tf_op jit(solution)/shard_map/weigh/pallas_call | solution.py:608
  119.5 2.8 %collective-permute-done.9.ceno = f32[30,32,128]{2,1,0:T(8,128)S(1)} collective-permute-done((f32[30,32,128]{2,1,0:T(8,128)S(1)}, f32[30,32,128]{2,1,0:T(8,128)S(1)}, u32[]{:S(2)}, u32[]{:S(2)}) %collective-permute-start.9) | collective-permute-done | bytes 491552 | tf_op jit(solution)/shard_map/ppermute | solution.py:769
  123.3 4.1 %collective-permute-done.11.colso = f32[64,16,128]{2,1,0:T(8,128)S(1)} collective-permute-done((f32[64,16,128]{2,1,0:T(8,128)S(1)}, f32[64,16,128]{2,1,0:T(8,128)S(1)}, u32[]{:S(2)}, u32[]{:S(2)}) %collective-permute-start.11) | collective-permute-done | bytes 524320 | tf_op jit(solution)/shard_map/ppermute | solution.py:769
  129.0 2.8 %collective-permute-start.13 = (f32[64,16,128]{2,1,0:T(8,128)S(1)}, f32[64,16,128]{2,1,0:T(8,128)S(1)}, u32[]{:S(2)}, u32[]{:S(2)}) collective-permute-start(f32[64,16,128]{2,1,0:T(8,128)S(1)} %get-tuple-element.83), channel_id=1, source_target_pairs={{8,16},{16,8},{24,32},{32,24},{40,48},{48,40},{56,64},{64,56},{72,... | collective-permute-start | bytes 1572872 | tf_op jit(solution)/shard_map/ppermute | solution.py:769
  133.8 8.7 %collective-permute-done.12.colse = f32[64,16,128]{2,1,0:T(8,128)S(1)} collective-permute-done((f32[64,16,128]{2,1,0:T(8,128)S(1)}, f32[64,16,128]{2,1,0:T(8,128)S(1)}, u32[]{:S(2)}, u32[]{:S(2)}) %collective-permute-start.12) | collective-permute-done | bytes 524320 | tf_op jit(solution)/shard_map/ppermute | solution.py:769
  142.5 4.0 %collective-permute-done.13.colso = f32[64,16,128]{2,1,0:T(8,128)S(1)} collective-permute-done((f32[64,16,128]{2,1,0:T(8,128)S(1)}, f32[64,16,128]{2,1,0:T(8,128)S(1)}, u32[]{:S(2)}, u32[]{:S(2)}) %collective-permute-start.13) | collective-permute-done | bytes 524320 | tf_op jit(solution)/shard_map/ppermute | solution.py:769
  149.3 8.2 %collective-permute-done.17.sido = f32[30,32,128]{2,1,0:T(8,128)S(1)} collective-permute-done((f32[30,32,128]{2,1,0:T(8,128)S(1)}, f32[30,32,128]{2,1,0:T(8,128)S(1)}, u32[]{:S(2)}, u32[]{:S(2)}) %collective-permute-start.17) | collective-permute-done | bytes 491552 | tf_op jit(solution)/shard_map/ppermute | solution.py:769
  157.5 13.8 %sweep.1 = (f32[64,32,128]{2,1,0:T(8,128)S(1)}, f32[64,16,128]{2,1,0:T(8,128)S(1)}, f32[64,16,128]{2,1,0:T(8,128)S(1)}, f32[30,32,128]{2,1,0:T(8,128)S(1)}, f32[...) custom-call(s32[2]{0:T(128)S(1)} %pad_add_fusion.par, s32[51]{0:T(128)S(1)} %concatenate.3.meta, ...), custom_call_target="tpu_custom_call" | custom-call | tf_op jit(solution)/shard_map/sweep/pallas_call | solution.py:350
  173.7 8.2 %collective-permute-done.19.sido = f32[30,32,128]{2,1,0:T(8,128)S(1)} collective-permute-done((f32[30,32,128]{2,1,0:T(8,128)S(1)}, f32[30,32,128]{2,1,0:T(8,128)S(1)}, u32[]{:S(2)}, u32[]{:S(2)}) %collective-permute-start.19) | collective-permute-done | bytes 491552 | tf_op jit(solution)/shard_map/ppermute | solution.py:769
  182.9 2.8 %collective-permute-start.23 = (f32[64,16,128]{2,1,0:T(8,128)S(1)}, f32[64,16,128]{2,1,0:T(8,128)S(1)}, u32[]{:S(2)}, u32[]{:S(2)}) collective-permute-start(f32[64,16,128]{2,1,0:T(8,128)S(1)} %get-tuple-element.100), channel_id=1, source_target_pairs={{8,16},{16,8},{24,32},{32,24},{40,48},{48,40},{56,64},{64,56},{72,... | collective-permute-start | bytes 1572872 | tf_op jit(solution)/shard_map/ppermute | solution.py:769
  187.7 8.2 %collective-permute-done.21.ceno = f32[30,32,128]{2,1,0:T(8,128)S(1)} collective-permute-done((f32[30,32,128]{2,1,0:T(8,128)S(1)}, f32[30,32,128]{2,1,0:T(8,128)S(1)}, u32[]{:S(2)}, u32[]{:S(2)}) %collective-permute-start.21) | collective-permute-done | bytes 491552 | tf_op jit(solution)/shard_map/ppermute | solution.py:769
  196.8 4.0 %collective-permute-done.23.colso = f32[64,16,128]{2,1,0:T(8,128)S(1)} collective-permute-done((f32[64,16,128]{2,1,0:T(8,128)S(1)}, f32[64,16,128]{2,1,0:T(8,128)S(1)}, u32[]{:S(2)}, u32[]{:S(2)}) %collective-permute-start.23) | collective-permute-done | bytes 524320 | tf_op jit(solution)/shard_map/ppermute | solution.py:769
  (82 shorter events, 41.3 us)
Async XLA Ops:
  1.8 13.7 %collective-permute-start = (f32[64,16,128]{2,1,0:T(8,128)S(1)}, f32[64,16,128]{2,1,0:T(8,128)S(1)}, u32[]{:S(2)}, u32[]{:S(2)}) collective-permute-start(f32[64,16,128]{2,1,0:T(8,128)S(1)} %get-tuple-element.53), channel_id=1, source_target_pairs={{0,8},{8,0},{16,24},{24,16},{32,40},{40,32},{48,56},{56,48},{64,72... | collective-permute-start | bytes 1572872 | tf_op jit(solution)/shard_map/ppermute | solution.py:769
  3.5 17.4 %collective-permute-start.1 = (f32[64,16,128]{2,1,0:T(8,128)S(1)}, f32[64,16,128]{2,1,0:T(8,128)S(1)}, u32[]{:S(2)}, u32[]{:S(2)}) collective-permute-start(f32[64,16,128]{2,1,0:T(8,128)S(1)} %get-tuple-element.54), channel_id=1, source_target_pairs={{8,16},{16,8},{24,32},{32,24},{40,48},{48,40},{56,64},{64,56},{72,... | collective-permute-start | bytes 1572872 | tf_op jit(solution)/shard_map/ppermute | solution.py:769
  20.9 66.7 %all-to-all-start = ((f32[16,520,128]{2,1,0:T(8,128)}), f32[16,520,128]{2,1,0:T(8,128)}, u32[]{:S(2)}, u32[]{:S(2)}) async-start(f32[16,520,128]{2,1,0:T(8,128)} %place.1), calls=%async_computation | async-start | bytes 8519680 | tf_op jit(solution)/shard_map/all_to_all | solution.py:788
  30.5 11.5 %collective-permute-start.2 = (f32[30,32,128]{2,1,0:T(8,128)}, f32[30,32,128]{2,1,0:T(8,128)}, u32[]{:S(2)}, u32[]{:S(2)}) collective-permute-start(f32[30,32,128]{2,1,0:T(8,128)} %get-tuple-element.59), channel_id=1, source_target_pairs={{0,1},{1,0},{2,3},{3,2},{4,5},{5,4},{6,7},{7,6},{8,9},{9,8},{10,11... | collective-permute-start | bytes 1474568 | tf_op jit(solution)/shard_map/ppermute | solution.py:769
  30.6 11.5 %collective-permute-start.3 = (f32[30,32,128]{2,1,0:T(8,128)}, f32[30,32,128]{2,1,0:T(8,128)}, u32[]{:S(2)}, u32[]{:S(2)}) collective-permute-start(f32[30,32,128]{2,1,0:T(8,128)} %get-tuple-element.60), channel_id=1, source_target_pairs={{1,2},{2,1},{3,4},{4,3},{5,6},{6,5},{9,10},{10,9},{11,12},{12,11},... | collective-permute-start | bytes 1474568 | tf_op jit(solution)/shard_map/ppermute | solution.py:769
  34.9 7.2 %collective-permute-start.4 = (f32[30,32,128]{2,1,0:T(8,128)}, f32[30,32,128]{2,1,0:T(8,128)}, u32[]{:S(2)}, u32[]{:S(2)}) collective-permute-start(f32[30,32,128]{2,1,0:T(8,128)} %get-tuple-element.61), channel_id=1, source_target_pairs={{0,1},{1,0},{2,3},{3,2},{4,5},{5,4},{6,7},{7,6},{8,9},{9,8},{10,11... | collective-permute-start | bytes 1474568 | tf_op jit(solution)/shard_map/ppermute | solution.py:769
  35.8 10.5 %collective-permute-start.5 = (f32[30,32,128]{2,1,0:T(8,128)}, f32[30,32,128]{2,1,0:T(8,128)}, u32[]{:S(2)}, u32[]{:S(2)}) collective-permute-start(f32[30,32,128]{2,1,0:T(8,128)} %get-tuple-element.62), channel_id=1, source_target_pairs={{1,2},{2,1},{3,4},{4,3},{5,6},{6,5},{9,10},{10,9},{11,12},{12,11},... | collective-permute-start | bytes 1474568 | tf_op jit(solution)/shard_map/ppermute | solution.py:769
  97.8 2.6 %collective-permute-start.6 = (f32[30,32,128]{2,1,0:T(8,128)S(1)}, f32[30,32,128]{2,1,0:T(8,128)S(1)}, u32[]{:S(2)}, u32[]{:S(2)}) collective-permute-start(f32[30,32,128]{2,1,0:T(8,128)S(1)} %get-tuple-element.73), channel_id=1, source_target_pairs={{0,1},{1,0},{2,3},{3,2},{4,5},{5,4},{6,7},{7,6},{8,9},{9,8},{10,11... | collective-permute-start | bytes 1474568 | tf_op jit(solution)/shard_map/ppermute | solution.py:769
  97.8 10.1 %collective-permute-start.7 = (f32[30,32,128]{2,1,0:T(8,128)S(1)}, f32[30,32,128]{2,1,0:T(8,128)S(1)}, u32[]{:S(2)}, u32[]{:S(2)}) collective-permute-start(f32[30,32,128]{2,1,0:T(8,128)S(1)} %get-tuple-element.74), channel_id=1, source_target_pairs={{1,2},{2,1},{3,4},{4,3},{5,6},{6,5},{9,10},{10,9},{11,12},{12,11},... | collective-permute-start | bytes 1474568 | tf_op jit(solution)/shard_map/ppermute | solution.py:769
  108.9 14.4 %collective-permute-start.10 = (f32[64,16,128]{2,1,0:T(8,128)S(1)}, f32[64,16,128]{2,1,0:T(8,128)S(1)}, u32[]{:S(2)}, u32[]{:S(2)}) collective-permute-start(f32[64,16,128]{2,1,0:T(8,128)S(1)} %get-tuple-element.79), channel_id=1, source_target_pairs={{0,8},{8,0},{16,24},{24,16},{32,40},{40,32},{48,56},{56,48},{64,72... | collective-permute-start | bytes 1572872 | tf_op jit(solution)/shard_map/ppermute | solution.py:769
  109.0 18.4 %collective-permute-start.11 = (f32[64,16,128]{2,1,0:T(8,128)S(1)}, f32[64,16,128]{2,1,0:T(8,128)S(1)}, u32[]{:S(2)}, u32[]{:S(2)}) collective-permute-start(f32[64,16,128]{2,1,0:T(8,128)S(1)} %get-tuple-element.80), channel_id=1, source_target_pairs={{8,16},{16,8},{24,32},{32,24},{40,48},{48,40},{56,64},{64,56},{72,... | collective-permute-start | bytes 1572872 | tf_op jit(solution)/shard_map/ppermute | solution.py:769
  111.9 7.6 %collective-permute-start.8 = (f32[30,32,128]{2,1,0:T(8,128)S(1)}, f32[30,32,128]{2,1,0:T(8,128)S(1)}, u32[]{:S(2)}, u32[]{:S(2)}) collective-permute-start(f32[30,32,128]{2,1,0:T(8,128)S(1)} %get-tuple-element.77), channel_id=1, source_target_pairs={{0,1},{1,0},{2,3},{3,2},{4,5},{5,4},{6,7},{7,6},{8,9},{9,8},{10,11... | collective-permute-start | bytes 1474568 | tf_op jit(solution)/shard_map/ppermute | solution.py:769
  112.2 10.1 %collective-permute-start.9 = (f32[30,32,128]{2,1,0:T(8,128)S(1)}, f32[30,32,128]{2,1,0:T(8,128)S(1)}, u32[]{:S(2)}, u32[]{:S(2)}) collective-permute-start(f32[30,32,128]{2,1,0:T(8,128)S(1)} %get-tuple-element.78), channel_id=1, source_target_pairs={{1,2},{2,1},{3,4},{4,3},{5,6},{6,5},{9,10},{10,9},{11,12},{12,11},... | collective-permute-start | bytes 1474568 | tf_op jit(solution)/shard_map/ppermute | solution.py:769
  128.7 13.8 %collective-permute-start.12 = (f32[64,16,128]{2,1,0:T(8,128)S(1)}, f32[64,16,128]{2,1,0:T(8,128)S(1)}, u32[]{:S(2)}, u32[]{:S(2)}) collective-permute-start(f32[64,16,128]{2,1,0:T(8,128)S(1)} %get-tuple-element.82), channel_id=1, source_target_pairs={{0,8},{8,0},{16,24},{24,16},{32,40},{40,32},{48,56},{56,48},{64,72... | collective-permute-start | bytes 1572872 | tf_op jit(solution)/shard_map/ppermute | solution.py:769
  129.0 17.5 %collective-permute-start.13 = (f32[64,16,128]{2,1,0:T(8,128)S(1)}, f32[64,16,128]{2,1,0:T(8,128)S(1)}, u32[]{:S(2)}, u32[]{:S(2)}) collective-permute-start(f32[64,16,128]{2,1,0:T(8,128)S(1)} %get-tuple-element.83), channel_id=1, source_target_pairs={{8,16},{16,8},{24,32},{32,24},{40,48},{48,40},{56,64},{64,56},{72,... | collective-permute-start | bytes 1572872 | tf_op jit(solution)/shard_map/ppermute | solution.py:769
  131.8 17.5 %collective-permute-start.14 = (f32[30,32,128]{2,1,0:T(8,128)S(1)}, f32[30,32,128]{2,1,0:T(8,128)S(1)}, u32[]{:S(2)}, u32[]{:S(2)}) collective-permute-start(f32[30,32,128]{2,1,0:T(8,128)S(1)} %get-tuple-element.84), channel_id=1, source_target_pairs={{0,1},{1,0},{2,3},{3,2},{4,5},{5,4},{6,7},{7,6},{8,9},{9,8},{10,11... | collective-permute-start | bytes 1474568 | tf_op jit(solution)/shard_map/ppermute | solution.py:769
  131.8 17.4 %collective-permute-start.15 = (f32[30,32,128]{2,1,0:T(8,128)S(1)}, f32[30,32,128]{2,1,0:T(8,128)S(1)}, u32[]{:S(2)}, u32[]{:S(2)}) collective-permute-start(f32[30,32,128]{2,1,0:T(8,128)S(1)} %get-tuple-element.85), channel_id=1, source_target_pairs={{1,2},{2,1},{3,4},{4,3},{5,6},{6,5},{9,10},{10,9},{11,12},{12,11},... | collective-permute-start | bytes 1474568 | tf_op jit(solution)/shard_map/ppermute | solution.py:769
  147.2 2.0 %collective-permute-start.16 = (f32[30,32,128]{2,1,0:T(8,128)S(1)}, f32[30,32,128]{2,1,0:T(8,128)S(1)}, u32[]{:S(2)}, u32[]{:S(2)}) collective-permute-start(f32[30,32,128]{2,1,0:T(8,128)S(1)} %get-tuple-element.86), channel_id=1, source_target_pairs={{0,1},{1,0},{2,3},{3,2},{4,5},{5,4},{6,7},{7,6},{8,9},{9,8},{10,11... | collective-permute-start | bytes 1474568 | tf_op jit(solution)/shard_map/ppermute | solution.py:769
  147.3 10.1 %collective-permute-start.17 = (f32[30,32,128]{2,1,0:T(8,128)S(1)}, f32[30,32,128]{2,1,0:T(8,128)S(1)}, u32[]{:S(2)}, u32[]{:S(2)}) collective-permute-start(f32[30,32,128]{2,1,0:T(8,128)S(1)} %get-tuple-element.87), channel_id=1, source_target_pairs={{1,2},{2,1},{3,4},{4,3},{5,6},{6,5},{9,10},{10,9},{11,12},{12,11},... | collective-permute-start | bytes 1474568 | tf_op jit(solution)/shard_map/ppermute | solution.py:769
  171.2 2.5 %collective-permute-start.18 = (f32[30,32,128]{2,1,0:T(8,128)S(1)}, f32[30,32,128]{2,1,0:T(8,128)S(1)}, u32[]{:S(2)}, u32[]{:S(2)}) collective-permute-start(f32[30,32,128]{2,1,0:T(8,128)S(1)} %get-tuple-element.93), channel_id=1, source_target_pairs={{0,1},{1,0},{2,3},{3,2},{4,5},{5,4},{6,7},{7,6},{8,9},{9,8},{10,11... | collective-permute-start | bytes 1474568 | tf_op jit(solution)/shard_map/ppermute | solution.py:769
  171.8 10.1 %collective-permute-start.19 = (f32[30,32,128]{2,1,0:T(8,128)S(1)}, f32[30,32,128]{2,1,0:T(8,128)S(1)}, u32[]{:S(2)}, u32[]{:S(2)}) collective-permute-start(f32[30,32,128]{2,1,0:T(8,128)S(1)} %get-tuple-element.94), channel_id=1, source_target_pairs={{1,2},{2,1},{3,4},{4,3},{5,6},{6,5},{9,10},{10,9},{11,12},{12,11},... | collective-permute-start | bytes 1474568 | tf_op jit(solution)/shard_map/ppermute | solution.py:769
  182.8 14.0 %collective-permute-start.22 = (f32[64,16,128]{2,1,0:T(8,128)S(1)}, f32[64,16,128]{2,1,0:T(8,128)S(1)}, u32[]{:S(2)}, u32[]{:S(2)}) collective-permute-start(f32[64,16,128]{2,1,0:T(8,128)S(1)} %get-tuple-element.99), channel_id=1, source_target_pairs={{0,8},{8,0},{16,24},{24,16},{32,40},{40,32},{48,56},{56,48},{64,72... | collective-permute-start | bytes 1572872 | tf_op jit(solution)/shard_map/ppermute | solution.py:769
  182.9 17.9 %collective-permute-start.23 = (f32[64,16,128]{2,1,0:T(8,128)S(1)}, f32[64,16,128]{2,1,0:T(8,128)S(1)}, u32[]{:S(2)}, u32[]{:S(2)}) collective-permute-start(f32[64,16,128]{2,1,0:T(8,128)S(1)} %get-tuple-element.100), channel_id=1, source_target_pairs={{8,16},{16,8},{24,32},{32,24},{40,48},{48,40},{56,64},{64,56},{72,... | collective-permute-start | bytes 1572872 | tf_op jit(solution)/shard_map/ppermute | solution.py:769
  185.8 10.1 %collective-permute-start.21 = (f32[30,32,128]{2,1,0:T(8,128)S(1)}, f32[30,32,128]{2,1,0:T(8,128)S(1)}, u32[]{:S(2)}, u32[]{:S(2)}) collective-permute-start(f32[30,32,128]{2,1,0:T(8,128)S(1)} %get-tuple-element.98), channel_id=1, source_target_pairs={{1,2},{2,1},{3,4},{4,3},{5,6},{6,5},{9,10},{10,9},{11,12},{12,11},... | collective-permute-start | bytes 1474568 | tf_op jit(solution)/shard_map/ppermute | solution.py:769
  (14 other events, 233.8 us)

commit v7 on v6

--- a/solution.py
+++ b/solution.py
@@ -122,19 +122,20 @@
     return jnp.swapaxes(jnp.stack(parts, axis=0), 0, 1)
 
 
-def backward_x(par, s_ref, xb_ref, midc, midl, midr, cene, ceno, side, sido):
-    def spread_pair(base):
-        both = jnp.concatenate([s_ref[base], s_ref[base + 1]], axis=1)
-        high, low = split(both)
-        out = mul(xb_ref[...], jnp.concatenate([high, low], axis=0))
-        return halves(out[:EX] + out[EX:])
-
+def spread_pair(s_ref, xb_ref, base):
+    both = jnp.concatenate([s_ref[base], s_ref[base + 1]], axis=1)
+    high, low = split(both)
+    out = mul(xb_ref[...], jnp.concatenate([high, low], axis=0))
+    return halves(out[:EX] + out[EX:])
+
+
+def backward_rims(par, s_ref, xb_ref, cene, ceno, side, sido):
     def rim(centre, sides, start):
         @pl.loop(0, RZ // 30)
         def _(group):
             for u in range(15):
                 at = 30 * group + 2 * u
-                for i, plane in enumerate(spread_pair(start + at)):
+                for i, plane in enumerate(spread_pair(s_ref, xb_ref, start + at)):
                     sides[at + i] = jnp.concatenate([plane[:RX], plane[RX + DX :]], axis=0)
                     centre[at + i] = plane[RX : RX + DX]
 
@@ -142,11 +143,13 @@
     rim(cene, side, even)
     rim(ceno, sido, odd)
 
+
+def middle_body(s_ref, xb_ref, midc, midl, midr):
     @pl.loop(0, DZ // 64)
     def _(group):
         for u in range(32):
             at = 64 * group + 2 * u
-            for i, plane in enumerate(spread_pair(PZ + at)):
+            for i, plane in enumerate(spread_pair(s_ref, xb_ref, PZ + at)):
                 midl[at + i] = plane[:RX]
                 midc[at + i] = plane[RX : RX + DX]
                 midr[at + i] = plane[RX + DX :]
@@ -242,8 +245,7 @@
 
 
 def sweep_body(slots, par, meta, est, colse, colso, cene, ceno, side, sido, got, fx, zf, zb, yf,
-               yb, omidc, omidl, omidr, ocene, oceno, oside, osido, s_ref, order, data, sem, picked,
-               xb, xf, held):
+               yb, ocene, oceno, oside, osido, s_ref, xb, order, data, sem, picked, xf, held):
     count, arrive = fetches(slots, meta, order, [data_move(got, data, sem)])
     gather_x(slots, meta, order, count, fx, picked, xf, xb)
     forward_x(par, s_ref, xf, est, colse, colso, cene, ceno, side, sido)
@@ -255,7 +257,7 @@
 
     visit_tiles(4, slots, meta, order, count, arrive, s_ref, data, zb, yb, predict)
     clear_rest(slots, count, s_ref)
-    backward_x(par, s_ref, xb, omidc, omidl, omidr, ocene, oceno, oside, osido)
+    backward_rims(par, s_ref, xb, ocene, oceno, oside, osido)
 
 
 def blur_body(par, est, colse, colso, cene, ceno, side, sido, xf, zf, yf, out, s_ref, staged, sem):
@@ -280,8 +282,7 @@
 
 
 def spread_body(slots, par, meta, blurred, got, far_fx, far_zb, far_yb,
-                omidc, omidl, omidr, ocene, oceno, oside, osido, s_ref, order, data, sem, picked,
-                xb, held, held_sem, fx, zb, yb, table_sem):
+                ocene, oceno, oside, osido, s_ref, xb, order, data, sem, picked, held, held_sem, fx, zb, yb, table_sem):
     tables = [
         pltpu.make_async_copy(far, close, table_sem.at[i])
         for i, (far, close) in enumerate(((far_fx, fx), (far_zb, zb), (far_yb, yb)))
@@ -302,7 +303,7 @@
 
     visit_tiles(4, slots, meta, order, count, arrive, s_ref, data, zb, yb, predict)
     clear_rest(slots, count, s_ref)
-    backward_x(par, s_ref, xb, omidc, omidl, omidr, ocene, oceno, oside, osido)
+    backward_rims(par, s_ref, xb, ocene, oceno, oside, osido)
 
 
 def f32(*shape):
@@ -329,12 +330,10 @@
 def visit_scratch(slots):
     rows = slots * BX
     return [
-        pltpu.VMEM((EZ, rows, NY), jnp.float32),
         pltpu.SMEM((slots + 1,), jnp.int32),
         pltpu.VMEM((slots + 1, BX * DZ, NY), jnp.float32),
         pltpu.SemaphoreType.DMA((slots + 1,)),
         pltpu.VMEM((rows, NY), jnp.float32),
-        pltpu.VMEM((2 * EX, 2 * rows), jnp.bfloat16),
     ]
 
 
@@ -345,19 +344,38 @@
     return pltpu.with_memory_space_constraint(value, pltpu.HBM)
 
 
+def spread_shapes(slots):
+    rows = slots * BX
+    return PIECES[3:] + (
+        pltpu.VMEM((EZ, rows, NY), jnp.float32),
+        pltpu.VMEM((2 * EX, 2 * rows), jnp.bfloat16),
+    )
+
+
+def middle(field, table):
+    return pl.pallas_call(
+        middle_body,
+        out_shape=(PIECES[0], PIECES[1], PIECES[2]),
+        in_specs=[VM] * 2,
+        out_specs=[VM] * 3,
+        compiler_params=params(16),
+        name="middle",
+    )(field, table)
+
+
 def sweep(par, meta, pieces, got, tables):
     slots = got.shape[0]
     return pl.pallas_call(
         functools.partial(sweep_body, slots),
-        out_shape=PIECES,
+        out_shape=spread_shapes(slots),
         in_specs=[SM] * 2 + [VM] * 7 + [HB] + [VM] * 5,
-        out_specs=[VM] * 7,
+        out_specs=[VM] * 6,
         scratch_shapes=visit_scratch(slots)
         + [
             pltpu.VMEM((slots * BX, 3 * EX), jnp.bfloat16),
             pltpu.VMEM((slots + 1, BX * DZ, NY), jnp.float32),
         ],
-        compiler_params=params(36),
+        compiler_params=params(28),
         name="sweep",
     )(par, meta, *pieces, in_hbm(got), *tables[1:])
 
@@ -385,9 +403,9 @@
     xf, fx, zf, zb, yf, yb = tables
     return pl.pallas_call(
         functools.partial(spread_body, slots),
-        out_shape=PIECES,
+        out_shape=spread_shapes(slots),
         in_specs=[SM] * 2 + [HB] * 5,
-        out_specs=[VM] * 7,
+        out_specs=[VM] * 6,
         scratch_shapes=visit_scratch(slots)
         + [
             pltpu.VMEM((slots + 1, BX * DZ, NY), jnp.float32),
@@ -395,7 +413,7 @@
         ]
         + [pltpu.VMEM(table.shape, table.dtype) for table in (fx, zb, yb)]
         + [pltpu.SemaphoreType.DMA((3,))],
-        compiler_params=params(36),
+        compiler_params=params(28),
         name="spread_ratio",
     )(par, meta, *[in_hbm(value) for value in (blurred, got, fx, zb, yb)])
 
@@ -811,8 +829,9 @@
             spread = spread_ratio(par, meta, blur_all(par, pieces, tables), got, tables)
         else:
             spread = sweep(par, meta, pieces, got, tables)
-        midc, midl, midr, cene, ceno, side, sido = spread
+        cene, ceno, side, sido, field, table = spread
         side, sido = swap(side, sido, "depth")
+        midc, midl, midr = middle(field, table)
         rims = fold_rims(par, midl, midr, side, sido)
         cene, ceno, *rims = lax.optimization_barrier((cene, ceno, *rims))
         columns = swap(*rims, "blocks")

time: 203 us -> 201 us (level)
    pallas_call x2 -> x4, Pallas kernels: 22.9 us -> 23.5 us  [the longest x1 13.3 us: sweep(): pl.pallas_call(functools.partial(sweep_body, slots), out_shape=spread_sha...]
  transfers between devices with their start and end apart: 25 -> 25, of which waited for: 15 -> 15; matrix products, arithmetic and copies ran while one was open for 1% -> 1% of each run, Pallas kernels for 13% -> 14%
where the time goes in v7:
time: 201 us; the launch traced here: 202 us
  waiting for transfers between devices  98.8 us (49%)
  Pallas kernels  55.9 us (28%)
  starting transfers between devices  38.8 us (19%)
  local copies, waits for them, and re-layouts  5.33 us (3%)
  other arithmetic  2.4 us (1%)
    ppermute x24, waiting for transfers between devices, swap(): out.append(lax.ppermute(value, axis, pairs))  70 us
    ppermute x24, starting transfers between devices, swap(): out.append(lax.ppermute(value, axis, pairs))  31.9 us
    all_to_all x1, waiting for transfers between devices, local(): lax.all_to_all(sent, 'blocks', split_axis=0, concat_axis=0, tiled=True)  28.8 us
    pallas_call x1, Pallas kernels, sweep(): pl.pallas_call(functools.partial(sweep_body, slots), out_shape=spread_sha...  13.3 us
    pallas_call x1, Pallas kernels, blur_all(): pl.pallas_call(blur_body, out_shape=pltpu.HBM((cells, BX * DZ, NY), jnp.f...  12.4 us
    pallas_call x1, Pallas kernels, spread_ratio(): pl.pallas_call(functools.partial(spread_body, slots), out_shape=spread_sh...  8.62 us
    all_to_all x1, starting transfers between devices, local(): lax.all_to_all(sent, 'blocks', split_axis=0, concat_axis=0, tiled=True)  6.89 us
    unnamed x26, local copies, waits for them, and re-layouts  5.23 us
  transfers between devices with their start and end apart: 25, of which 15 were waited for; matrix products, arithmetic and copies ran while one was open for 1% of the time, Pallas kernels for 14%

profile of v7, /device:TPU:34, one launch (start us, length us, event | category | flops | bytes accessed | tf_op | source)
XLA Modules:
  0.0 201.8 jit_solution(6158287440259261151)
XLA Ops:
  3.5 3.6 %collective-permute-start.1 = (f32[64,16,128]{2,1,0:T(8,128)S(1)}, f32[64,16,128]{2,1,0:T(8,128)S(1)}, u32[]{:S(2)}, u32[]{:S(2)}) collective-permute-start(f32[64,16,128]{2,1,0:T(8,128)S(1)} %get-tuple-element.58), channel_id=1, source_target_pairs={{8,16},{16,8},{24,32},{32,24},{40,48},{48,40},{56,64},{64,56},{72,... | collective-permute-start | bytes 1572872 | tf_op jit(solution)/shard_map/ppermute | solution.py:787
  10.7 2.3 %place.1 = f32[16,520,128]{2,1,0:T(8,128)} custom-call(s32[8]{0:T(128)S(1)} %and_select_fusion.2.owner, s32[8]{0:T(128)S(1)} %copy-done.8, s32[8]{0:T(128)S(1)} %copy-done.9, f32[8,64,8,128]{3,2,1,0:T(8,128)S(1)} %copy-done.3), custom_call_target="tpu_custom_call" | custom-call | tf_op jit(solution)/shard_map/place/pallas_call | solution.py:454
  13.0 2.6 %collective-permute-done.colse = f32[64,16,128]{2,1,0:T(8,128)S(1)} collective-permute-done((f32[64,16,128]{2,1,0:T(8,128)S(1)}, f32[64,16,128]{2,1,0:T(8,128)S(1)}, u32[]{:S(2)}, u32[]{:S(2)}) %collective-permute-start) | collective-permute-done | bytes 524320 | tf_op jit(solution)/shard_map/ppermute | solution.py:787
  15.6 5.3 %collective-permute-done.1.colso = f32[64,16,128]{2,1,0:T(8,128)S(1)} collective-permute-done((f32[64,16,128]{2,1,0:T(8,128)S(1)}, f32[64,16,128]{2,1,0:T(8,128)S(1)}, u32[]{:S(2)}, u32[]{:S(2)}) %collective-permute-start.1) | collective-permute-done | bytes 524320 | tf_op jit(solution)/shard_map/ppermute | solution.py:787
  20.9 6.9 %all-to-all-start = ((f32[16,520,128]{2,1,0:T(8,128)}), f32[16,520,128]{2,1,0:T(8,128)}, u32[]{:S(2)}, u32[]{:S(2)}) async-start(f32[16,520,128]{2,1,0:T(8,128)} %place.1), calls=%async_computation | async-start | bytes 8519680 | tf_op jit(solution)/shard_map/all_to_all | solution.py:806
  27.8 2.7 %first_planes.1 = (f32[30,32,128]{2,1,0:T(8,128)}, f32[30,32,128]{2,1,0:T(8,128)}) custom-call(s32[2]{0:T(128)S(1)} %pad_add_fusion.par, f32[64,32,128]{2,1,0:T(8,128)} %est.7), custom_call_target="tpu_custom_call" | custom-call | tf_op jit(solution)/shard_map/first_planes/pallas_call | solution.py:502
  30.6 2.5 %collective-permute-start.3 = (f32[30,32,128]{2,1,0:T(8,128)}, f32[30,32,128]{2,1,0:T(8,128)}, u32[]{:S(2)}, u32[]{:S(2)}) collective-permute-start(f32[30,32,128]{2,1,0:T(8,128)} %get-tuple-element.64), channel_id=1, source_target_pairs={{1,2},{2,1},{3,4},{4,3},{5,6},{6,5},{9,10},{10,9},{11,12},{12,11},... | collective-permute-start | bytes 1474568 | tf_op jit(solution)/shard_map/ppermute | solution.py:787
  42.1 4.2 %collective-permute-done.5.sido = f32[30,32,128]{2,1,0:T(8,128)} collective-permute-done((f32[30,32,128]{2,1,0:T(8,128)}, f32[30,32,128]{2,1,0:T(8,128)}, u32[]{:S(2)}, u32[]{:S(2)}) %collective-permute-start.5) | collective-permute-done | bytes 491552 | tf_op jit(solution)/shard_map/ppermute | solution.py:787
  46.3 12.4 %blur_all.1.blurred = f32[24,512,128]{2,1,0:T(8,128)} custom-call(s32[2]{0:T(128)S(1)} %pad_add_fusion.par, f32[64,32,128]{2,1,0:T(8,128)S(1)} %copy-done, f32[64,16,128]{2,1,0:T(8,128)S(1)} %collective-permute-done.colse, f32[64,16,128]{2,1,0:T(8,128)S(1)} %collective-permute-done.1.colso, f32[30,32,128]{2,1,0:T(8,128)} %collective-permute-done.2.cene, ...), custom_call_target="tpu_custom_call" | custom-call | tf_op jit(solution)/shard_map/blur_all/pallas_call | solution.py:386
  58.7 28.8 %all-to-all-done.got = f32[16,520,128]{2,1,0:T(8,128)} async-done(((f32[16,520,128]{2,1,0:T(8,128)}), f32[16,520,128]{2,1,0:T(8,128)}, u32[]{:S(2)}, u32[]{:S(2)}) %all-to-all-start) | async-done | bytes 4259872 | tf_op jit(solution)/shard_map/all_to_all | solution.py:806
  88.6 8.6 %spread_ratio.1 = (f32[30,32,128]{2,1,0:T(8,128)S(1)}, f32[30,32,128]{2,1,0:T(8,128)S(1)}, f32[30,32,128]{2,1,0:T(8,128)S(1)}, f32[30,32,128]{2,1,0:T(8,128)S(1)...) custom-call(s32[2]{0:T(128)S(1)} %pad_add_fusion.par, s32[51]{0:T(128)S(1)} %concatenate.3.meta, ...), custom_call_target="tpu_custom_call" | custom-call | tf_op jit(solution)/shard_map/spread_ratio/pallas_call | solution.py:404
  97.3 2.5 %collective-permute-start.7 = (f32[30,32,128]{2,1,0:T(8,128)S(1)}, f32[30,32,128]{2,1,0:T(8,128)S(1)}, u32[]{:S(2)}, u32[]{:S(2)}) collective-permute-start(f32[30,32,128]{2,1,0:T(8,128)S(1)} %get-tuple-element.80), channel_id=1, source_target_pairs={{1,2},{2,1},{3,4},{4,3},{5,6},{6,5},{9,10},{10,9},{11,12},{12,11},... | collective-permute-start | bytes 1474568 | tf_op jit(solution)/shard_map/ppermute | solution.py:787
  100.7 6.8 %collective-permute-done.7.sido = f32[30,32,128]{2,1,0:T(8,128)S(1)} collective-permute-done((f32[30,32,128]{2,1,0:T(8,128)S(1)}, f32[30,32,128]{2,1,0:T(8,128)S(1)}, u32[]{:S(2)}, u32[]{:S(2)}) %collective-permute-start.7) | collective-permute-done | bytes 491552 | tf_op jit(solution)/shard_map/ppermute | solution.py:787
  111.1 2.5 %collective-permute-start.9 = (f32[30,32,128]{2,1,0:T(8,128)S(1)}, f32[30,32,128]{2,1,0:T(8,128)S(1)}, u32[]{:S(2)}, u32[]{:S(2)}) collective-permute-start(f32[30,32,128]{2,1,0:T(8,128)S(1)} %get-tuple-element.84), channel_id=1, source_target_pairs={{1,2},{2,1},{3,4},{4,3},{5,6},{6,5},{9,10},{10,9},{11,12},{12,11},... | collective-permute-start | bytes 1474568 | tf_op jit(solution)/shard_map/ppermute | solution.py:787
  113.7 4.7 %weigh.1.weight = f32[64,32,128]{2,1,0:T(8,128)S(1)} custom-call(s32[2]{0:T(128)S(1)} %pad_add_fusion.1.at, s32[16,16]{1,0:T(8,128)S(1)} %bitcast.6, f32[8,128]{1,0:T(8,128)S(1)} %pad.12.kz, f32[8,128]{1,0:T(8,128)S(1)} %pad.13.kx, bf16[6,256,256]{2,1,0:T(8,128)(2,1)S(1)} %copy-done.2), custom_call_target="tpu_custom_call" | custom-call | tf_op jit(solution)/shard_map/weigh/pallas_call | solution.py:626
  118.4 2.8 %collective-permute-done.9.ceno = f32[30,32,128]{2,1,0:T(8,128)S(1)} collective-permute-done((f32[30,32,128]{2,1,0:T(8,128)S(1)}, f32[30,32,128]{2,1,0:T(8,128)S(1)}, u32[]{:S(2)}, u32[]{:S(2)}) %collective-permute-start.9) | collective-permute-done | bytes 491552 | tf_op jit(solution)/shard_map/ppermute | solution.py:787
  122.8 4.1 %collective-permute-done.11.colso = f32[64,16,128]{2,1,0:T(8,128)S(1)} collective-permute-done((f32[64,16,128]{2,1,0:T(8,128)S(1)}, f32[64,16,128]{2,1,0:T(8,128)S(1)}, u32[]{:S(2)}, u32[]{:S(2)}) %collective-permute-start.11) | collective-permute-done | bytes 524320 | tf_op jit(solution)/shard_map/ppermute | solution.py:787
  132.5 9.3 %collective-permute-done.12.colse = f32[64,16,128]{2,1,0:T(8,128)S(1)} collective-permute-done((f32[64,16,128]{2,1,0:T(8,128)S(1)}, f32[64,16,128]{2,1,0:T(8,128)S(1)}, u32[]{:S(2)}, u32[]{:S(2)}) %collective-permute-start.12) | collective-permute-done | bytes 524320 | tf_op jit(solution)/shard_map/ppermute | solution.py:787
  141.8 4.0 %collective-permute-done.13.colso = f32[64,16,128]{2,1,0:T(8,128)S(1)} collective-permute-done((f32[64,16,128]{2,1,0:T(8,128)S(1)}, f32[64,16,128]{2,1,0:T(8,128)S(1)}, u32[]{:S(2)}, u32[]{:S(2)}) %collective-permute-start.13) | collective-permute-done | bytes 524320 | tf_op jit(solution)/shard_map/ppermute | solution.py:787
  148.6 8.2 %collective-permute-done.17.sido = f32[30,32,128]{2,1,0:T(8,128)S(1)} collective-permute-done((f32[30,32,128]{2,1,0:T(8,128)S(1)}, f32[30,32,128]{2,1,0:T(8,128)S(1)}, u32[]{:S(2)}, u32[]{:S(2)}) %collective-permute-start.17) | collective-permute-done | bytes 491552 | tf_op jit(solution)/shard_map/ppermute | solution.py:787
  156.8 13.3 %sweep.1 = (f32[30,32,128]{2,1,0:T(8,128)S(1)}, f32[30,32,128]{2,1,0:T(8,128)S(1)}, f32[30,32,128]{2,1,0:T(8,128)S(1)}, f32[30,32,128]{2,1,0:T(8,128)S(1)}, f32[...) custom-call(s32[2]{0:T(128)S(1)} %pad_add_fusion.par, s32[51]{0:T(128)S(1)} %concatenate.3.meta, ...), custom_call_target="tpu_custom_call" | custom-call | tf_op jit(solution)/shard_map/sweep/pallas_call | solution.py:368
  173.4 7.4 %collective-permute-done.19.sido = f32[30,32,128]{2,1,0:T(8,128)S(1)} collective-permute-done((f32[30,32,128]{2,1,0:T(8,128)S(1)}, f32[30,32,128]{2,1,0:T(8,128)S(1)}, u32[]{:S(2)}, u32[]{:S(2)}) %collective-permute-start.19) | collective-permute-done | bytes 491552 | tf_op jit(solution)/shard_map/ppermute | solution.py:787
  186.0 8.0 %collective-permute-done.21.ceno = f32[30,32,128]{2,1,0:T(8,128)S(1)} collective-permute-done((f32[30,32,128]{2,1,0:T(8,128)S(1)}, f32[30,32,128]{2,1,0:T(8,128)S(1)}, u32[]{:S(2)}, u32[]{:S(2)}) %collective-permute-start.21) | collective-permute-done | bytes 491552 | tf_op jit(solution)/shard_map/ppermute | solution.py:787
  195.7 4.0 %collective-permute-done.23.colso = f32[64,16,128]{2,1,0:T(8,128)S(1)} collective-permute-done((f32[64,16,128]{2,1,0:T(8,128)S(1)}, f32[64,16,128]{2,1,0:T(8,128)S(1)}, u32[]{:S(2)}, u32[]{:S(2)}) %collective-permute-start.23) | collective-permute-done | bytes 524320 | tf_op jit(solution)/shard_map/ppermute | solution.py:787
  (84 shorter events, 43.6 us)
Async XLA Ops:
  1.8 13.7 %collective-permute-start = (f32[64,16,128]{2,1,0:T(8,128)S(1)}, f32[64,16,128]{2,1,0:T(8,128)S(1)}, u32[]{:S(2)}, u32[]{:S(2)}) collective-permute-start(f32[64,16,128]{2,1,0:T(8,128)S(1)} %get-tuple-element.57), channel_id=1, source_target_pairs={{0,8},{8,0},{16,24},{24,16},{32,40},{40,32},{48,56},{56,48},{64,72... | collective-permute-start | bytes 1572872 | tf_op jit(solution)/shard_map/ppermute | solution.py:787
  3.5 17.4 %collective-permute-start.1 = (f32[64,16,128]{2,1,0:T(8,128)S(1)}, f32[64,16,128]{2,1,0:T(8,128)S(1)}, u32[]{:S(2)}, u32[]{:S(2)}) collective-permute-start(f32[64,16,128]{2,1,0:T(8,128)S(1)} %get-tuple-element.58), channel_id=1, source_target_pairs={{8,16},{16,8},{24,32},{32,24},{40,48},{48,40},{56,64},{64,56},{72,... | collective-permute-start | bytes 1572872 | tf_op jit(solution)/shard_map/ppermute | solution.py:787
  20.9 66.7 %all-to-all-start = ((f32[16,520,128]{2,1,0:T(8,128)}), f32[16,520,128]{2,1,0:T(8,128)}, u32[]{:S(2)}, u32[]{:S(2)}) async-start(f32[16,520,128]{2,1,0:T(8,128)} %place.1), calls=%async_computation | async-start | bytes 8519680 | tf_op jit(solution)/shard_map/all_to_all | solution.py:806
  30.5 11.6 %collective-permute-start.2 = (f32[30,32,128]{2,1,0:T(8,128)}, f32[30,32,128]{2,1,0:T(8,128)}, u32[]{:S(2)}, u32[]{:S(2)}) collective-permute-start(f32[30,32,128]{2,1,0:T(8,128)} %get-tuple-element.63), channel_id=1, source_target_pairs={{0,1},{1,0},{2,3},{3,2},{4,5},{5,4},{6,7},{7,6},{8,9},{9,8},{10,11... | collective-permute-start | bytes 1474568 | tf_op jit(solution)/shard_map/ppermute | solution.py:787
  30.6 11.5 %collective-permute-start.3 = (f32[30,32,128]{2,1,0:T(8,128)}, f32[30,32,128]{2,1,0:T(8,128)}, u32[]{:S(2)}, u32[]{:S(2)}) collective-permute-start(f32[30,32,128]{2,1,0:T(8,128)} %get-tuple-element.64), channel_id=1, source_target_pairs={{1,2},{2,1},{3,4},{4,3},{5,6},{6,5},{9,10},{10,9},{11,12},{12,11},... | collective-permute-start | bytes 1474568 | tf_op jit(solution)/shard_map/ppermute | solution.py:787
  34.9 7.2 %collective-permute-start.4 = (f32[30,32,128]{2,1,0:T(8,128)}, f32[30,32,128]{2,1,0:T(8,128)}, u32[]{:S(2)}, u32[]{:S(2)}) collective-permute-start(f32[30,32,128]{2,1,0:T(8,128)} %get-tuple-element.65), channel_id=1, source_target_pairs={{0,1},{1,0},{2,3},{3,2},{4,5},{5,4},{6,7},{7,6},{8,9},{9,8},{10,11... | collective-permute-start | bytes 1474568 | tf_op jit(solution)/shard_map/ppermute | solution.py:787
  35.9 10.5 %collective-permute-start.5 = (f32[30,32,128]{2,1,0:T(8,128)}, f32[30,32,128]{2,1,0:T(8,128)}, u32[]{:S(2)}, u32[]{:S(2)}) collective-permute-start(f32[30,32,128]{2,1,0:T(8,128)} %get-tuple-element.66), channel_id=1, source_target_pairs={{1,2},{2,1},{3,4},{4,3},{5,6},{6,5},{9,10},{10,9},{11,12},{12,11},... | collective-permute-start | bytes 1474568 | tf_op jit(solution)/shard_map/ppermute | solution.py:787
  97.2 3.5 %collective-permute-start.6 = (f32[30,32,128]{2,1,0:T(8,128)S(1)}, f32[30,32,128]{2,1,0:T(8,128)S(1)}, u32[]{:S(2)}, u32[]{:S(2)}) collective-permute-start(f32[30,32,128]{2,1,0:T(8,128)S(1)} %get-tuple-element.79), channel_id=1, source_target_pairs={{0,1},{1,0},{2,3},{3,2},{4,5},{5,4},{6,7},{7,6},{8,9},{9,8},{10,11... | collective-permute-start | bytes 1474568 | tf_op jit(solution)/shard_map/ppermute | solution.py:787
  97.3 10.1 %collective-permute-start.7 = (f32[30,32,128]{2,1,0:T(8,128)S(1)}, f32[30,32,128]{2,1,0:T(8,128)S(1)}, u32[]{:S(2)}, u32[]{:S(2)}) collective-permute-start(f32[30,32,128]{2,1,0:T(8,128)S(1)} %get-tuple-element.80), channel_id=1, source_target_pairs={{1,2},{2,1},{3,4},{4,3},{5,6},{6,5},{9,10},{10,9},{11,12},{12,11},... | collective-permute-start | bytes 1474568 | tf_op jit(solution)/shard_map/ppermute | solution.py:787
  108.4 14.4 %collective-permute-start.10 = (f32[64,16,128]{2,1,0:T(8,128)S(1)}, f32[64,16,128]{2,1,0:T(8,128)S(1)}, u32[]{:S(2)}, u32[]{:S(2)}) collective-permute-start(f32[64,16,128]{2,1,0:T(8,128)S(1)} %get-tuple-element.85), channel_id=1, source_target_pairs={{0,8},{8,0},{16,24},{24,16},{32,40},{40,32},{48,56},{56,48},{64,72... | collective-permute-start | bytes 1572872 | tf_op jit(solution)/shard_map/ppermute | solution.py:787
  108.5 18.4 %collective-permute-start.11 = (f32[64,16,128]{2,1,0:T(8,128)S(1)}, f32[64,16,128]{2,1,0:T(8,128)S(1)}, u32[]{:S(2)}, u32[]{:S(2)}) collective-permute-start(f32[64,16,128]{2,1,0:T(8,128)S(1)} %get-tuple-element.86), channel_id=1, source_target_pairs={{8,16},{16,8},{24,32},{32,24},{40,48},{48,40},{56,64},{64,56},{72,... | collective-permute-start | bytes 1572872 | tf_op jit(solution)/shard_map/ppermute | solution.py:787
  110.5 7.9 %collective-permute-start.8 = (f32[30,32,128]{2,1,0:T(8,128)S(1)}, f32[30,32,128]{2,1,0:T(8,128)S(1)}, u32[]{:S(2)}, u32[]{:S(2)}) collective-permute-start(f32[30,32,128]{2,1,0:T(8,128)S(1)} %get-tuple-element.83), channel_id=1, source_target_pairs={{0,1},{1,0},{2,3},{3,2},{4,5},{5,4},{6,7},{7,6},{8,9},{9,8},{10,11... | collective-permute-start | bytes 1474568 | tf_op jit(solution)/shard_map/ppermute | solution.py:787
  111.1 10.1 %collective-permute-start.9 = (f32[30,32,128]{2,1,0:T(8,128)S(1)}, f32[30,32,128]{2,1,0:T(8,128)S(1)}, u32[]{:S(2)}, u32[]{:S(2)}) collective-permute-start(f32[30,32,128]{2,1,0:T(8,128)S(1)} %get-tuple-element.84), channel_id=1, source_target_pairs={{1,2},{2,1},{3,4},{4,3},{5,6},{6,5},{9,10},{10,9},{11,12},{12,11},... | collective-permute-start | bytes 1474568 | tf_op jit(solution)/shard_map/ppermute | solution.py:787
  128.2 13.6 %collective-permute-start.12 = (f32[64,16,128]{2,1,0:T(8,128)S(1)}, f32[64,16,128]{2,1,0:T(8,128)S(1)}, u32[]{:S(2)}, u32[]{:S(2)}) collective-permute-start(f32[64,16,128]{2,1,0:T(8,128)S(1)} %get-tuple-element.88), channel_id=1, source_target_pairs={{0,8},{8,0},{16,24},{24,16},{32,40},{40,32},{48,56},{56,48},{64,72... | collective-permute-start | bytes 1572872 | tf_op jit(solution)/shard_map/ppermute | solution.py:787
  128.3 17.5 %collective-permute-start.13 = (f32[64,16,128]{2,1,0:T(8,128)S(1)}, f32[64,16,128]{2,1,0:T(8,128)S(1)}, u32[]{:S(2)}, u32[]{:S(2)}) collective-permute-start(f32[64,16,128]{2,1,0:T(8,128)S(1)} %get-tuple-element.89), channel_id=1, source_target_pairs={{8,16},{16,8},{24,32},{32,24},{40,48},{48,40},{56,64},{64,56},{72,... | collective-permute-start | bytes 1572872 | tf_op jit(solution)/shard_map/ppermute | solution.py:787
  130.5 18.0 %collective-permute-start.14 = (f32[30,32,128]{2,1,0:T(8,128)S(1)}, f32[30,32,128]{2,1,0:T(8,128)S(1)}, u32[]{:S(2)}, u32[]{:S(2)}) collective-permute-start(f32[30,32,128]{2,1,0:T(8,128)S(1)} %get-tuple-element.90), channel_id=1, source_target_pairs={{0,1},{1,0},{2,3},{3,2},{4,5},{5,4},{6,7},{7,6},{8,9},{9,8},{10,11... | collective-permute-start | bytes 1474568 | tf_op jit(solution)/shard_map/ppermute | solution.py:787
  130.6 18.0 %collective-permute-start.15 = (f32[30,32,128]{2,1,0:T(8,128)S(1)}, f32[30,32,128]{2,1,0:T(8,128)S(1)}, u32[]{:S(2)}, u32[]{:S(2)}) collective-permute-start(f32[30,32,128]{2,1,0:T(8,128)S(1)} %get-tuple-element.91), channel_id=1, source_target_pairs={{1,2},{2,1},{3,4},{4,3},{5,6},{6,5},{9,10},{10,9},{11,12},{12,11},... | collective-permute-start | bytes 1474568 | tf_op jit(solution)/shard_map/ppermute | solution.py:787
  146.6 10.1 %collective-permute-start.17 = (f32[30,32,128]{2,1,0:T(8,128)S(1)}, f32[30,32,128]{2,1,0:T(8,128)S(1)}, u32[]{:S(2)}, u32[]{:S(2)}) collective-permute-start(f32[30,32,128]{2,1,0:T(8,128)S(1)} %get-tuple-element.93), channel_id=1, source_target_pairs={{1,2},{2,1},{3,4},{4,3},{5,6},{6,5},{9,10},{10,9},{11,12},{12,11},... | collective-permute-start | bytes 1474568 | tf_op jit(solution)/shard_map/ppermute | solution.py:787
  170.1 3.3 %collective-permute-start.18 = (f32[30,32,128]{2,1,0:T(8,128)S(1)}, f32[30,32,128]{2,1,0:T(8,128)S(1)}, u32[]{:S(2)}, u32[]{:S(2)}) collective-permute-start(f32[30,32,128]{2,1,0:T(8,128)S(1)} %get-tuple-element.101), channel_id=1, source_target_pairs={{0,1},{1,0},{2,3},{3,2},{4,5},{5,4},{6,7},{7,6},{8,9},{9,8},{10,11... | collective-permute-start | bytes 1474568 | tf_op jit(solution)/shard_map/ppermute | solution.py:787
  170.6 10.1 %collective-permute-start.19 = (f32[30,32,128]{2,1,0:T(8,128)S(1)}, f32[30,32,128]{2,1,0:T(8,128)S(1)}, u32[]{:S(2)}, u32[]{:S(2)}) collective-permute-start(f32[30,32,128]{2,1,0:T(8,128)S(1)} %get-tuple-element.102), channel_id=1, source_target_pairs={{1,2},{2,1},{3,4},{4,3},{5,6},{6,5},{9,10},{10,9},{11,12},{12,11},... | collective-permute-start | bytes 1474568 | tf_op jit(solution)/shard_map/ppermute | solution.py:787
  181.6 14.0 %collective-permute-start.22 = (f32[64,16,128]{2,1,0:T(8,128)S(1)}, f32[64,16,128]{2,1,0:T(8,128)S(1)}, u32[]{:S(2)}, u32[]{:S(2)}) collective-permute-start(f32[64,16,128]{2,1,0:T(8,128)S(1)} %get-tuple-element.107), channel_id=1, source_target_pairs={{0,8},{8,0},{16,24},{24,16},{32,40},{40,32},{48,56},{56,48},{64,72... | collective-permute-start | bytes 1572872 | tf_op jit(solution)/shard_map/ppermute | solution.py:787
  181.7 17.9 %collective-permute-start.23 = (f32[64,16,128]{2,1,0:T(8,128)S(1)}, f32[64,16,128]{2,1,0:T(8,128)S(1)}, u32[]{:S(2)}, u32[]{:S(2)}) collective-permute-start(f32[64,16,128]{2,1,0:T(8,128)S(1)} %get-tuple-element.108), channel_id=1, source_target_pairs={{8,16},{16,8},{24,32},{32,24},{40,48},{48,40},{56,64},{64,56},{72,... | collective-permute-start | bytes 1572872 | tf_op jit(solution)/shard_map/ppermute | solution.py:787
  183.7 2.3 %collective-permute-start.20 = (f32[30,32,128]{2,1,0:T(8,128)S(1)}, f32[30,32,128]{2,1,0:T(8,128)S(1)}, u32[]{:S(2)}, u32[]{:S(2)}) collective-permute-start(f32[30,32,128]{2,1,0:T(8,128)S(1)} %get-tuple-element.105), channel_id=1, source_target_pairs={{0,1},{1,0},{2,3},{3,2},{4,5},{5,4},{6,7},{7,6},{8,9},{9,8},{10,11... | collective-permute-start | bytes 1474568 | tf_op jit(solution)/shard_map/ppermute | solution.py:787
  183.9 10.1 %collective-permute-start.21 = (f32[30,32,128]{2,1,0:T(8,128)S(1)}, f32[30,32,128]{2,1,0:T(8,128)S(1)}, u32[]{:S(2)}, u32[]{:S(2)}) collective-permute-start(f32[30,32,128]{2,1,0:T(8,128)S(1)} %get-tuple-element.106), channel_id=1, source_target_pairs={{1,2},{2,1},{3,4},{4,3},{5,6},{6,5},{9,10},{10,9},{11,12},{12,11},... | collective-permute-start | bytes 1474568 | tf_op jit(solution)/shard_map/ppermute | solution.py:787
  (14 other events, 221.5 us)
